TPU v7x, 32 devices: a whole 2x2x4 slice. The times are simulated.
32 devices in a mesh: dp: 8 (over y, x, core), tensor: 4 (over z).
Axes of the slice: x: 2, y: 2, z: 4, core: 2. Of those that a mesh axis runs over, the one named last changes fastest.
Arguments:
- hidden_in: bfloat16 [1024, 2048], P('dp'), may hold values from -6 to 6
- seq_lengths: int32 [16, 4], P('dp'), may hold values from 1 to 32, 64 in all within a row
- norm_gains: float32 [4, 2048], replicated, may hold values from 0.25 to 1.75
- mixer_in: bfloat16 [2, 2048, 4096], P(None, 'dp', 'tensor'), may hold values from -0.125 to 0.125
- mixer_rows: bfloat16 [2336, 4096], P('dp', 'tensor'), may hold values from -0.375 to 0.375
- conv_weight: float32 [4096, 4], P('tensor'), may hold values from -3 to 3
- conv_bias: float32 [4096], P('tensor'), may hold values from -3 to 3
- step_bias: float32 [4096], P('tensor'), may hold values from -5 to -2
- decay_log: float32 [4096, 16], P('tensor'), may hold values from 0 to 2.8
- skip_gain: float32 [4096], P('tensor'), may hold values from 0.5 to 1.5
- early_gate_up: bfloat16 [2, 2048, 8192], P(None, 'dp', 'tensor'), may hold values from -0.125 to 0.125
- early_down: bfloat16 [2048, 8192], P('dp', 'tensor'), may hold values from -0.0625 to 0.0625
- attention_in: bfloat16 [3, 2048, 2048], P(None, 'dp', 'tensor'), may hold values from -0.1875 to 0.1875
- attention_out: bfloat16 [2048, 2048], P('dp', 'tensor'), may hold values from -0.5 to 0.5
- late_gate_up: bfloat16 [2, 2048, 8192], P(None, 'dp', 'tensor'), may hold values from -0.125 to 0.125
- late_down: bfloat16 [2048, 8192], P('dp', 'tensor'), may hold values from -0.0625 to 0.0625
- output_grad: bfloat16 [1024, 2048], P('dp'), may hold values from -6 to 6
Outputs:
- output: float32 [1024, 2048], P('dp')
- input_grad: float32 [1024, 2048], P('dp')
- norm_gains_grad: float32 [4, 2048], replicated
- mixer_in_grad: float32 [2, 2048, 4096], P(None, 'dp', 'tensor')
- mixer_rows_grad: float32 [2336, 4096], P('dp', 'tensor')
- conv_weight_grad: float32 [4096, 4], P('tensor')
- conv_bias_grad: float32 [4096], P('tensor')
- step_bias_grad: float32 [4096], P('tensor')
- decay_log_grad: float32 [4096, 16], P('tensor')
- skip_gain_grad: float32 [4096], P('tensor')
- early_gate_up_grad: float32 [2, 2048, 8192], P(None, 'dp', 'tensor')
- early_down_grad: float32 [2048, 8192], P('dp', 'tensor')
- attention_in_grad: float32 [3, 2048, 2048], P(None, 'dp', 'tensor')
- attention_out_grad: float32 [2048, 2048], P('dp', 'tensor')
- late_gate_up_grad: float32 [2, 2048, 8192], P(None, 'dp', 'tensor')
- late_down_grad: float32 [2048, 8192], P('dp', 'tensor')
Inputs may be any that keep to these rules, and one draw needn't show every extreme that they name: `seq_lengths`: each row lists the lengths of the 4 sequences packed one after another into one micro-batch; every row sums to 64 and its longest sequence has exactly 32 tokens.
All inputs are finite; a program needn't handle non-finite values.
Results may differ from a plain program's by a relative error of at most 0.025.
The roundings to bfloat16 on the way count: a program that leaves them out, or rounds other values in their place, can miss the bound.
Values may be sent and summed in bfloat16 or wider, within the bound.
A program may use at most 320 MiB of HBM per device.

v0:
```python
from functools import partial
import math

import jax
import jax.numpy as jnp
from jax import lax
from jax.sharding import PartitionSpec as P

STATE = 16
CONV = 4
DT_RANK = 128
HEAD_DIM = 128
WINDOW = 2048
PROJ_OUT = 160


EPS = 1e-05
SCAN_BLOCK = 64
NEG_FILL = -1e30


def project(left, right):
    return jnp.dot(left, right, preferred_element_type=jnp.float32)


def project_t(left, right):
    return lax.dot_general(
        left, right, (((1,), (1,)), ((), ())), preferred_element_type=jnp.float32
    )


def outer_rows(left, right):
    return lax.dot_general(
        left, right, (((0,), (0,)), ((), ())), preferred_element_type=jnp.float32
    )


def rms_norm(values, weight):
    return values * lax.rsqrt(jnp.mean(values * values, axis=-1, keepdims=True) + EPS) * weight


def segment_info(lengths, tokens):
    flat_lengths = lengths.reshape(-1)
    ends = jnp.cumsum(flat_lengths, dtype=jnp.int32)
    firsts = ends - flat_lengths
    places = jnp.arange(tokens, dtype=jnp.int32)
    segs = jnp.sum((places[:, None] >= ends[None, :]).astype(jnp.int32), axis=1)
    starts = jnp.any(places[:, None] == firsts[None, :], axis=1)
    return (segs, starts)


def allowed_pairs(segs):
    places = jnp.arange(segs.shape[-1], dtype=jnp.int32)
    distance = places[:, None] - places[None, :]
    return (segs[:, None] == segs[None, :]) & (distance >= 0) & (distance < WINDOW)


def causal_conv(segs, stream, weight, offset):
    total = offset + stream * weight[:, 0]
    for lag_step in range(1, CONV):
        moved = jnp.concatenate(
            [jnp.zeros_like(stream[..., :lag_step, :]), stream[..., :-lag_step, :]], axis=-2
        )
        moved_segs = jnp.concatenate(
            [jnp.full_like(segs[..., :lag_step], -1), segs[..., :-lag_step]], axis=-1
        )
        linked = (segs == moved_segs).astype(stream.dtype)
        total = total + moved * weight[:, lag_step] * linked[..., None]
    return jax.nn.silu(total)


def combine_pairs(earlier, later):
    return (earlier[0] * later[0], later[0] * earlier[1] + later[1])


def blocked_scan(step_size, channel_in, input_map, output_map, keeping, rates, block_rows):
    groups, length, channels = step_size.shape
    block_count = length // block_rows

    def to_blocks(values):
        shaped = values.reshape((groups, block_count, block_rows) + values.shape[2:])
        return jnp.moveaxis(shaped, 1, 0)

    def advance(carry_state, pieces):
        step_block, channel_block, input_block, output_block, keep_block = pieces
        decay_rate = jnp.exp(step_block[..., None] * rates) * keep_block[..., None, None]
        driven = (step_block * channel_block)[..., None] * input_block[:, :, None, :]
        decay_run, driven_run = lax.associative_scan(combine_pairs, (decay_rate, driven), axis=1)
        states = decay_run * carry_state[:, None] + driven_run
        return (states[:, -1], jnp.sum(states * output_block[:, :, None, :], axis=-1))

    zero_state = jnp.zeros((groups, channels, rates.shape[1]), step_size.dtype)
    pieces = (
        to_blocks(step_size),
        to_blocks(channel_in),
        to_blocks(input_map),
        to_blocks(output_map),
        to_blocks(keeping),
    )
    _, outputs = lax.scan(jax.checkpoint(advance), zero_state, pieces)
    return jnp.moveaxis(outputs, 0, 1).reshape(groups, length, channels)


def selective_scan(
    starts, channel_in, step_raw, mixed_rows, gate_half, step_bias, decay_log, skip_gain
):
    step_size = jax.nn.softplus(step_raw + step_bias)
    input_map = mixed_rows[:, DT_RANK : DT_RANK + STATE]
    output_map = mixed_rows[:, DT_RANK + STATE :]
    keeping = 1.0 - starts.astype(jnp.float32)
    block_rows = min(SCAN_BLOCK, channel_in.shape[0])
    scanned = blocked_scan(
        step_size[None],
        channel_in[None],
        input_map[None],
        output_map[None],
        keeping[None],
        -jnp.exp(decay_log),
        block_rows,
    )[0]
    return (scanned + skip_gain * channel_in) * jax.nn.silu(gate_half)


def attention_scores(query, keys, allowed):
    scores = jnp.einsum("qhd,khd->hqk", query, keys, preferred_element_type=jnp.float32) * (
        1.0 / math.sqrt(HEAD_DIM)
    )
    return jnp.where(allowed[None], scores, NEG_FILL)


def attention_forward(query, keys, values, allowed):
    scores = attention_scores(query, keys, allowed)
    row_max = jnp.max(scores, axis=-1, keepdims=True)
    shifted = jnp.exp(scores - row_max)
    totals = jnp.sum(shifted, axis=-1, keepdims=True)
    probs = shifted / totals
    mixed = jnp.einsum(
        "hqk,khd->qhd", probs.astype(jnp.bfloat16), values, preferred_element_type=jnp.float32
    )
    return (mixed, row_max + jnp.log(totals))


def attention_backward(query, keys, values, allowed, log_total, grad_mixed):
    scale = 1.0 / math.sqrt(HEAD_DIM)
    probs = jnp.exp(attention_scores(query, keys, allowed) - log_total)
    grad_values = jnp.einsum(
        "hqk,qhd->khd", probs.astype(jnp.bfloat16), grad_mixed, preferred_element_type=jnp.float32
    )
    grad_probs = jnp.einsum("qhd,khd->hqk", grad_mixed, values, preferred_element_type=jnp.float32)
    inner_sum = jnp.sum(probs * grad_probs, axis=-1, keepdims=True)
    grad_scores = (probs * (grad_probs - inner_sum)).astype(jnp.bfloat16)
    grad_query = (
        jnp.einsum("hqk,khd->qhd", grad_scores, keys, preferred_element_type=jnp.float32) * scale
    )
    grad_keys = (
        jnp.einsum("hqk,qhd->khd", grad_scores, query, preferred_element_type=jnp.float32) * scale
    )
    return (grad_query, grad_keys, grad_values)


def gated_unit(gate, upward):
    return jax.nn.silu(gate) * upward


def ffn_forward(normed_low, gate_up, down_mat):
    gate = project(normed_low, gate_up[0])
    upward = project(normed_low, gate_up[1])
    hidden = gated_unit(gate, upward).astype(jnp.bfloat16)
    return (project_t(hidden, down_mat), gate, upward, hidden)


def ffn_backward(grad_low, normed_low, gate, upward, hidden, gate_up, down_mat):
    grad_hidden = project(grad_low, down_mat)
    down_grad = outer_rows(grad_low, hidden)
    _, unit_back = jax.vjp(gated_unit, gate, upward)
    grad_gate, grad_up = unit_back(grad_hidden)
    gate_low = grad_gate.astype(jnp.bfloat16)
    up_low = grad_up.astype(jnp.bfloat16)
    joined_grad = outer_rows(normed_low, jnp.concatenate([gate_low, up_low], axis=1))
    grad_normed = project_t(gate_low, gate_up[0]) + project_t(up_low, gate_up[1])
    return (grad_normed, joined_grad, down_grad)


def flatten_low(grad_heads, tokens):
    return grad_heads.astype(jnp.bfloat16).reshape(tokens, -1)


def collect(stacked, row_block):
    return (
        lax.all_gather(stacked, "dp", axis=1, tiled=True),
        lax.all_gather(row_block, "dp", axis=0, tiled=True),
    )


def collect_again(stacked, row_block):
    return (
        lax.all_gather(stacked, "dp", axis=1, tiled=True),
        lax.all_gather(row_block, "dp", axis=0, tiled=True),
    )


def spread_grads(joined, row_block, count):
    summed = (
        lax.psum_scatter(joined, "dp", scatter_dimension=0, tiled=True),
        lax.psum_scatter(row_block, "dp", scatter_dimension=0, tiled=True),
    )
    rows_here = summed[0].shape[0]
    restacked = jnp.transpose(summed[0].reshape(rows_here, count, -1), (1, 0, 2))
    return (restacked, summed[1])


def branch_total(piece_sum):
    return lax.psum(piece_sum, "tensor")


def input_total(piece_sum):
    return lax.psum(piece_sum, "tensor")


def body(
    hidden_in,
    seq_lengths,
    norm_gains,
    mixer_in,
    mixer_rows,
    conv_weight,
    conv_bias,
    step_bias,
    decay_log,
    skip_gain,
    early_gate_up,
    early_down,
    attention_in,
    attention_out,
    late_gate_up,
    late_down,
    output_grad,
):
    tokens = hidden_in.shape[0]
    width = hidden_in.shape[1]
    segs, starts = segment_info(seq_lengths, tokens)
    allowed = allowed_pairs(segs)
    stream_zero = hidden_in.astype(jnp.float32)
    mixer_stack, mixer_mats = collect(mixer_in, mixer_rows)
    first_normed, first_back = jax.vjp(rms_norm, stream_zero, norm_gains[0])
    first_low = first_normed.astype(jnp.bfloat16)
    conv_in = project(first_low, mixer_stack[0])
    gate_half = project(first_low, mixer_stack[1])
    channel_full, conv_back = jax.vjp(partial(causal_conv, segs), conv_in, conv_weight, conv_bias)
    channel_low = channel_full.astype(jnp.bfloat16)
    mix_rows = lax.psum(project_t(channel_low, mixer_mats[width : width + PROJ_OUT]), "tensor")
    rank_low = mix_rows[:, :DT_RANK].astype(jnp.bfloat16)
    step_raw = project(rank_low, mixer_mats[width + PROJ_OUT :])
    scanned, scan_back = jax.vjp(
        partial(selective_scan, starts),
        channel_low.astype(jnp.float32),
        step_raw,
        mix_rows,
        gate_half,
        step_bias,
        decay_log,
        skip_gain,
    )
    mixer_low = scanned.astype(jnp.bfloat16)
    stream_one = stream_zero + branch_total(project_t(mixer_low, mixer_mats[:width]))
    early_stack, early_mat = collect(early_gate_up, early_down)
    second_normed, second_back = jax.vjp(rms_norm, stream_one, norm_gains[1])
    second_low = second_normed.astype(jnp.bfloat16)
    early_part, early_gate, early_up, early_hidden = ffn_forward(second_low, early_stack, early_mat)
    stream_two = stream_one + branch_total(early_part)
    focus_stack, focus_mat = collect(attention_in, attention_out)
    heads_here = focus_stack.shape[2] // HEAD_DIM
    third_normed, third_back = jax.vjp(rms_norm, stream_two, norm_gains[2])
    third_low = third_normed.astype(jnp.bfloat16)
    query = (
        project(third_low, focus_stack[0])
        .astype(jnp.bfloat16)
        .reshape(tokens, heads_here, HEAD_DIM)
    )
    keys = (
        project(third_low, focus_stack[1])
        .astype(jnp.bfloat16)
        .reshape(tokens, heads_here, HEAD_DIM)
    )
    values = (
        project(third_low, focus_stack[2])
        .astype(jnp.bfloat16)
        .reshape(tokens, heads_here, HEAD_DIM)
    )
    attended, log_total = attention_forward(query, keys, values, allowed)
    attended_low = attended.reshape(tokens, heads_here * HEAD_DIM).astype(jnp.bfloat16)
    stream_three = stream_two + branch_total(project_t(attended_low, focus_mat))
    late_stack, late_mat = collect(late_gate_up, late_down)
    fourth_normed, fourth_back = jax.vjp(rms_norm, stream_three, norm_gains[3])
    fourth_low = fourth_normed.astype(jnp.bfloat16)
    late_part, late_gate, late_up, late_hidden = ffn_forward(fourth_low, late_stack, late_mat)
    output = stream_three + branch_total(late_part)
    grad_three = output_grad.astype(jnp.float32)
    late_pair = collect_again(late_gate_up, late_down)
    grad_fourth, late_joined, late_mat_grad = ffn_backward(
        output_grad, fourth_low, late_gate, late_up, late_hidden, late_pair[0], late_pair[1]
    )
    grad_stream, gain_four = fourth_back(input_total(grad_fourth))
    grad_three = grad_three + grad_stream
    late_grads = spread_grads(late_joined, late_mat_grad, 2)
    focus_pair = collect_again(attention_in, attention_out)
    grad_branch_low = grad_three.astype(jnp.bfloat16)
    focus_mat_grad = outer_rows(grad_branch_low, attended_low)
    grad_attended = (
        project(grad_branch_low, focus_pair[1])
        .astype(jnp.bfloat16)
        .reshape(tokens, heads_here, HEAD_DIM)
    )
    grad_query, grad_keys, grad_values = attention_backward(
        query, keys, values, allowed, log_total, grad_attended
    )
    query_low = flatten_low(grad_query, tokens)
    keys_low = flatten_low(grad_keys, tokens)
    values_low = flatten_low(grad_values, tokens)
    focus_joined = outer_rows(third_low, jnp.concatenate([query_low, keys_low, values_low], axis=1))
    grad_third = (
        project_t(query_low, focus_pair[0][0])
        + project_t(keys_low, focus_pair[0][1])
        + project_t(values_low, focus_pair[0][2])
    )
    grad_stream, gain_three = third_back(input_total(grad_third))
    grad_two = grad_three + grad_stream
    focus_grads = spread_grads(focus_joined, focus_mat_grad, 3)
    early_pair = collect_again(early_gate_up, early_down)
    grad_second, early_joined, early_mat_grad = ffn_backward(
        grad_two.astype(jnp.bfloat16),
        second_low,
        early_gate,
        early_up,
        early_hidden,
        early_pair[0],
        early_pair[1],
    )
    grad_stream, gain_two = second_back(input_total(grad_second))
    grad_one = grad_two + grad_stream
    early_grads = spread_grads(early_joined, early_mat_grad, 2)
    mixer_pair = collect_again(mixer_in, mixer_rows)
    grad_mixer_low = grad_one.astype(jnp.bfloat16)
    out_mat_grad = outer_rows(grad_mixer_low, mixer_low)
    grad_scanned = project(grad_mixer_low, mixer_pair[1][:width])
    (
        grad_channel,
        grad_step,
        grad_rows_scan,
        grad_gate,
        step_bias_grad,
        decay_log_grad,
        skip_gain_grad,
    ) = scan_back(grad_scanned)
    grad_step_low = grad_step.astype(jnp.bfloat16)
    step_mat_grad = outer_rows(rank_low, grad_step_low)
    grad_rank = project_t(grad_step_low, mixer_pair[1][width + PROJ_OUT :])
    grad_rows = lax.psum(
        jnp.concatenate([grad_rank, grad_rows_scan[:, DT_RANK:]], axis=1), "tensor"
    )
    grad_rows_low = grad_rows.astype(jnp.bfloat16)
    select_mat_grad = outer_rows(grad_rows_low, channel_low)
    grad_channel = grad_channel + project(grad_rows_low, mixer_pair[1][width : width + PROJ_OUT])
    grad_conv_in, conv_weight_grad, conv_bias_grad = conv_back(grad_channel)
    conv_low = grad_conv_in.astype(jnp.bfloat16)
    gate_low = grad_gate.astype(jnp.bfloat16)
    mixer_joined = outer_rows(first_low, jnp.concatenate([conv_low, gate_low], axis=1))
    grad_first = project_t(conv_low, mixer_pair[0][0]) + project_t(gate_low, mixer_pair[0][1])
    grad_stream, gain_one = first_back(input_total(grad_first))
    input_grad = grad_one + grad_stream
    mixer_grads = spread_grads(
        mixer_joined, jnp.concatenate([out_mat_grad, select_mat_grad, step_mat_grad], axis=0), 2
    )
    small_sums = lax.psum(
        (
            jnp.stack([gain_one, gain_two, gain_three, gain_four]),
            conv_weight_grad,
            conv_bias_grad,
            step_bias_grad,
            decay_log_grad,
            skip_gain_grad,
        ),
        "dp",
    )
    return (
        output,
        input_grad,
        small_sums[0],
        mixer_grads[0],
        mixer_grads[1],
        small_sums[1],
        small_sums[2],
        small_sums[3],
        small_sums[4],
        small_sums[5],
        early_grads[0],
        early_grads[1],
        focus_grads[0],
        focus_grads[1],
        late_grads[0],
        late_grads[1],
    )


def solution(mesh):
    return jax.shard_map(
        body,
        mesh=mesh,
        in_specs=(
            P("dp", None),
            P("dp", None),
            P(),
            P(None, "dp", "tensor"),
            P("dp", "tensor"),
            P("tensor", None),
            P("tensor"),
            P("tensor"),
            P("tensor", None),
            P("tensor"),
            P(None, "dp", "tensor"),
            P("dp", "tensor"),
            P(None, "dp", "tensor"),
            P("dp", "tensor"),
            P(None, "dp", "tensor"),
            P("dp", "tensor"),
            P("dp", None),
        ),
        out_specs=(
            P("dp", None),
            P("dp", None),
            P(),
            P(None, "dp", "tensor"),
            P("dp", "tensor"),
            P("tensor", None),
            P("tensor"),
            P("tensor"),
            P("tensor", None),
            P("tensor"),
            P(None, "dp", "tensor"),
            P("dp", "tensor"),
            P(None, "dp", "tensor"),
            P("dp", "tensor"),
            P(None, "dp", "tensor"),
            P("dp", "tensor"),
        ),
        check_vma=False,
    )
```

profile of v0, /device:TPU:1, one launch (start us, length us, event | category | flops | bytes accessed | tf_op | source)
XLA Modules:
  0.0 3609.6 jit_solution(1869659520465810039)
XLA Ops:
  15.9 36.0 all-gather.24.cloned.1.call-done
  57.3 50.9 %all-gather.10.cloned.1.call-done = bf16[2,2048,1024]{2,1,0:T(8,128)(2,1)} async-done(((bf16[2,256,1024]{2,1,0:T(8,128)(2,1)}), bf16[2,2048,1024]{2,1,0:T(8,128)(2,1)}) %all-gather.10.cloned.1.call-update) | async-done | bytes 8388624 | tf_op jit(solution)/shard_map/all_gather | solution.py:190
  117.0 30.1 all-reduce.131.cloned.1.call-done
  151.9 412.0 %while.39 = (s32[]{:T(128)}, f32[1,1024,16]{1,2,0:T(8,128)S(1)}, f32[2,1,64,1024]{3,2,1,0:T(8,128)}, f32[2,1,1024,16]{2,3,1,0:T(8,128)}, f32[2,1,64,1024]{3,2,1,...) while((s32[]{:T(128)}, f32[1,1024,16]{1,2,0:T(8,128)S(1)}, ...), condition=%wide.region_7.8_spmd, body=%wide.region_5.7_spmd.sunk | while | flops 21266432 | bytes 254862928 | solution.py:100
  264.8 18.5 pad.1569
  287.5 18.5 pad.1570
  309.1 18.5 pad.1571
  330.9 18.6 pad.1572
  470.7 18.5 pad.1569
  493.4 18.5 pad.1570
  515.0 18.5 pad.1571
  536.8 18.6 pad.1572
  572.0 52.8 %all-reduce.133.cloned.1.call-done = f32[128,2048]{1,0:T(8,128)} async-done(((f32[128,2048]{1,0:T(8,128)}), f32[128,2048]{1,0:T(8,128)}) %all-reduce.133.cloned.1.call-update) | async-done | bytes 1048592 | tf_op jit(solution)/shard_map/psum | solution.py:213
  626.5 89.6 %all-gather.12.cloned.1.call-done = bf16[2,2048,2048]{2,1,0:T(8,128)(2,1)} async-done(((bf16[2,256,2048]{2,1,0:T(8,128)(2,1)}), bf16[2,2048,2048]{2,1,0:T(8,128)(2,1)}) %all-gather.12.cloned.1.call-update) | async-done | bytes 16777232 | tf_op jit(solution)/shard_map/all_gather | solution.py:190
  727.0 45.3 %all-gather.14.cloned.1.call-done = bf16[2048,2048]{1,0:T(8,128)(2,1)} async-done(((bf16[256,2048]{1,0:T(8,128)(2,1)}), bf16[2048,2048]{1,0:T(8,128)(2,1)}) %all-gather.14.cloned.1.call-update) | async-done | bytes 8388624 | tf_op jit(solution)/shard_map/all_gather | solution.py:191
  781.2 50.1 %all-reduce.135.cloned.1.call-done = f32[128,2048]{1,0:T(8,128)} async-done(((f32[128,2048]{1,0:T(8,128)}), f32[128,2048]{1,0:T(8,128)}) %all-reduce.135.cloned.1.call-update) | async-done | bytes 1048592 | tf_op jit(solution)/shard_map/psum | solution.py:213
  833.3 45.2 %all-gather.16.cloned.1.call-done = bf16[3,2048,512]{2,1,0:T(8,128)(2,1)} async-done(((bf16[3,256,512]{2,1,0:T(8,128)(2,1)}), bf16[3,2048,512]{2,1,0:T(8,128)(2,1)}) %all-gather.16.cloned.1.call-update) | async-done | bytes 6291472 | tf_op jit(solution)/shard_map/all_gather | solution.py:190
  885.6 23.0 all-gather.18.cloned.1.call-done
  913.7 50.0 %all-reduce.137.cloned.1.call-done = f32[128,2048]{1,0:T(8,128)} async-done(((f32[128,2048]{1,0:T(8,128)}), f32[128,2048]{1,0:T(8,128)}) %all-reduce.137.cloned.1.call-update) | async-done | bytes 1048592 | tf_op jit(solution)/shard_map/psum | solution.py:213
  967.8 87.3 %all-gather.20.cloned.1.call-done = bf16[2,2048,2048]{2,1,0:T(8,128)(2,1)} async-done(((bf16[2,256,2048]{2,1,0:T(8,128)(2,1)}), bf16[2,2048,2048]{2,1,0:T(8,128)(2,1)}) %all-gather.20.cloned.1.call-update) | async-done | bytes 16777232 | tf_op jit(solution)/shard_map/all_gather | solution.py:190
  1066.9 44.3 %all-gather.22.cloned.1.call-done = bf16[2048,2048]{1,0:T(8,128)(2,1)} async-done(((bf16[256,2048]{1,0:T(8,128)(2,1)}), bf16[2048,2048]{1,0:T(8,128)(2,1)}) %all-gather.22.cloned.1.call-update) | async-done | bytes 8388624 | tf_op jit(solution)/shard_map/all_gather | solution.py:191
  1130.2 50.4 %all-reduce.139.cloned.1.call-done = f32[128,2048]{1,0:T(8,128)} async-done(((f32[128,2048]{1,0:T(8,128)}), f32[128,2048]{1,0:T(8,128)}) %all-reduce.139.cloned.1.call-update) | async-done | bytes 1048592 | tf_op jit(solution)/shard_map/psum | solution.py:217
  1198.3 51.1 %all-reduce.141.cloned.1.call-done = f32[128,2048]{1,0:T(8,128)} async-done(((f32[128,2048]{1,0:T(8,128)}), f32[128,2048]{1,0:T(8,128)}) %all-reduce.141.cloned.1.call-update) | async-done | bytes 1048592 | tf_op jit(solution)/shard_map/psum | solution.py:217
  1277.7 43.9 %all-reduce.143.cloned.1.call-done = f32[128,2048]{1,0:T(8,128)} async-done(((f32[128,2048]{1,0:T(8,128)}), f32[128,2048]{1,0:T(8,128)}) %all-reduce.143.cloned.1.call-update) | async-done | bytes 1048592 | tf_op jit(solution)/shard_map/psum | solution.py:217
  1334.0 1123.8 %while.40 = (s32[]{:T(128)}, f32[1024,16]{1,0:T(8,128)}, f32[1,1024,16]{1,2,0:T(8,128)}, f32[2,1,64,1024]{3,2,1,0:T(8,128)}, f32[2,1,64,1024]{3,2,1,0:T(8,128)},...) while((s32[]{:T(128)}, f32[1024,16]{1,0:T(8,128)}, ...), condition=%wide.region_31.32_spmd.clone, body=%wide.region_24.31_spmd.clone.sunk | while | flops 65435648 | bytes 762754240 | solution.py:100
  1677.5 18.5 pad.1675
  1696.1 18.6 pad.1676
  1743.2 18.5 pad.1678
  1765.8 18.5 pad.1679
  1787.4 18.5 pad.1680
  1810.1 18.6 pad.1681
  1836.1 18.5 pad.1682
  2235.0 18.5 pad.1675
  2253.6 18.6 pad.1676
  2301.7 18.5 pad.1678
  2324.3 18.5 pad.1679
  2345.9 18.5 pad.1680
  2368.6 18.6 pad.1681
  2394.6 18.5 pad.1682
  2564.8 151.9 %fusion = f32[296,1024]{1,0:T(8,128)} fusion(f32[2336,1024]{1,0:T(8,128)} %pad_maximum_fusion.20), kind=kCustom, calls=%all-reduce-scatter | all-reduce-scatter fusion | flops 2424833 | bytes 10781184
  2736.9 23.5 all-reduce.119
  2766.4 66.0 %reduce-scatter.22.cloned.1.call-done = f32[256,2048]{0,1:T(8,128)} async-done(((f32[2048,2048]{0,1:T(8,128)}), f32[256,2048]{0,1:T(8,128)}) %reduce-scatter.22.cloned.1.call-update) | async-done | bytes 2097168 | tf_op jit(solution)/shard_map/reduce_scatter | solution.py:205
  2835.2 116.7 %reduce-scatter.10.cloned.1.call-done = f32[256,2048]{1,0:T(8,128)} async-done(((f32[2048,2048]{1,0:T(8,128)}), f32[256,2048]{1,0:T(8,128)}) %reduce-scatter.10.cloned.1.call-update) | async-done | bytes 2097168 | tf_op jit(solution)/shard_map/reduce_scatter | solution.py:204
  2955.1 205.5 %reduce-scatter.20.cloned.1.call-done = f32[256,4096]{1,0:T(8,128)} async-done(((f32[2048,4096]{1,0:T(8,128)}), f32[256,4096]{1,0:T(8,128)}) %reduce-scatter.20.cloned.1.call-update) | async-done | bytes 4194320 | tf_op jit(solution)/shard_map/reduce_scatter | solution.py:204
  3165.3 204.6 %reduce-scatter.12.cloned.1.call-done = f32[256,4096]{1,0:T(8,128)} async-done(((f32[2048,4096]{1,0:T(8,128)}), f32[256,4096]{1,0:T(8,128)}) %reduce-scatter.12.cloned.1.call-update) | async-done | bytes 4194320 | tf_op jit(solution)/shard_map/reduce_scatter | solution.py:204
  3374.6 50.7 %all-reduce.145.cloned.1.call-done = f32[1024,16]{0,1:T(8,128)} async-done(((f32[1024,16]{0,1:T(8,128)}), f32[1024,16]{0,1:T(8,128)}) %all-reduce.145.cloned.1.call-update) | async-done | bytes 65552 | tf_op jit(solution)/shard_map/psum | solution.py:374
  3425.3 55.8 %reduce-scatter.18.cloned.1.call-done = f32[256,512]{1,0:T(8,128)} async-done(((f32[2048,512]{1,0:T(8,128)}), f32[256,512]{1,0:T(8,128)}) %reduce-scatter.18.cloned.1.call-update) | async-done | bytes 524304 | tf_op jit(solution)/shard_map/reduce_scatter | solution.py:205
  3481.1 119.9 %reduce-scatter.14.cloned.1.call-done = f32[256,2048]{1,0:T(8,128)} async-done(((f32[2048,2048]{1,0:T(8,128)}), f32[256,2048]{1,0:T(8,128)}) %reduce-scatter.14.cloned.1.call-update) | async-done | bytes 2097168 | tf_op jit(solution)/shard_map/reduce_scatter | solution.py:205
  (1321 shorter events, 1429.3 us)
Async XLA Ops:
  7.2 44.7 %all-gather.24.cloned.1.call-start = ((), (), s32[]{:S(2)}) async-start(), calls=%async_computation.29 | async-start | bytes 5455872 | tf_op jit(solution)/shard_map/all_gather | solution.py:191
  7.9 100.3 %all-gather.10.cloned.1.call-start = ((), (), s32[]{:S(2)}) async-start(), calls=%async_computation.7 | async-start | bytes 9437184 | tf_op jit(solution)/shard_map/all_gather | solution.py:190
  8.7 138.5 %all-reduce.131.cloned.1.call-start = ((), (), s32[]{:S(2)}) async-start(), calls=%async_computation.8 | async-start | bytes 163840 | tf_op jit(solution)/shard_map/psum | solution.py:251
  11.8 96.4 %copy-start.191 = (f32[128]{0:T(128)}, f32[128]{0:T(128)S(1)}, u32[]{:S(2)}) copy-start(f32[128]{0:T(128)S(1)} %fusion.135) | copy-start | bytes 1540
  11.9 99.3 %copy-start.195 = (f32[128]{0:T(128)}, f32[128]{0:T(128)S(1)}, u32[]{:S(2)}) copy-start(f32[128]{0:T(128)S(1)} %get-tuple-element.888) | copy-start | bytes 1540
  11.9 99.3 %copy-start.196 = (f32[128]{0:T(128)}, f32[128]{0:T(128)S(1)}, u32[]{:S(2)}) copy-start(f32[128]{0:T(128)S(1)} %get-tuple-element.889) | copy-start | bytes 1540
  11.9 99.3 %copy-start.197 = (f32[128]{0:T(128)}, f32[128]{0:T(128)S(1)}, u32[]{:S(2)}) copy-start(f32[128]{0:T(128)S(1)} %get-tuple-element.890) | copy-start | bytes 1540
  12.8 98.4 %copy-start.172 = (f32[1024,1]{0,1:T(1,128)}, f32[1024,1]{0,1:T(1,128)S(1)}, u32[]{:S(2)}) copy-start(f32[1024,1]{0,1:T(1,128)S(1)} %get-tuple-element.884) | copy-start | bytes 12292
  12.8 98.4 %copy-start.174 = (f32[1024,1]{0,1:T(1,128)}, f32[1024,1]{0,1:T(1,128)S(1)}, u32[]{:S(2)}) copy-start(f32[1024,1]{0,1:T(1,128)S(1)} %get-tuple-element.886) | copy-start | bytes 12292
  12.8 98.4 %copy-start.176 = (f32[1024,1]{0,1:T(1,128)}, f32[1024,1]{0,1:T(1,128)S(1)}, u32[]{:S(2)}) copy-start(f32[1024,1]{0,1:T(1,128)S(1)} %get-tuple-element.887) | copy-start | bytes 12292
  12.9 98.4 %copy-start.178 = (f32[1024,1]{0,1:T(1,128)}, f32[1024,1]{0,1:T(1,128)S(1)}, u32[]{:S(2)}) copy-start(f32[1024,1]{0,1:T(1,128)S(1)} %get-tuple-element.885) | copy-start | bytes 12292
  15.9 92.3 %copy-start.160 = (f32[1,2048]{1,0:T(1,128)}, f32[1,2048]{1,0:T(1,128)S(1)}, u32[]{:S(2)}) copy-start(f32[1,2048]{1,0:T(1,128)S(1)} %get-tuple-element.882) | copy-start | bytes 24580
  15.9 92.3 %copy-start.89 = (bf16[128,2048]{1,0:T(8,128)(2,1)S(1)}, bf16[128,2048]{1,0:T(8,128)(2,1)}, u32[]{:S(2)}) copy-start(bf16[128,2048]{1,0:T(8,128)(2,1)} %param.21) | copy-start | bytes 1572868
  115.2 509.6 %all-reduce.133.cloned.1.call-start = ((), (), s32[]{:S(2)}) async-start(), calls=%async_computation.9 | async-start | bytes 2097152 | tf_op jit(solution)/shard_map/psum | solution.py:213
  568.3 56.6 %copy-start.90 = (bf16[128,2048]{1,0:T(8,128)(2,1)S(1)}, bf16[128,2048]{1,0:T(8,128)(2,1)}, u32[]{:S(2)}) copy-start(bf16[128,2048]{1,0:T(8,128)(2,1)} %param.21) | copy-start | bytes 1572868
  570.8 55.6 %copy-start.162 = (f32[1,2048]{1,0:T(1,128)S(1)}, f32[1,2048]{1,0:T(1,128)}, u32[]{:S(2)}) copy-start(f32[1,2048]{1,0:T(1,128)} %get-tuple-element.881) | copy-start | bytes 24580
  570.8 145.3 %all-gather.12.cloned.1.call-start = ((), (), s32[]{:S(2)}) async-start(), calls=%async_computation.10 | async-start | bytes 18874368 | tf_op jit(solution)/shard_map/all_gather | solution.py:190
  571.4 200.9 %all-gather.14.cloned.1.call-start = ((), (), s32[]{:S(2)}) async-start(), calls=%async_computation.11 | async-start | bytes 9437184 | tf_op jit(solution)/shard_map/all_gather | solution.py:191
  572.0 259.3 %all-reduce.135.cloned.1.call-start = ((), (), s32[]{:S(2)}) async-start(), calls=%async_computation.12 | async-start | bytes 2097152 | tf_op jit(solution)/shard_map/psum | solution.py:213
  626.3 89.8 %copy-start.209 = (f32[128]{0:T(128)}, f32[128]{0:T(128)S(1)}, u32[]{:S(2)}) copy-start(f32[128]{0:T(128)S(1)} %get-tuple-element.749) | copy-start | bytes 1540
  626.3 89.8 %copy-start.198 = (f32[128]{0:T(128)}, f32[128]{0:T(128)S(1)}, u32[]{:S(2)}) copy-start(f32[128]{0:T(128)S(1)} %fusion.136) | copy-start | bytes 1540
  626.5 94.2 %copy-start.111 = (bf16[128,2048]{1,0:T(8,128)(2,1)}, bf16[128,2048]{1,0:T(8,128)(2,1)S(1)}, u32[]{:S(2)}) copy-start(bf16[128,2048]{1,0:T(8,128)(2,1)S(1)} %multiply_convert_fusion.6) | copy-start | bytes 1572868
  779.5 99.0 %all-gather.16.cloned.1.call-start = ((), (), s32[]{:S(2)}) async-start(), calls=%async_computation.13 | async-start | bytes 7077888 | tf_op jit(solution)/shard_map/all_gather | solution.py:190
  780.3 128.2 %all-gather.18.cloned.1.call-start = ((), (), s32[]{:S(2)}) async-start(), calls=%async_computation.14 | async-start | bytes 2359296 | tf_op jit(solution)/shard_map/all_gather | solution.py:191
  781.0 182.6 %all-reduce.137.cloned.1.call-start = ((), (), s32[]{:S(2)}) async-start(), calls=%async_computation.15 | async-start | bytes 2097152 | tf_op jit(solution)/shard_map/psum | solution.py:213
  911.9 143.2 %all-gather.20.cloned.1.call-start = ((), (), s32[]{:S(2)}) async-start(), calls=%async_computation.16 | async-start | bytes 18874368 | tf_op jit(solution)/shard_map/all_gather | solution.py:190
  912.7 198.6 %all-gather.22.cloned.1.call-start = ((), (), s32[]{:S(2)}) async-start(), calls=%async_computation.17 | async-start | bytes 9437184 | tf_op jit(solution)/shard_map/all_gather | solution.py:191
  913.3 267.4 %all-reduce.139.cloned.1.call-start = ((), (), s32[]{:S(2)}) async-start(), calls=%async_computation.18 | async-start | bytes 2097152 | tf_op jit(solution)/shard_map/psum | solution.py:217
  965.1 218.4 %copy-start.66 = (f32[128,2048]{1,0:T(8,128)}, f32[128,2048]{1,0:T(8,128)S(1)}, u32[]{:S(2)}) copy-start(f32[128,2048]{1,0:T(8,128)S(1)} %get-tuple-element.746) | copy-start | bytes 3145732
  1128.9 120.6 %all-reduce.141.cloned.1.call-start = ((), (), s32[]{:S(2)}) async-start(), calls=%async_computation.19 | async-start | bytes 2097152 | tf_op jit(solution)/shard_map/psum | solution.py:217
  1192.1 57.4 %copy-start.165 = (f32[1,2048]{1,0:T(1,128)S(1)}, f32[1,2048]{1,0:T(1,128)}, u32[]{:S(2)}) copy-start(f32[1,2048]{1,0:T(1,128)} %get-tuple-element.883) | copy-start | bytes 24580
  1192.1 57.3 %copy-start.201 = (f32[128]{0:T(128)S(1)}, f32[128]{0:T(128)}, u32[]{:S(2)}) copy-start(f32[128]{0:T(128)} %copy-done.200) | copy-start | bytes 1540
  1194.6 57.1 %copy-start.212 = (f32[128]{0:T(128)S(1)}, f32[128]{0:T(128)}, u32[]{:S(2)}) copy-start(f32[128]{0:T(128)} %copy-done.211) | copy-start | bytes 1540
  1194.6 57.1 %copy-start.80 = (f32[128,2048]{1,0:T(8,128)S(1)}, f32[128,2048]{1,0:T(8,128)}, u32[]{:S(2)}) copy-start(f32[128,2048]{1,0:T(8,128)} %copy-done.79) | copy-start | bytes 3145732
  1198.1 123.5 %all-reduce.143.cloned.1.call-start = ((), (), s32[]{:S(2)}) async-start(), calls=%async_computation.20 | async-start | bytes 2097152 | tf_op jit(solution)/shard_map/psum | solution.py:217
  1270.3 1462.2 %all-reduce.147.cloned.1.call-start = ((), (), s32[]{:S(2)}) async-start(), calls=%async_computation.30 | async-start | bytes 4194304 | tf_op jit(solution)/shard_map/psum | solution.py:213
  2486.6 276.3 %reduce-scatter.16.cloned.1.call-start = ((), (), s32[]{:S(2)}) async-start(), calls=%async_computation.25 | async-start | bytes 14155776 | tf_op jit(solution)/shard_map/reduce_scatter | solution.py:204
  2493.0 339.4 %reduce-scatter.22.cloned.1.call-start = ((), (), s32[]{:S(2)}) async-start(), calls=%async_computation.28 | async-start | bytes 18874368 | tf_op jit(solution)/shard_map/reduce_scatter | solution.py:205
  2502.4 449.5 %reduce-scatter.10.cloned.1.call-start = ((), (), s32[]{:S(2)}) async-start(), calls=%async_computation.21 | async-start | bytes 18874368 | tf_op jit(solution)/shard_map/reduce_scatter | solution.py:204
  2511.6 649.0 %reduce-scatter.20.cloned.1.call-start = ((), (), s32[]{:S(2)}) async-start(), calls=%async_computation.27 | async-start | bytes 37748736 | tf_op jit(solution)/shard_map/reduce_scatter | solution.py:204
  2526.7 843.2 %reduce-scatter.12.cloned.1.call-start = ((), (), s32[]{:S(2)}) async-start(), calls=%async_computation.23 | async-start | bytes 37748736 | tf_op jit(solution)/shard_map/reduce_scatter | solution.py:204
  2541.8 883.5 %all-reduce.145.cloned.1.call-start = ((), (), s32[]{:S(2)}) async-start(), calls=%async_computation.22 | async-start | bytes 131072 | tf_op jit(solution)/shard_map/psum | solution.py:374
  2543.7 937.4 %reduce-scatter.18.cloned.1.call-start = ((), (), s32[]{:S(2)}) async-start(), calls=%async_computation.26 | async-start | bytes 4718592 | tf_op jit(solution)/shard_map/reduce_scatter | solution.py:205
  2546.5 1054.5 %reduce-scatter.14.cloned.1.call-start = ((), (), s32[]{:S(2)}) async-start(), calls=%async_computation.24 | async-start | bytes 18874368 | tf_op jit(solution)/shard_map/reduce_scatter | solution.py:205
  2564.8 157.3 %copy-start.208 = (u32[32]{0:T(128)S(1)}, u32[32]{0:T(128)}, u32[]{:S(2)}) copy-start(u32[32]{0:T(128)} %constant.384) | copy-start | bytes 388
  2564.8 158.6 %copy-start.187 = (f32[1024]{0:T(1024)S(1)}, f32[1024]{0:T(1024)}, u32[]{:S(2)}) copy-start(f32[1024]{0:T(1024)} %get-tuple-element.874) | copy-start | bytes 12292
  2564.8 158.6 %copy-start.188 = (f32[1024]{0:T(1024)S(1)}, f32[1024]{0:T(1024)}, u32[]{:S(2)}) copy-start(f32[1024]{0:T(1024)} %get-tuple-element.659) | copy-start | bytes 12292
  2717.7 6.3 collective-permute-start
  (332 other events, 2972.3 us)
Sparse Core Ops, SparseCore 0:
  9.9 41.9 all-gather.23
  53.8 54.3 all-gather.9
  115.4 31.7 all-reduce.130
  570.9 53.8 all-reduce.132
  626.6 89.4 all-gather.11
  717.9 54.3 all-gather.13
  779.7 51.5 all-reduce.134
  833.4 45.1 all-gather.15
  880.6 27.8 all-gather.17
  912.0 51.5 all-reduce.136
  965.6 89.4 all-gather.19
  1056.8 54.3 all-gather.21
  1129.0 51.5 all-reduce.138
  1198.2 51.1 all-reduce.140
  1270.4 51.1 all-reduce.142
  2486.7 89.1 all-reduce.146
  2579.2 134.2 reduce-scatter.15
  2717.0 115.3 reduce-scatter.21
  2835.9 115.9 reduce-scatter.9
  2955.3 205.2 reduce-scatter.19
  3164.6 205.2 reduce-scatter.11
  3373.5 51.7 all-reduce.144
  3429.6 51.4 reduce-scatter.17
  3485.1 115.8 reduce-scatter.13
where the time goes:
time: 3670 us; the launch traced here: 3610 us
  waiting for transfers between devices  1580 us (43%)
  local copies, waits for them, and re-layouts  1200 us (33%)
  other arithmetic  425 us (12%)
  blocking collectives  190 us (5%)
  matrix products  183 us (5%)
    pad x156, local copies, waits for them, and re-layouts, advance(): lax.associative_scan(combine_pairs, (decay_rate, driven), axis=1)  1060 us
    reduce_scatter x4, waiting for transfers between devices, spread_grads(): lax.psum_scatter(joined, 'dp', scatter_dimension=0, tiled=True)  527 us
    all_gather x4, waiting for transfers between devices, collect(): lax.all_gather(stacked, 'dp', axis=1, tiled=True)  273 us
    reduce_scatter x3, waiting for transfers between devices, spread_grads(): lax.psum_scatter(row_block, 'dp', scatter_dimension=0, tiled=True)  242 us
    psum x4, waiting for transfers between devices, branch_total(): return lax.psum(piece_sum, 'tensor')  153 us
    unnamed x1, blocking collectives  152 us
    all_gather x4, waiting for transfers between devices, collect(): lax.all_gather(row_block, 'dp', axis=0, tiled=True)  149 us
    psum x3, waiting for transfers between devices, input_total(): return lax.psum(piece_sum, 'tensor')  145 us
  transfers between devices with their start and end apart: 25, of which 23 were waited for; matrix products, arithmetic and copies ran while one was open for 9% of the time, Pallas kernels for 0%

commit v1 on v0

--- a/solution.py
+++ b/solution.py
@@ -4,6 +4,8 @@
 import jax
 import jax.numpy as jnp
 from jax import lax
+from jax.experimental import pallas as pl
+from jax.experimental.pallas import tpu as pltpu
 from jax.sharding import PartitionSpec as P
 
 STATE = 16
@@ -15,7 +17,6 @@
 
 
 EPS = 1e-05
-SCAN_BLOCK = 64
 NEG_FILL = -1e30
 
 
@@ -69,56 +70,178 @@
     return jax.nn.silu(total)
 
 
-def combine_pairs(earlier, later):
-    return (earlier[0] * later[0], later[0] * earlier[1] + later[1])
-
-
-def blocked_scan(step_size, channel_in, input_map, output_map, keeping, rates, block_rows):
-    groups, length, channels = step_size.shape
-    block_count = length // block_rows
-
-    def to_blocks(values):
-        shaped = values.reshape((groups, block_count, block_rows) + values.shape[2:])
-        return jnp.moveaxis(shaped, 1, 0)
-
-    def advance(carry_state, pieces):
-        step_block, channel_block, input_block, output_block, keep_block = pieces
-        decay_rate = jnp.exp(step_block[..., None] * rates) * keep_block[..., None, None]
-        driven = (step_block * channel_block)[..., None] * input_block[:, :, None, :]
-        decay_run, driven_run = lax.associative_scan(combine_pairs, (decay_rate, driven), axis=1)
-        states = decay_run * carry_state[:, None] + driven_run
-        return (states[:, -1], jnp.sum(states * output_block[:, :, None, :], axis=-1))
-
-    zero_state = jnp.zeros((groups, channels, rates.shape[1]), step_size.dtype)
-    pieces = (
-        to_blocks(step_size),
-        to_blocks(channel_in),
-        to_blocks(input_map),
-        to_blocks(output_map),
-        to_blocks(keeping),
-    )
-    _, outputs = lax.scan(jax.checkpoint(advance), zero_state, pieces)
-    return jnp.moveaxis(outputs, 0, 1).reshape(groups, length, channels)
-
-
-def selective_scan(
-    starts, channel_in, step_raw, mixed_rows, gate_half, step_bias, decay_log, skip_gain
+LANES = 128
+
+
+def softplus(v):
+    return jnp.maximum(v, 0.0) + jnp.log1p(jnp.exp(-jnp.abs(v)))
+
+
+def scan_forward_kernel(
+    groups, length, keep_ref, chan_ref, raw_ref, gate_ref, bias_ref, rate_ref, skip_ref, in_ref, out_ref,
+    mixed_ref, step_s, drive_s, y_s,
 ):
-    step_size = jax.nn.softplus(step_raw + step_bias)
-    input_map = mixed_rows[:, DT_RANK : DT_RANK + STATE]
-    output_map = mixed_rows[:, DT_RANK + STATE :]
-    keeping = 1.0 - starts.astype(jnp.float32)
-    block_rows = min(SCAN_BLOCK, channel_in.shape[0])
-    scanned = blocked_scan(
-        step_size[None],
-        channel_in[None],
-        input_map[None],
-        output_map[None],
-        keeping[None],
-        -jnp.exp(decay_log),
-        block_rows,
-    )[0]
-    return (scanned + skip_gain * channel_in) * jax.nn.silu(gate_half)
+    width = chan_ref.shape[1]
+    blocks = width // LANES
+    step_s[...] = softplus(raw_ref[...] + bias_ref[...])
+    drive_s[...] = step_s[...] * chan_ref[...].astype(jnp.float32)
+    rates = [rate_ref[:, pl.ds(b * LANES, LANES)] for b in range(blocks)]
+
+    def advance(t, states):
+        fresh = []
+        for g in range(groups):
+            row = g * length + t
+            keep = keep_ref[row]
+            input_map = in_ref[row]
+            output_map = out_ref[row]
+            for b in range(blocks):
+                lanes = pl.ds(b * LANES, LANES)
+                decay = jnp.exp(step_s[pl.ds(row, 1), lanes] * rates[b]) * keep
+                state = decay * states[g * blocks + b] + drive_s[pl.ds(row, 1), lanes] * input_map
+                y_s[pl.ds(row, 1), lanes] = jnp.sum(state * output_map, axis=0, keepdims=True)
+                fresh.append(state)
+        return tuple(fresh)
+
+    zero = jnp.zeros((STATE, LANES), jnp.float32)
+    lax.fori_loop(0, length, advance, (zero,) * (groups * blocks))
+    gate = gate_ref[...]
+    silu = gate / (1.0 + jnp.exp(-gate))
+    mixed_ref[...] = (
+        (y_s[...] + skip_ref[...] * chan_ref[...].astype(jnp.float32)) * silu
+    ).astype(mixed_ref.dtype)
+
+
+def scan_forward(keep, channel, step_raw, gate_half, step_bias, rates_t, skip_gain, in_wide, out_wide, groups, width):
+    tokens, channels = channel.shape
+    column = pl.BlockSpec((tokens, width), lambda i: (0, i))
+    row = pl.BlockSpec((1, width), lambda i: (0, i))
+    maps = pl.BlockSpec((tokens, STATE, LANES), lambda i: (0, 0, 0))
+    return pl.pallas_call(
+        partial(scan_forward_kernel, groups, tokens // groups),
+        grid=(channels // width,),
+        in_specs=[
+            pl.BlockSpec(memory_space=pltpu.SMEM), column, column, column, row,
+            pl.BlockSpec((STATE, width), lambda i: (0, i)), row, maps, maps,
+        ],
+        out_specs=column,
+        out_shape=jax.ShapeDtypeStruct((tokens, channels), jnp.bfloat16),
+        scratch_shapes=[pltpu.VMEM((tokens, width), jnp.float32)] * 3,
+        compiler_params=pltpu.CompilerParams(vmem_limit_bytes=48 << 20),
+        cost_estimate=pl.CostEstimate(flops=1, bytes_accessed=28 << 20, transcendentals=0),
+        name="scan_forward",
+    )(keep, channel, step_raw, gate_half, step_bias[None], rates_t, skip_gain[None], in_wide, out_wide)
+
+
+def scan_backward_kernel(
+    groups, length, keep_ref, chan_ref, raw_ref, gate_ref, dmix_ref, bias_ref, rate_ref, skip_ref, in_ref, out_ref,
+    dchan_ref, draw_ref, dgate_ref, din_ref, dout_ref, dbias_ref, drate_ref, dskip_ref,
+    step_s, drive_s, y_s, dy_s, dd_s, ds_s, state_s, decay_s,
+):
+    width = chan_ref.shape[1]
+    blocks = width // LANES
+    chan = chan_ref[...].astype(jnp.float32)
+    step_s[...] = softplus(raw_ref[...] + bias_ref[...])
+    drive_s[...] = step_s[...] * chan
+    gate = gate_ref[...]
+    sig = 1.0 / (1.0 + jnp.exp(-gate))
+    dy_s[...] = dmix_ref[...] * (gate * sig)
+    rates = [rate_ref[:, pl.ds(b * LANES, LANES)] for b in range(blocks)]
+
+    @pl.when(pl.program_id(0) == 0)
+    def _():
+        din_ref[...] = jnp.zeros_like(din_ref)
+        dout_ref[...] = jnp.zeros_like(dout_ref)
+
+    def advance(t, states):
+        fresh = []
+        for g in range(groups):
+            row = g * length + t
+            keep = keep_ref[row]
+            input_map = in_ref[row]
+            output_map = out_ref[row]
+            total = None
+            for b in range(blocks):
+                lanes = pl.ds(b * LANES, LANES)
+                decay = jnp.exp(step_s[pl.ds(row, 1), lanes] * rates[b]) * keep
+                decay_s[row, :, lanes] = decay
+                carried = decay * states[g * blocks + b]
+                state_s[row, :, lanes] = carried
+                state = carried + drive_s[pl.ds(row, 1), lanes] * input_map
+                y_s[pl.ds(row, 1), lanes] = jnp.sum(state * output_map, axis=0, keepdims=True)
+                term = state * dy_s[pl.ds(row, 1), lanes]
+                total = term if total is None else total + term
+                fresh.append(state)
+            dout_ref[row] += total
+        return tuple(fresh)
+
+    zero = jnp.zeros((STATE, LANES), jnp.float32)
+    count = groups * blocks
+    lax.fori_loop(0, length, advance, (zero,) * count)
+
+    def retreat(back, carry):
+        t = length - 1 - back
+        fresh, rate_sums = [], []
+        for g in range(groups):
+            row = g * length + t
+            input_map = in_ref[row]
+            output_map = out_ref[row]
+            total = None
+            for b in range(blocks):
+                lanes = pl.ds(b * LANES, LANES)
+                at = g * blocks + b
+                dstate = carry[0][at] + dy_s[pl.ds(row, 1), lanes] * output_map
+                dlog = dstate * state_s[row, :, lanes]
+                dd_s[pl.ds(row, 1), lanes] = jnp.sum(dstate * input_map, axis=0, keepdims=True)
+                ds_s[pl.ds(row, 1), lanes] = jnp.sum(dlog * rates[b], axis=0, keepdims=True)
+                term = dstate * drive_s[pl.ds(row, 1), lanes]
+                total = term if total is None else total + term
+                rate_sums.append(carry[1][at] + dlog * step_s[pl.ds(row, 1), lanes])
+                fresh.append(dstate * decay_s[row, :, lanes])
+            din_ref[row] += total
+        return (tuple(fresh), tuple(rate_sums))
+
+    _, rate_sums = lax.fori_loop(0, length, retreat, ((zero,) * count, (zero,) * count))
+    for b in range(blocks):
+        lanes = pl.ds(b * LANES, LANES)
+        drate_ref[:, lanes] = rates[b] * sum(rate_sums[g * blocks + b] for g in range(groups))
+    direct = y_s[...] + skip_ref[...] * chan
+    dgate_ref[...] = (dmix_ref[...] * direct * (sig * (1.0 + gate * (1.0 - sig)))).astype(dgate_ref.dtype)
+    dskip_ref[...] = jnp.sum(dy_s[...] * chan, axis=0, keepdims=True)
+    dchan_ref[...] = dd_s[...] * step_s[...] + skip_ref[...] * dy_s[...]
+    shifted = raw_ref[...] + bias_ref[...]
+    draw = (ds_s[...] + dd_s[...] * chan) / (1.0 + jnp.exp(-shifted))
+    draw_ref[...] = draw.astype(draw_ref.dtype)
+    dbias_ref[...] = jnp.sum(draw, axis=0, keepdims=True)
+
+
+def scan_backward(
+    keep, channel, step_raw, gate_half, dmixed, step_bias, rates_t, skip_gain, in_wide, out_wide, groups, width
+):
+    tokens, channels = channel.shape
+    column = pl.BlockSpec((tokens, width), lambda i: (0, i))
+    row = pl.BlockSpec((1, width), lambda i: (0, i))
+    states = pl.BlockSpec((STATE, width), lambda i: (0, i))
+    maps = pl.BlockSpec((tokens, STATE, LANES), lambda i: (0, 0, 0))
+    sheet = jax.ShapeDtypeStruct((tokens, channels), jnp.float32)
+    low = jax.ShapeDtypeStruct((tokens, channels), jnp.bfloat16)
+    wide = jax.ShapeDtypeStruct((tokens, STATE, LANES), jnp.float32)
+    line = jax.ShapeDtypeStruct((1, channels), jnp.float32)
+    return pl.pallas_call(
+        partial(scan_backward_kernel, groups, tokens // groups),
+        grid=(channels // width,),
+        in_specs=[
+            pl.BlockSpec(memory_space=pltpu.SMEM), column, column, column, column, row, states, row, maps, maps,
+        ],
+        out_specs=[column, column, column, maps, maps, row, states, row],
+        out_shape=[
+            sheet, low, low, wide, wide, line, jax.ShapeDtypeStruct((STATE, channels), jnp.float32), line,
+        ],
+        scratch_shapes=[pltpu.VMEM((tokens, width), jnp.float32)] * 6
+        + [pltpu.VMEM((tokens, STATE, width), jnp.float32)] * 2,
+        compiler_params=pltpu.CompilerParams(vmem_limit_bytes=56 << 20),
+        cost_estimate=pl.CostEstimate(flops=1, bytes_accessed=75 << 20, transcendentals=0),
+        name="scan_backward",
+    )(keep, channel, step_raw, gate_half, dmixed, step_bias[None], rates_t, skip_gain[None], in_wide, out_wide)
 
 
 def attention_scores(query, keys, allowed):
@@ -192,21 +315,14 @@
     )
 
 
-def collect_again(stacked, row_block):
-    return (
-        lax.all_gather(stacked, "dp", axis=1, tiled=True),
-        lax.all_gather(row_block, "dp", axis=0, tiled=True),
-    )
-
-
 def spread_grads(joined, row_block, count):
     summed = (
-        lax.psum_scatter(joined, "dp", scatter_dimension=0, tiled=True),
-        lax.psum_scatter(row_block, "dp", scatter_dimension=0, tiled=True),
+        lax.psum_scatter(joined.astype(jnp.bfloat16), "dp", scatter_dimension=0, tiled=True),
+        lax.psum_scatter(row_block.astype(jnp.bfloat16), "dp", scatter_dimension=0, tiled=True),
     )
     rows_here = summed[0].shape[0]
     restacked = jnp.transpose(summed[0].reshape(rows_here, count, -1), (1, 0, 2))
-    return (restacked, summed[1])
+    return (restacked.astype(jnp.float32), summed[1].astype(jnp.float32))
 
 
 def branch_total(piece_sum):
@@ -251,17 +367,15 @@
     mix_rows = lax.psum(project_t(channel_low, mixer_mats[width : width + PROJ_OUT]), "tensor")
     rank_low = mix_rows[:, :DT_RANK].astype(jnp.bfloat16)
     step_raw = project(rank_low, mixer_mats[width + PROJ_OUT :])
-    scanned, scan_back = jax.vjp(
-        partial(selective_scan, starts),
-        channel_low.astype(jnp.float32),
-        step_raw,
-        mix_rows,
-        gate_half,
-        step_bias,
-        decay_log,
-        skip_gain,
-    )
-    mixer_low = scanned.astype(jnp.bfloat16)
+    groups = seq_lengths.shape[0]
+    keeping = 1.0 - starts.astype(jnp.float32)
+    rates_t = -jnp.exp(decay_log).T
+    wide = (tokens, STATE, LANES)
+    in_wide = jnp.broadcast_to(mix_rows[:, DT_RANK : DT_RANK + STATE, None], wide)
+    out_wide = jnp.broadcast_to(mix_rows[:, DT_RANK + STATE :, None], wide)
+    mixer_low = scan_forward(
+        keeping, channel_low, step_raw, gate_half, step_bias, rates_t, skip_gain, in_wide, out_wide, groups, LANES
+    )
     stream_one = stream_zero + branch_total(project_t(mixer_low, mixer_mats[:width]))
     early_stack, early_mat = collect(early_gate_up, early_down)
     second_normed, second_back = jax.vjp(rms_norm, stream_one, norm_gains[1])
@@ -296,14 +410,14 @@
     late_part, late_gate, late_up, late_hidden = ffn_forward(fourth_low, late_stack, late_mat)
     output = stream_three + branch_total(late_part)
     grad_three = output_grad.astype(jnp.float32)
-    late_pair = collect_again(late_gate_up, late_down)
+    late_pair = (late_stack, late_mat)
     grad_fourth, late_joined, late_mat_grad = ffn_backward(
         output_grad, fourth_low, late_gate, late_up, late_hidden, late_pair[0], late_pair[1]
     )
     grad_stream, gain_four = fourth_back(input_total(grad_fourth))
     grad_three = grad_three + grad_stream
     late_grads = spread_grads(late_joined, late_mat_grad, 2)
-    focus_pair = collect_again(attention_in, attention_out)
+    focus_pair = (focus_stack, focus_mat)
     grad_branch_low = grad_three.astype(jnp.bfloat16)
     focus_mat_grad = outer_rows(grad_branch_low, attended_low)
     grad_attended = (
@@ -326,7 +440,7 @@
     grad_stream, gain_three = third_back(input_total(grad_third))
     grad_two = grad_three + grad_stream
     focus_grads = spread_grads(focus_joined, focus_mat_grad, 3)
-    early_pair = collect_again(early_gate_up, early_down)
+    early_pair = (early_stack, early_mat)
     grad_second, early_joined, early_mat_grad = ffn_backward(
         grad_two.astype(jnp.bfloat16),
         second_low,
@@ -339,31 +453,33 @@
     grad_stream, gain_two = second_back(input_total(grad_second))
     grad_one = grad_two + grad_stream
     early_grads = spread_grads(early_joined, early_mat_grad, 2)
-    mixer_pair = collect_again(mixer_in, mixer_rows)
+    mixer_pair = (mixer_stack, mixer_mats)
     grad_mixer_low = grad_one.astype(jnp.bfloat16)
     out_mat_grad = outer_rows(grad_mixer_low, mixer_low)
     grad_scanned = project(grad_mixer_low, mixer_pair[1][:width])
     (
         grad_channel,
-        grad_step,
-        grad_rows_scan,
-        grad_gate,
+        grad_step_low,
+        gate_low,
+        in_sums,
+        out_sums,
         step_bias_grad,
         decay_log_grad,
         skip_gain_grad,
-    ) = scan_back(grad_scanned)
-    grad_step_low = grad_step.astype(jnp.bfloat16)
+    ) = scan_backward(
+        keeping, channel_low, step_raw, gate_half, grad_scanned, step_bias, rates_t, skip_gain, in_wide, out_wide,
+        groups, LANES,
+    )
     step_mat_grad = outer_rows(rank_low, grad_step_low)
     grad_rank = project_t(grad_step_low, mixer_pair[1][width + PROJ_OUT :])
     grad_rows = lax.psum(
-        jnp.concatenate([grad_rank, grad_rows_scan[:, DT_RANK:]], axis=1), "tensor"
+        jnp.concatenate([grad_rank, jnp.sum(in_sums, axis=-1), jnp.sum(out_sums, axis=-1)], axis=1), "tensor"
     )
     grad_rows_low = grad_rows.astype(jnp.bfloat16)
     select_mat_grad = outer_rows(grad_rows_low, channel_low)
     grad_channel = grad_channel + project(grad_rows_low, mixer_pair[1][width : width + PROJ_OUT])
     grad_conv_in, conv_weight_grad, conv_bias_grad = conv_back(grad_channel)
     conv_low = grad_conv_in.astype(jnp.bfloat16)
-    gate_low = grad_gate.astype(jnp.bfloat16)
     mixer_joined = outer_rows(first_low, jnp.concatenate([conv_low, gate_low], axis=1))
     grad_first = project_t(conv_low, mixer_pair[0][0]) + project_t(gate_low, mixer_pair[0][1])
     grad_stream, gain_one = first_back(input_total(grad_first))
@@ -376,9 +492,9 @@
             jnp.stack([gain_one, gain_two, gain_three, gain_four]),
             conv_weight_grad,
             conv_bias_grad,
-            step_bias_grad,
-            decay_log_grad,
-            skip_gain_grad,
+            step_bias_grad[0],
+            decay_log_grad.T,
+            skip_gain_grad[0],
         ),
         "dp",
     )
@@ -402,9 +518,739 @@
     )
 
 
+MESH = pl.DeviceIdType.MESH
+
+
+def turns(group):
+    return [turned for turned in (6, 2, 4) if turned & group == turned]
+
+
+class Place:
+    def __init__(self, ways):
+        self.spot = lax.axis_index("dp")
+        self.depth = lax.axis_index("tensor")
+        self.ways = ways
+        self.core = lax.rem(self.spot, 2)
+        self.partner = self.spot + 1 - 2 * self.core
+
+    def bit(self, axis, turned):
+        value = lax.rem(self.spot // axis, 2)
+        return 1 - value if turned & axis else value
+
+    def across(self, turned):
+        move = 0
+        for axis in (2, 4):
+            if turned & axis:
+                move = move + axis * (1 - 2 * self.bit(axis, 0))
+        return self.spot + move
+
+    def side(self, group, turned=0):
+        if group == 6:
+            return self.bit(2, turned) + 2 * self.bit(4, turned)
+        return self.bit(group, turned) if group else 0
+
+    def along(self, offset):
+        return lax.rem(self.depth + offset, self.ways)
+
+
+def send(source, target, sems, at, spot, depth):
+    copy = pltpu.make_async_remote_copy(
+        src_ref=source,
+        dst_ref=target,
+        send_sem=sems[0].at[at],
+        recv_sem=sems[1].at[at],
+        device_id=(spot, depth),
+        device_id_type=MESH,
+    )
+    copy.start()
+    return copy
+
+
+def greet(place, ways):
+    barrier = pltpu.get_barrier_semaphore()
+    peers = [(place.partner, place.depth)]
+    peers += [(place.across(turned), place.depth) for turned in ways]
+    peers += [(place.spot, place.along(offset)) for offset in range(1, place.ways)]
+    for peer in peers:
+        pl.semaphore_signal(barrier, inc=1, device_id=peer, device_id_type=MESH)
+    pl.semaphore_wait(barrier, len(peers))
+
+
+def rows_at(start, size, unit):
+    return pl.ds(pl.multiple_of(start * unit, unit), size)
+
+
+def reduce_stage(place, group, rows, parts, part_ref, near_s, sum_s, far_s, deep_s, sems):
+    share = rows // place.ways
+    step = part_ref.shape[1] // parts
+    ways = turns(group) + [0]
+    sides = len(ways)
+    near = {}
+    for part in range(parts):
+        lanes = pl.ds(part * step, step)
+        for at, turned in enumerate(ways):
+            side = place.side(group, turned)
+            near[part, turned] = send(
+                part_ref.at[rows_at(side * 2 + 1 - place.core, rows, rows), lanes],
+                near_s.at[rows_at(side, rows, rows), lanes],
+                sems["near"], part * sides + at, place.partner, place.depth,
+            )
+
+    def joined(side, lanes):
+        own = part_ref[rows_at(side * 2 + place.core, rows, rows), lanes].astype(jnp.float32)
+        return own + near_s[rows_at(side, rows, rows), lanes].astype(jnp.float32)
+
+    far = {}
+    for part in range(parts):
+        lanes = pl.ds(part * step, step)
+        for at, turned in enumerate(ways[:-1]):
+            side = place.side(group, turned)
+            near[part, turned].wait_recv()
+            sum_s[rows_at(side, rows, rows), lanes] = joined(side, lanes).astype(sum_s.dtype)
+            far[part, turned] = send(
+                sum_s.at[rows_at(side, rows, rows), lanes], far_s.at[at, :, lanes],
+                sems["far"], part * (sides - 1) + at, place.across(turned), place.depth,
+            )
+    deep = []
+    mine = place.side(group)
+    for part in range(parts):
+        lanes = pl.ds(part * step, step)
+        near[part, 0].wait_recv()
+        total = joined(mine, lanes)
+        for at, turned in enumerate(ways[:-1]):
+            far[part, turned].wait_recv()
+            total = total + far_s[at, :, lanes].astype(jnp.float32)
+        sum_s[rows_at(mine, rows, rows), lanes] = total.astype(sum_s.dtype)
+        for offset in range(1, place.ways):
+            deep.append(
+                send(
+                    sum_s.at[pl.ds(pl.multiple_of(mine * rows + place.along(offset) * share, share), share), lanes],
+                    deep_s.at[offset - 1, :, lanes],
+                    sems["deep"], part * (place.ways - 1) + offset - 1, place.spot, place.along(offset),
+                )
+            )
+    for copy in deep:
+        copy.wait_recv()
+    total = sum_s[pl.ds(pl.multiple_of(mine * rows + place.depth * share, share), share), :].astype(jnp.float32)
+    for offset in range(1, place.ways):
+        total = total + deep_s[offset - 1].astype(jnp.float32)
+    return total, list(near.values()) + list(far.values()) + deep
+
+
+def gather_stage(place, group, rows, all_ref, sems):
+    share = rows // place.ways
+    ways = turns(group)
+    mine = place.side(group)
+
+    def piece(side, depth):
+        return all_ref.at[pl.ds(pl.multiple_of((side * 2 + place.core) * rows + depth * share, share), share), :]
+
+    own = piece(mine, place.depth)
+    deep = [
+        send(own, own, sems["deep_back"], offset - 1, place.spot, place.along(offset)) for offset in range(1, place.ways)
+    ]
+    far, near = {}, []
+    for offset in range(place.ways):
+        if offset:
+            deep[offset - 1].wait_recv()
+        came = piece(mine, place.along(place.ways - offset) if offset else place.depth)
+        for at, turned in enumerate(ways):
+            far[offset, turned] = send(
+                came, came, sems["far_back"], offset * len(ways) + at, place.across(turned), place.depth
+            )
+        near.append(send(came, came, sems["near_back"], offset, place.partner, place.depth))
+    for offset in range(place.ways):
+        for at, turned in enumerate(ways):
+            far[offset, turned].wait_recv()
+            came = piece(place.side(group, turned), place.along(place.ways - offset) if offset else place.depth)
+            near.append(
+                send(came, came, sems["near_back"], (1 + at) * place.ways + offset, place.partner, place.depth)
+            )
+    for copy in near:
+        copy.wait_recv()
+    return deep + list(far.values()) + near
+
+
+def spread_stage(place, rows, all_ref, sems):
+    share = rows // place.ways
+    own = all_ref.at[pl.ds(pl.multiple_of(place.depth * share, share), share), :]
+    deep = [
+        send(own, own, sems["deep_back"], offset - 1, place.spot, place.along(offset)) for offset in range(1, place.ways)
+    ]
+    return deep
+
+
+def small_stage(place, half, sum_ref, small_s, sems):
+    near = [
+        send(
+            sum_ref.at[pl.ds(part * half, half), :], small_s.at[part], sems["small"], part, place.partner, place.depth
+        )
+        for part in range(2)
+    ]
+    for copy in near:
+        copy.wait()
+    mine = pl.ds(pl.multiple_of(place.core * half, half), half)
+    small_s[2] = sum_ref[mine, :] + small_s[place.core]
+    chips = [
+        send(small_s.at[2], small_s.at[3 + at], sems["small"], 2 + at, spot, place.depth)
+        for at, spot in enumerate((place.across(2), place.across(4), place.across(6)))
+    ]
+    for copy in chips:
+        copy.wait_recv()
+    total = small_s[2] + small_s[3] + small_s[4] + small_s[5]
+    small_s[6] = total
+    deep = [
+        send(
+            small_s.at[6, pl.ds(half - 8, 8), :], small_s.at[6 + offset, pl.ds(half - 8, 8), :],
+            sems["small"], 4 + offset, place.spot, place.along(offset),
+        )
+        for offset in range(1, place.ways)
+    ]
+    for copy in deep:
+        copy.wait_recv()
+    gains = small_s[6, half - 8 : half, :]
+    for offset in range(1, place.ways):
+        gains = gains + small_s[6 + offset, half - 8 : half, :]
+    last = jnp.where(place.core == 1, gains, total[half - 8 : half, :])
+    ready, came = 6 + place.ways, 7 + place.ways
+    small_s[ready] = jnp.concatenate([total[: half - 8, :], last], axis=0)
+    back = send(small_s.at[ready], small_s.at[came], sems["small"], 4 + place.ways, place.partner, place.depth)
+    sum_ref[mine, :] = small_s[ready]
+    back.wait_recv()
+    sum_ref[pl.ds(pl.multiple_of((1 - place.core) * half, half), half), :] = small_s[came]
+    return chips + deep + [back]
+
+
+def sem_shapes(names):
+    shapes = []
+    for count in names.values():
+        shapes += [pltpu.SemaphoreType.DMA((count,))] * 2
+    return shapes
+
+
+def sem_dict(names, refs):
+    return {name: (refs[2 * at], refs[2 * at + 1]) for at, name in enumerate(names)}
+
+
+def edge_kernel(kind, ways, rows, parts, in_group, out_group, names, *refs):
+    place = Place(ways)
+    share = rows // ways
+    refs = list(refs)
+    part_ref = refs.pop(0)
+    if kind == "forward":
+        stream_ref, gain_ref = refs.pop(0), refs.pop(0)
+        all_ref, fresh_ref = refs.pop(0), refs.pop(0)
+    elif kind in ("backward", "last"):
+        stream_ref, gain_ref, grad_ref = refs.pop(0), refs.pop(0), refs.pop(0)
+        small_ref = refs.pop(0) if kind == "last" else None
+        all_ref = refs.pop(0)
+        fresh_ref = refs.pop(0) if kind == "backward" else None
+        dgain_ref = refs.pop(0)
+    else:
+        all_ref = refs.pop(0)
+    near_s, sum_s, far_s, deep_s = refs.pop(0), refs.pop(0), refs.pop(0), refs.pop(0)
+    if kind == "last":
+        low_s, small_s = refs.pop(0), refs.pop(0)
+    sems = sem_dict(names, refs)
+    greet(place, turns(6) if kind == "last" else sorted({*turns(in_group), *turns(out_group)}))
+    total, waiting = reduce_stage(
+        place, in_group, rows, parts, part_ref, near_s, sum_s, far_s, deep_s, sems
+    )
+    if kind == "forward":
+        fresh = stream_ref[...] + total
+        fresh_ref[...] = fresh
+        scale = lax.rsqrt(jnp.mean(fresh * fresh, axis=-1, keepdims=True) + EPS)
+        value = fresh * scale * gain_ref[...]
+    elif kind in ("backward", "last"):
+        stream = stream_ref[...]
+        scale = lax.rsqrt(jnp.mean(stream * stream, axis=-1, keepdims=True) + EPS)
+        leaned = total * gain_ref[...]
+        inner = jnp.mean(leaned * stream, axis=-1, keepdims=True)
+        value = grad_ref[...] + scale * leaned - stream * (scale * scale * scale * inner)
+        dgain = jnp.sum(total * stream * scale, axis=0, keepdims=True)
+        if kind == "backward":
+            dgain_ref[...] = dgain
+            fresh_ref[...] = value
+    else:
+        value = total
+    if kind == "last":
+        low_s[pl.ds(pl.multiple_of(place.depth * share, share), share), :] = value.astype(low_s.dtype)
+        half, span = small_ref.shape[0] // 2, small_ref.shape[1]
+        dgain_ref[...] = small_ref[...]
+        for at in range(dgain.shape[1] // span):
+            dgain_ref[pl.ds(2 * half - 8 + at, 1), :] = dgain[:, at * span : (at + 1) * span]
+        spread = spread_stage(place, rows, low_s, sems)
+        waiting += spread + small_stage(place, half, dgain_ref, small_s, sems)
+        for copy in spread:
+            copy.wait_recv()
+        all_ref[...] = low_s[...].astype(jnp.float32)
+    else:
+        spot = pl.multiple_of((place.side(out_group) * 2 + place.core) * rows + place.depth * share, share)
+        all_ref[pl.ds(spot, share), :] = value.astype(all_ref.dtype)
+        waiting += gather_stage(place, out_group, rows, all_ref, sems)
+    for copy in waiting:
+        copy.wait_send()
+
+
+def edge(kind, part, extras, ways, rows, parts, in_group, out_group, ident, name):
+    width = part.shape[1]
+    share = rows // ways
+    in_far, out_far = len(turns(in_group)), len(turns(out_group or 0))
+    in_sides, out_sides = in_far + 1, out_far + 1
+    dtype = part.dtype
+    line = jax.ShapeDtypeStruct((1, width), jnp.float32)
+    strip = jax.ShapeDtypeStruct((share, width), jnp.float32)
+    whole = jax.ShapeDtypeStruct((out_sides * 2 * rows, width), dtype)
+    outs = {
+        "forward": [whole, strip],
+        "backward": [whole, strip, line],
+        "last": [jax.ShapeDtypeStruct((rows, width), jnp.float32)]
+        + [jax.ShapeDtypeStruct(extra.shape, extra.dtype) for extra in extras[3:]],
+        "sum": [whole],
+    }[kind]
+    names = {"near": parts * in_sides, "far": parts * in_far, "deep": parts * (ways - 1), "deep_back": ways - 1}
+    if kind == "last":
+        names["small"] = 5 + ways
+    else:
+        names.update({"far_back": ways * out_far, "near_back": ways * out_sides})
+    if not in_group:
+        del names["far"]
+    if kind != "last" and not out_group:
+        del names["far_back"]
+    scratch = [
+        pltpu.VMEM((in_sides * rows, width), dtype),
+        pltpu.VMEM((in_sides * rows, width), dtype),
+        pltpu.VMEM((max(in_far, 1), rows if in_far else 16, width), dtype),
+        pltpu.VMEM((ways - 1, share, width), dtype),
+    ]
+    if kind == "last":
+        scratch.append(pltpu.VMEM((rows, width), dtype))
+        scratch.append(pltpu.VMEM((8 + ways, extras[3].shape[0] // 2, extras[3].shape[1]), jnp.float32))
+    vmem = pl.BlockSpec(memory_space=pltpu.VMEM)
+    return pl.pallas_call(
+        partial(edge_kernel, kind, ways, rows, parts, in_group, out_group, names),
+        in_specs=[vmem] * (1 + len(extras)),
+        out_specs=[vmem] * len(outs),
+        out_shape=outs,
+        scratch_shapes=scratch + sem_shapes(names),
+        compiler_params=pltpu.CompilerParams(
+            collective_id=ident, has_side_effects=True, vmem_limit_bytes=40 << 20
+        ),
+        cost_estimate=pl.CostEstimate(flops=1, bytes_accessed=1, transcendentals=0),
+        name=name,
+    )(part, *extras)
+
+
+def opening_kernel(ways, rows, hidden_ref, gain_ref, first_ref, send_sem, recv_sem):
+    place = Place(ways)
+    barrier = pltpu.get_barrier_semaphore()
+    pl.semaphore_signal(barrier, inc=1, device_id=(place.partner, place.depth), device_id_type=MESH)
+    pl.semaphore_wait(barrier, 1)
+    stream = hidden_ref[...].astype(jnp.float32)
+    scale = lax.rsqrt(jnp.mean(stream * stream, axis=-1, keepdims=True) + EPS)
+    first_ref[rows_at(place.core, rows, rows), :] = (stream * scale * gain_ref[...]).astype(jnp.bfloat16)
+    mine = first_ref.at[rows_at(place.core, rows, rows), :]
+    send(mine, mine, (send_sem, recv_sem), 0, place.partner, place.depth).wait()
+
+
+def opening(hidden, gain, ways, ident):
+    rows, width = hidden.shape
+    vmem = pl.BlockSpec(memory_space=pltpu.VMEM)
+    return pl.pallas_call(
+        partial(opening_kernel, ways, rows),
+        in_specs=[vmem] * 2,
+        out_specs=vmem,
+        out_shape=jax.ShapeDtypeStruct((2 * rows, width), jnp.bfloat16),
+        scratch_shapes=[pltpu.SemaphoreType.DMA((1,))] * 2,
+        compiler_params=pltpu.CompilerParams(
+            collective_id=ident, has_side_effects=True, vmem_limit_bytes=40 << 20
+        ),
+        cost_estimate=pl.CostEstimate(flops=1, bytes_accessed=1, transcendentals=0),
+        name="opening",
+    )(hidden, gain)
+
+
+def probs_of(query, keys, allowed):
+    scores = project_t(query, keys) * (1.0 / math.sqrt(HEAD_DIM))
+    scores = jnp.where(allowed, scores, NEG_FILL)
+    shifted = jnp.exp(scores - jnp.max(scores, axis=-1, keepdims=True))
+    return shifted / jnp.sum(shifted, axis=-1, keepdims=True)
+
+
+def allowed_in(down_ref, side_ref, rows, group):
+    shape = (rows, rows)
+    distance = lax.broadcasted_iota(jnp.int32, shape, 0) - lax.broadcasted_iota(jnp.int32, shape, 1)
+    same = down_ref[group * rows : (group + 1) * rows, :] == side_ref[group : group + 1, :]
+    return same & (distance >= 0) & (distance < WINDOW)
+
+
+def attend_kernel(heads, rows, joint_ref, down_ref, side_ref, low_ref, out_ref):
+    low_ref[...] = joint_ref[...].astype(jnp.bfloat16)
+    size = heads * HEAD_DIM
+    for group in range(joint_ref.shape[0] // rows):
+        allowed = allowed_in(down_ref, side_ref, rows, group)
+        span = slice(group * rows, (group + 1) * rows)
+        for head in range(heads):
+            at = slice(head * HEAD_DIM, (head + 1) * HEAD_DIM)
+            query, keys, values = [
+                low_ref[span, part * size + head * HEAD_DIM : part * size + (head + 1) * HEAD_DIM] for part in range(3)
+            ]
+            probs = probs_of(query, keys, allowed)
+            out_ref[span, at] = project(probs.astype(jnp.bfloat16), values).astype(jnp.bfloat16)
+
+
+def attend(joint, down, side, rows):
+    count, size = joint.shape
+    return pl.pallas_call(
+        partial(attend_kernel, size // (3 * HEAD_DIM), rows),
+        out_shape=[
+            jax.ShapeDtypeStruct((count, size), jnp.bfloat16),
+            jax.ShapeDtypeStruct((count, size // 3), jnp.bfloat16),
+        ],
+        compiler_params=pltpu.CompilerParams(vmem_limit_bytes=32 << 20),
+        name="attend",
+    )(joint, down, side)
+
+
+def attend_back_kernel(heads, rows, low_ref, grad_ref, down_ref, side_ref, out_ref):
+    size = heads * HEAD_DIM
+    scale = 1.0 / math.sqrt(HEAD_DIM)
+    for group in range(low_ref.shape[0] // rows):
+        allowed = allowed_in(down_ref, side_ref, rows, group)
+        span = slice(group * rows, (group + 1) * rows)
+        for head in range(heads):
+            places = [slice(part * size + head * HEAD_DIM, part * size + (head + 1) * HEAD_DIM) for part in range(3)]
+            query, keys, values = [low_ref[span, place] for place in places]
+            grad = grad_ref[span, head * HEAD_DIM : (head + 1) * HEAD_DIM].astype(jnp.bfloat16)
+            probs = probs_of(query, keys, allowed)
+            grad_probs = project_t(grad, values)
+            inner = jnp.sum(probs * grad_probs, axis=-1, keepdims=True)
+            grad_scores = (probs * (grad_probs - inner)).astype(jnp.bfloat16)
+            out_ref[span, places[0]] = (project(grad_scores, keys) * scale).astype(jnp.bfloat16)
+            out_ref[span, places[1]] = (outer_rows(grad_scores, query) * scale).astype(jnp.bfloat16)
+            out_ref[span, places[2]] = outer_rows(probs.astype(jnp.bfloat16), grad).astype(jnp.bfloat16)
+
+
+def attend_back(low, grad, down, side, rows):
+    count, size = low.shape
+    return pl.pallas_call(
+        partial(attend_back_kernel, size // (3 * HEAD_DIM), rows),
+        out_shape=jax.ShapeDtypeStruct((count, size), jnp.bfloat16),
+        compiler_params=pltpu.CompilerParams(vmem_limit_bytes=32 << 20),
+        name="attend_back",
+    )(low, grad, down, side)
+
+
+def sub_of(spot, group):
+    if group == 6:
+        return spot
+    return spot % 2 + (2 * ((spot // group) % 2) if group else 0)
+
+
+def subs_of(group):
+    return 2 * (len(turns(group)) + 1)
+
+
+def pull(count, *sets):
+    def cut(block, group, spot):
+        size = block.shape[1] // subs_of(group)
+        return block[:, sub_of(spot, group) * size : (sub_of(spot, group) + 1) * size]
+
+    return jnp.stack(
+        [
+            jnp.concatenate([cut(block, group, spot) for blocks, group in sets for block in blocks], axis=1)
+            for spot in range(count)
+        ]
+    )
+
+
+def swap(stacked):
+    return lax.all_to_all(stacked, "dp", 0, 0, tiled=True)
+
+
+def settle(swapped, group, blocks):
+    subs = subs_of(group)
+    count = swapped.shape[0]
+    size = swapped.shape[2] // blocks
+    sums = []
+    for sub in range(subs):
+        sums.append(sum(swapped[spot].astype(jnp.float32) for spot in range(count) if sub_of(spot, group) == sub))
+    return [
+        jnp.concatenate([one[:, block * size : (block + 1) * size] for one in sums], axis=1) for block in range(blocks)
+    ]
+
+
+def by_half(place, first, second):
+    return [jnp.where(place == 0, first, second), jnp.where(place == 0, second, first)]
+
+
+def after(value, *others):
+    return lax.optimization_barrier((value,) + others)[0]
+
+
+def grouped_body(
+    counts,
+    early_group,
+    focus_group,
+    late_group,
+    hidden_in,
+    seq_lengths,
+    norm_gains,
+    mixer_in,
+    mixer_rows,
+    conv_weight,
+    conv_bias,
+    step_bias,
+    decay_log,
+    skip_gain,
+    early_gate_up,
+    early_down,
+    attention_in,
+    attention_out,
+    late_gate_up,
+    late_down,
+    output_grad,
+):
+    spots, ways = counts
+    rows, width = hidden_in.shape
+    share = rows // ways
+    spot = lax.axis_index("dp")
+    depth = lax.axis_index("tensor")
+    core = spot % 2
+    low = jnp.bfloat16
+
+    def swapped_core(value):
+        return lax.ppermute(value, "dp", [(at, at ^ 1) for at in range(spots)])
+
+    same_core = [[2 * chip + at for chip in range(spots // 2)] for at in range(2)]
+
+    def whole_group(value, group):
+        if group == 6:
+            value = jnp.broadcast_to(value[None], (spots // 2,) + value.shape)
+            value = lax.all_to_all(value, "dp", 0, 0, tiled=True, axis_index_groups=same_core)
+        else:
+            value = value[None]
+        if group in (2, 4):
+            moved = lax.ppermute(value, "dp", [(at, at ^ group) for at in range(spots)])
+            value = jnp.concatenate(by_half((spot // group) % 2, value, moved))
+        return jnp.stack(by_half(core, value, swapped_core(value)), axis=1).reshape(-1, value.shape[-1])
+
+    def group_sum(part, group):
+        part = part.reshape(-1, 2, rows, width)
+        mine, other = by_half(core, part[:, 0], part[:, 1])
+        part = mine + swapped_core(other)
+        if group == 6:
+            part = lax.all_to_all(part, "dp", 0, 0, tiled=True, axis_index_groups=same_core)
+            return jnp.sum(part.astype(jnp.float32), axis=0).astype(low)
+        if group:
+            mine, other = by_half((spot // group) % 2, part[0], part[1])
+            return mine + lax.ppermute(other, "dp", [(at, at ^ group) for at in range(spots)])
+        return part[0]
+
+    in_weights = swap(pull(spots, ([mixer_in[0], mixer_in[1]], 0)))
+
+    other_lengths = swapped_core(seq_lengths)
+    lengths = jnp.where(
+        core == 0, jnp.stack([seq_lengths, other_lengths]), jnp.stack([other_lengths, seq_lengths])
+    )
+    segs, starts = jax.vmap(lambda own: segment_info(own, rows))(lengths)
+    flat_segs = (segs + jnp.arange(2, dtype=jnp.int32)[:, None] * rows).reshape(-1)
+    keeping = 1.0 - starts.reshape(-1).astype(jnp.float32)
+    groups = 2 * seq_lengths.shape[0]
+
+    first_low = opening(hidden_in, norm_gains[0:1], ways, 20)
+    row_weights = swap(after(pull(spots, ([mixer_rows], 0)), in_weights, first_low))
+    stream_zero = lax.dynamic_slice_in_dim(hidden_in, depth * share, share, 0).astype(jnp.float32)
+
+    channels = conv_weight.shape[0] // 2
+
+    def half(values):
+        return lax.dynamic_slice_in_dim(values, core * channels, channels, 0)
+
+    taps, offset, bias, decay, skip = [half(v) for v in (conv_weight, conv_bias, step_bias, decay_log, skip_gain)]
+    in_mat = in_weights.reshape(width, 2 * channels)
+    both = project(first_low, in_mat)
+    conv_in, gate_half = both[:, :channels], both[:, channels:]
+    channel_full, conv_back = jax.vjp(partial(causal_conv, flat_segs), conv_in, taps, offset)
+    channel_low = channel_full.astype(low)
+    row_mat = row_weights.reshape(-1, channels)
+    early_blocks = [early_gate_up[0], early_gate_up[1], early_down]
+    focus_blocks = [attention_in[0], attention_in[1], attention_in[2], attention_out]
+    middle_weights = swap(
+        after(pull(spots, (early_blocks, early_group), (focus_blocks, focus_group)), row_weights, both)
+    ).reshape(width, -1)
+    units = 3 * early_down.shape[1] // subs_of(early_group)
+    early_mat, focus_mat = middle_weights[:, :units], middle_weights[:, units:]
+    out_mat = row_mat[:width]
+    select_mat = row_mat[width : width + PROJ_OUT]
+    step_mat = row_mat[width + PROJ_OUT :]
+
+    def mixed_sum(part, ident, name):
+        padded = jnp.pad(part, ((0, 0), (0, 256 - PROJ_OUT)))
+        return edge("sum", padded, [], ways, rows, 1, 0, 0, ident, name)[0][:, :PROJ_OUT]
+
+    mix_rows = mixed_sum(project_t(channel_low, select_mat), 1, "mix_sum")
+    rank_low = mix_rows[:, :DT_RANK].astype(low)
+    step_raw = project(rank_low, step_mat)
+    rates_t = -jnp.exp(decay).T
+    wide = (2 * rows, STATE, LANES)
+    in_wide = jnp.broadcast_to(mix_rows[:, DT_RANK : DT_RANK + STATE, None], wide)
+    out_wide = jnp.broadcast_to(mix_rows[:, DT_RANK + STATE :, None], wide)
+    mixer_low = scan_forward(
+        keeping, channel_low, step_raw, gate_half, bias, rates_t, skip, in_wide, out_wide, groups, LANES
+    )
+    second_low, stream_one = edge(
+        "forward", project_t(mixer_low, out_mat).astype(low), [stream_zero, norm_gains[1:2]],
+        ways, rows, 4, 0, early_group, 2, "edge_one",
+    )
+
+    late_blocks = [late_gate_up[0], late_gate_up[1], late_down]
+    late_weights = swap(after(pull(spots, (late_blocks, late_group)), middle_weights, second_low))
+
+    def ffn(normed, mat):
+        units = mat.shape[1] // 3
+        both = project(normed, mat[:, : 2 * units])
+        hidden = gated_unit(both[:, :units], both[:, units:]).astype(low)
+        return project_t(hidden, mat[:, 2 * units :]).astype(low), both, hidden
+
+    early_part, early_both, early_hidden = ffn(second_low, early_mat)
+    third_low, stream_two = edge(
+        "forward", early_part, [stream_one, norm_gains[2:3]], ways, rows, 4, early_group, 0, 3, "edge_two"
+    )
+
+    last_grad = whole_group(after(output_grad, late_weights, third_low), late_group)
+    heads_width = focus_mat.shape[1] // 4
+    down, side = flat_segs[:, None], flat_segs.reshape(2, rows)
+    joint_low, attended_low = attend(project(third_low, focus_mat[:, : 3 * heads_width]), down, side, rows)
+    fourth_low, stream_three = edge(
+        "forward", project_t(attended_low, focus_mat[:, 3 * heads_width :]).astype(low),
+        [stream_two, norm_gains[3:4]], ways, rows, 4, 0, late_group, 4, "edge_three",
+    )
+
+    late_mat = late_weights.reshape(width, -1)
+    late_part, late_both, late_hidden = ffn(fourth_low, late_mat)
+
+    def ffn_back(grad_low, normed, both, hidden, mat):
+        units = mat.shape[1] // 3
+        grad_hidden = project(grad_low, mat[:, 2 * units :])
+        _, unit_back = jax.vjp(gated_unit, both[:, :units], both[:, units:])
+        both_low = jnp.concatenate(unit_back(grad_hidden), axis=1).astype(low)
+        grad_normed = project_t(both_low, mat[:, : 2 * units]).astype(low)
+        joint = jnp.concatenate([outer_rows(normed, both_low), outer_rows(grad_low, hidden)], axis=1)
+        return grad_normed, joint.astype(low).reshape(spots, -1, 3 * units)
+
+    grad_fourth, late_joint = ffn_back(last_grad, fourth_low, late_both, late_hidden, late_mat)
+    grad_zero = lax.dynamic_slice_in_dim(output_grad, depth * share, share, 0).astype(jnp.float32)
+    output_part = group_sum(late_part, late_group)
+    grad_low_three, grad_three, gain_four = edge(
+        "backward", after(grad_fourth, output_part), [stream_three, norm_gains[3:4], grad_zero],
+        ways, rows, 4, late_group, 0, 5, "edge_four",
+    )
+    late_swapped = swap(after(late_joint, grad_low_three))
+
+    output_rows = lax.all_to_all(output_part.reshape(ways, share, width), "tensor", 0, 0, tiled=True)
+    output_rows = stream_three + jnp.sum(output_rows.astype(jnp.float32), axis=0)
+    output = lax.all_gather(output_rows, "tensor", axis=0, tiled=True)
+
+    grad_attended = project(grad_low_three, focus_mat[:, 3 * heads_width :])
+    joint_grad = attend_back(joint_low, grad_attended, down, side, rows)
+    grad_low_two, grad_two, gain_three = edge(
+        "backward", project_t(joint_grad, focus_mat[:, : 3 * heads_width]).astype(low),
+        [stream_two, norm_gains[2:3], grad_three], ways, rows, 4, 0, early_group, 6, "edge_five",
+    )
+    focus_joint = jnp.concatenate(
+        [outer_rows(third_low, joint_grad), outer_rows(grad_low_three, attended_low)], axis=1
+    ).astype(low)
+    focus_swapped = swap(after(focus_joint.reshape(spots, -1, 4 * heads_width), late_swapped, grad_low_two))
+
+    grad_second, early_joint = ffn_back(grad_low_two, second_low, early_both, early_hidden, early_mat)
+    grad_low_one, grad_one, gain_two = edge(
+        "backward", after(grad_second, late_swapped), [stream_one, norm_gains[1:2], grad_two],
+        ways, rows, 4, early_group, 0, 7, "edge_six",
+    )
+
+    early_swapped = swap(after(early_joint, focus_swapped, grad_low_one))
+
+    grad_scanned = after(project(grad_low_one, out_mat), focus_swapped)
+    (
+        grad_channel,
+        grad_step_low,
+        gate_low,
+        in_sums,
+        out_sums,
+        bias_grad,
+        decay_grad,
+        skip_grad,
+    ) = scan_backward(
+        keeping, channel_low, step_raw, gate_half, grad_scanned, bias, rates_t, skip, in_wide, out_wide,
+        groups, LANES,
+    )
+    grad_rank = project_t(grad_step_low, step_mat)
+    grad_rows = mixed_sum(
+        jnp.concatenate([grad_rank, jnp.sum(in_sums, axis=-1), jnp.sum(out_sums, axis=-1)], axis=1), 8, "mix_grad_sum"
+    )
+    grad_rows_low = grad_rows.astype(low)
+    rows_joint = jnp.concatenate(
+        [
+            outer_rows(grad_low_one, mixer_low),
+            outer_rows(grad_rows_low, channel_low),
+            outer_rows(rank_low, grad_step_low),
+        ],
+        axis=0,
+    ).astype(low)
+    grad_channel = grad_channel + project(grad_rows_low, select_mat)
+    grad_conv_in, taps_grad, offset_grad = conv_back(grad_channel)
+    conv_low = grad_conv_in.astype(low)
+    in_grad = jnp.concatenate([conv_low, gate_low], axis=1)
+    grad_first = project_t(in_grad, in_mat).astype(low)
+    in_joints = [outer_rows(first_low, grad).astype(low) for grad in (conv_low, gate_low)]
+    mixer_joint = jnp.concatenate(
+        [joint.reshape(spots, -1, channels) for joint in (in_joints[0], in_joints[1], rows_joint)], axis=1
+    )
+    mixer_swapped = swap(after(mixer_joint, early_swapped))
+    lines = jnp.concatenate([taps_grad.T, offset_grad[None], bias_grad, skip_grad, decay_grad], axis=0)
+    lines = jnp.pad(lines, ((0, 1), (0, 0)))
+    blank = jnp.zeros_like(lines)
+    lines = jnp.where(core == 0, jnp.concatenate([lines, blank], axis=1), jnp.concatenate([blank, lines], axis=1))
+    gains = jnp.concatenate([jnp.zeros_like(gain_two), gain_two, gain_three, gain_four], axis=0)
+    small = jnp.concatenate([lines, gains.reshape(8, -1)], axis=0)
+    input_grad, small = edge(
+        "last", grad_first, [stream_zero, norm_gains[0:1], grad_one, small],
+        ways, rows, 4, 0, None, 9, "edge_seven",
+    )
+    lines = small[: CONV + 3 + STATE]
+    gains = small[-8:].reshape(norm_gains.shape)
+
+    late_grads = settle(late_swapped, late_group, 3)
+    focus_grads = settle(focus_swapped, focus_group, 4)
+    early_grads = settle(early_swapped, early_group, 3)
+    mixer_grads = settle(mixer_swapped, 0, 1)[0]
+    in_rows = mixer_in.shape[1]
+    return (
+        output,
+        input_grad,
+        gains,
+        mixer_grads[: 2 * in_rows].reshape(2, in_rows, -1),
+        mixer_grads[2 * in_rows :],
+        lines[:CONV].T,
+        lines[CONV],
+        lines[CONV + 1],
+        lines[CONV + 3 :].T,
+        lines[CONV + 2],
+        jnp.stack(early_grads[:2]),
+        early_grads[2],
+        jnp.stack(focus_grads[:3]),
+        focus_grads[3],
+        jnp.stack(late_grads[:2]),
+        late_grads[2],
+    )
+
+
 def solution(mesh):
+    counts = (mesh.shape["dp"], mesh.shape["tensor"])
+    chosen = partial(grouped_body, counts, 6, 0, 6) if counts == (8, 4) else body
     return jax.shard_map(
-        body,
+        chosen,
         mesh=mesh,
         in_specs=(
             P("dp", None),

time: 3670 us -> 890 us (0.24); the launches traced: 3610 us -> 881 us
  waiting for transfers between devices: 1580 us -> 69.2 us
  local copies, waits for them, and re-layouts: 1200 us -> 58.9 us
  Pallas kernels: 0 us -> 499 us
  other arithmetic: 425 us -> 64.7 us
  blocking collectives: 190 us -> 29 us
  matrix products: 183 us -> 83.6 us
  starting transfers between devices: 6.11 us -> 59.3 us
    pad x156 -> x2, local copies, waits for them, and re-layouts: 1060 us -> 0.03 us  [the longest x1 0.02 us: mixed_sum(): padded = jnp.pad(part, ((0, 0), (0, 256 - PROJ_OUT)))]
    reduce_scatter x7 -> x0, waiting for transfers between devices: 768 us -> none  [the longest x4 527 us: spread_grads(): lax.psum_scatter(joined, 'dp', scatter_dimension=0, tiled=True)]
    pallas_call x0 -> x14, Pallas kernels: none -> 499 us  [the longest x9 465 us: edge(): pl.pallas_call(partial(edge_kernel, kind, ways, rows, parts, in_group, ou...]
    all_gather x8 -> x1, waiting for transfers between devices: 422 us -> 7 us  [grouped_body(): output = lax.all_gather(output_rows, 'tensor', axis=0, tiled=True)]
    psum x9 -> x0, waiting for transfers between devices: 379 us -> none  [the longest x4 153 us: branch_total(): return lax.psum(piece_sum, 'tensor')]
    unnamed x1 -> x0, blocking collectives: 152 us -> none
    mul x65 -> x1, other arithmetic: 137 us -> 0.01 us  [grouped_body(): jnp.arange(2, dtype=jnp.int32)[:, None] * rows]
    add x56 -> x6, other arithmetic: 98.3 us -> 9.23 us  [the longest x2 6.73 us: settle(): sum((swapped[spot].astype(jnp.float32) for spot in range(count) if sub_of...]
  transfers between devices with their start and end apart: 25 -> 14, of which waited for: 23 -> 6; matrix products, arithmetic and copies ran while one was open for 9% -> 17% of each run, Pallas kernels for 0% -> 54%
where the time goes in v1:
time: 890 us; the launch traced here: 881 us
  Pallas kernels  499 us (56%)
  matrix products  83.6 us (9%)
  waiting for transfers between devices  69.2 us (8%)
  other arithmetic  64.7 us (7%)
  starting transfers between devices  59.3 us (7%)
  local copies, waits for them, and re-layouts  58.9 us (7%)
  blocking collectives  29 us (3%)
  between operations  16.6 us (2%)
    pallas_call x9, Pallas kernels, edge(): pl.pallas_call(partial(edge_kernel, kind, ways, rows, parts, in_group, ou...  465 us
    all_to_all x8, waiting for transfers between devices, swap(): return lax.all_to_all(stacked, 'dp', 0, 0, tiled=True)  54 us
    all_to_all x8, starting transfers between devices, swap(): return lax.all_to_all(stacked, 'dp', 0, 0, tiled=True)  48.8 us
    dot_general x10, matrix products, project(): return jnp.dot(left, right, preferred_element_type=jnp.float32)  31.4 us
    all_to_all x1, blocking collectives, whole_group(): lax.all_to_all(value, 'dp', 0, 0, tiled=True, axis_index_groups=same_core)  29 us
    dot_general x10, matrix products, project_t(): lax.dot_general(left, right, (((1,), (1,)), ((), ())), preferred_element_...  27.4 us
    unnamed x244, local copies, waits for them, and re-layouts  25.6 us
    dot_general x11, matrix products, outer_rows(): lax.dot_general(left, right, (((0,), (0,)), ((), ())), preferred_element_...  24.8 us
  transfers between devices with their start and end apart: 14, of which 6 were waited for; matrix products, arithmetic and copies ran while one was open for 17% of the time, Pallas kernels for 54%

profile of v1, /device:TPU:1, one launch (start us, length us, event | category | flops | bytes accessed | tf_op | source)
XLA Modules:
  0.0 880.5 jit_solution(1401695349733216042)
XLA Ops:
  15.5 5.4 all-to-all-start
  33.7 32.8 %all-to-all-done = bf16[8,256,1024]{2,1,0:T(8,128)(2,1)} async-done(((bf16[8,256,1024]{2,1,0:T(8,128)(2,1)}), bf16[8,256,1024]{2,1,0:T(8,128)(2,1)}, u32[]{:S(2)}, u32[]{:S(2)}) %all-to-all-start) | async-done | bytes 4194336 | tf_op jit(solution)/shard_map/all_to_all | solution.py:968
  66.5 7.8 all-to-all-start.1
  78.8 3.4 fusion.91
  82.3 18.6 %all-to-all-done.1 = bf16[8,292,512]{2,1,0:T(8,128)(2,1)} async-done(((bf16[8,292,512]{2,1,0:T(8,128)(2,1)}), bf16[8,292,512]{2,1,0:T(8,128)(2,1)}, u32[]{:S(2)}, u32[]{:S(2)}) %all-to-all-start.1) | async-done | bytes 2392096 | tf_op jit(solution)/shard_map/all_to_all | solution.py:968
  100.9 8.4 all-to-all-start.2
  119.4 4.2 reshape.282
  124.8 16.0 %mix_sum.1 = f32[256,256]{1,0:T(8,128)S(1)} custom-call(f32[256,256]{1,0:T(8,128)S(1)} %pad.39.refs_0_), custom_call_target="tpu_custom_call" | custom-call | flops 1 | bytes 1 | tf_op jit(solution)/shard_map/mix_sum/pallas_call | solution.py:830
  143.4 7.9 scan_forward.1
  152.3 63.5 %edge_one.1 = (bf16[1024,2048]{1,0:T(8,128)(2,1)S(1)}, f32[32,2048]{1,0:T(8,128)S(1)}) custom-call(bf16[256,2048]{1,0:T(8,128)(2,1)S(1)} %convolution_convert_fusion.10.refs_0_, f32[32,2048]{1,0:T(8,128)S(1)} %copy-done.7, f32[1,2048]{1,0:T(1,128)S(1)} %get-tuple-element.290.refs_2_), custom_call_target="tpu_custom_call" | custom-call | flops 1 | bytes 1 | tf_op jit(solution)/shard_map/edge_one/pallas_call | solution.py:830
  217.9 4.7 all-to-all-start.3
  222.5 5.2 fusion.15
  228.1 3.1 convolution_convert_fusion.3.refs_0_
  231.3 69.5 %edge_two.1 = (bf16[256,2048]{1,0:T(8,128)(2,1)S(1)}, f32[32,2048]{1,0:T(8,128)S(1)}) custom-call(bf16[1024,2048]{1,0:T(8,128)(2,1)S(1)} %convolution_convert_fusion.3.refs_0_, f32[32,2048]{1,0:T(8,128)S(1)} %get-tuple-element.57.refs_1_, f32[1,2048]{1,0:T(1,128)S(1)} %get-tuple-element.292.refs_2_), custom_call_target="tpu_custom_call" | custom-call | flops 1 | bytes 1 | tf_op jit(solution)/shard_map/edge_two/pallas_call | solution.py:830
  302.2 29.0 %all_to_all.55 = bf16[4,128,2048]{2,1,0:T(8,128)(2,1)} all-to-all(bf16[4,128,2048]{2,1,0:T(8,128)(2,1)S(1)} %broadcast_in_dim.24), channel_id=1, replica_groups={{0,8,16,24},{4,12,20,28},{1,9,17,25},{5,13,21,29},{2,10,18,26},{6,14,22..., dimensions={0} | all-to-all | bytes 4194304 | tf_op jit(solution)/shard_map/all_to_all | solution.py:1030
  338.4 44.2 %edge_three.1 = (bf16[1024,2048]{1,0:T(8,128)(2,1)S(1)}, f32[32,2048]{1,0:T(8,128)S(1)}) custom-call(bf16[256,2048]{1,0:T(8,128)(2,1)S(1)} %convolution_convert_fusion.14.refs_0_, f32[32,2048]{1,0:T(8,128)S(1)} %get-tuple-element.60.refs_1_, f32[1,2048]{1,0:T(1,128)S(1)} %copy-done.26), custom_call_target="tpu_custom_call" | custom-call | flops 1 | bytes 1 | tf_op jit(solution)/shard_map/edge_three/pallas_call | solution.py:830
  382.6 5.5 fusion.12
  391.6 4.7 fusion.22
  399.4 4.1 collective-permute-done.1
  405.1 4.9 all-to-all-start.4
  411.5 6.4 copy.72
  417.9 4.6 convolution_convert_fusion.15
  424.7 6.2 convolution_convert_fusion.9
  430.9 4.1 all-to-all-done.4
  437.9 4.2 all-to-all-start.5
  442.1 3.9 pad_maximum_fusion.5
  446.0 4.0 convolution_convert_fusion.1.refs_0_
  450.0 48.4 %edge_four.1 = (bf16[256,2048]{1,0:T(8,128)(2,1)S(1)}, f32[32,2048]{1,0:T(8,128)S(1)}, f32[1,2048]{1,0:T(1,128)S(1)}) custom-call(bf16[1024,2048]{1,0:T(8,128)(2,1)S(1)} %convolution_convert_fusion.1.refs_0_, f32[32,2048]{1,0:T(8,128)S(1)} %get-tuple-element.61.refs_1_, f32[1,2048]{1,0:T(1,128)S(1)} %copy-done.26, ...), custom_call_target="tpu_custom_call" | custom-call | flops 1 | bytes 1 | tf_op jit(solution)/shard_map/edge_four/pallas_call | solution.py:830
  502.6 4.4 all-to-all-start.7
  507.3 3.0 fusion.4.refs_0_
  510.3 58.2 %edge_five.1 = (bf16[1024,2048]{1,0:T(8,128)(2,1)S(1)}, f32[32,2048]{1,0:T(8,128)S(1)}, f32[1,2048]{1,0:T(1,128)S(1)}) custom-call(bf16[256,2048]{1,0:T(8,128)(2,1)S(1)} %fusion.4.refs_0_, f32[32,2048]{1,0:T(8,128)S(1)} %copy-done.15, f32[1,2048]{1,0:T(1,128)S(1)} %get-tuple-element.292.refs_2_, f32[32,2048]{1,0:T(8,128)S(1)} %copy-done.23), custom_call_target="tpu_custom_call" | custom-call | flops 1 | bytes 1 | tf_op jit(solution)/shard_map/edge_five/pallas_call | solution.py:830
  577.6 6.2 convolution_convert_fusion.refs_0_
  583.7 3.8 convolution_convert_fusion.5
  587.6 4.9 all-to-all-start.8
  592.5 3.7 convolution_convert_fusion.11
  598.1 7.0 all-gather.2.cloned.1.call-done
  607.3 74.3 %edge_six.1 = (bf16[256,2048]{1,0:T(8,128)(2,1)S(1)}, f32[32,2048]{1,0:T(8,128)S(1)}, f32[1,2048]{1,0:T(1,128)S(1)}) custom-call(bf16[1024,2048]{1,0:T(8,128)(2,1)S(1)} %copy-done.6, f32[32,2048]{1,0:T(8,128)S(1)} %get-tuple-element.57.refs_1_, f32[1,2048]{1,0:T(1,128)S(1)} %get-tuple-element.290.refs_2_, f32[32,2048]{1,0:T(8,128)S(1)} %copy-done.21), custom_call_target="tpu_custom_call" | custom-call | flops 1 | bytes 1 | tf_op jit(solution)/shard_map/edge_six/pallas_call | solution.py:830
  690.5 21.1 %scan_backward.1 = (f32[256,512]{1,0:T(8,128)}, bf16[256,512]{1,0:T(8,128)(2,1)}, bf16[256,512]{1,0:T(8,128)(2,1)}, f32[256,16,128]{2,1,0:T(8,128)}, f32[256,16,...) custom-call(f32[256]{0:T(256)} %copy-done.33, bf16[256,512]{1,0:T(8,128)(2,1)} %copy-done.2, ...), custom_call_target="tpu_custom_call" | custom-call | flops 1 | bytes 78643200 | tf_op jit(solution)/shard_map/scan_backward/pallas_call | solution.py:229
  718.6 4.6 all-to-all-start.9
  723.2 14.8 %mix_grad_sum.1 = f32[256,256]{1,0:T(8,128)S(1)} custom-call(f32[256,256]{1,0:T(8,128)S(1)} %select_maximum_fusion.refs_0_), custom_call_target="tpu_custom_call" | custom-call | flops 1 | bytes 1 | tf_op jit(solution)/shard_map/mix_grad_sum/pallas_call | solution.py:830
  738.2 3.2 pad_maximum_fusion.7
  741.5 4.1 convert_element_type.275
  751.7 3.2 pad_maximum_fusion
  757.5 8.7 all-to-all-start.10
  766.3 4.8 pad_maximum_fusion.4
  771.4 3.5 convolution_convert_fusion.12.refs_0_
  774.9 75.9 %edge_seven.1 = (f32[128,2048]{1,0:T(8,128)S(1)}, f32[32,1024]{1,0:T(8,128)S(1)}) custom-call(bf16[256,2048]{1,0:T(8,128)(2,1)S(1)} %convolution_convert_fusion.12.refs_0_, f32[32,2048]{1,0:T(8,128)S(1)} %copy-done.7, f32[1,2048]{1,0:T(1,128)S(1)} %copy-done.25, f32[32,2048]{1,0:T(8,128)S(1)} %get-tuple-element.81.refs_3_, ...), custom_call_target="tpu_custom_call" | custom-call | flops 1 | bytes 1 | tf_op jit(solution)/shard_map/edge_seven/pallas_call | solution.py:830
  864.9 3.8 add_bitcast_fusion
  (382 shorter events, 126.2 us)
Async XLA Ops:
  15.5 5.4 copy-start.76
  15.5 6.0 copy-start.71
  15.5 51.0 %all-to-all-start = ((bf16[8,256,1024]{2,1,0:T(8,128)(2,1)}), bf16[8,256,1024]{2,1,0:T(8,128)(2,1)}, u32[]{:S(2)}, u32[]{:S(2)}) async-start(bf16[8,256,1024]{2,1,0:T(8,128)(2,1)} %constant_dynamic-update-slice_fusion), calls=%async_computation | async-start | bytes 8388608 | tf_op jit(solution)/shard_map/all_to_all | solution.py:968
  33.7 40.6 %copy-start.68 = (bf16[256,1792]{1,0:T(8,128)(2,1)S(1)}, bf16[256,1792]{1,0:T(8,128)(2,1)}, u32[]{:S(2)}) copy-start(bf16[256,1792]{1,0:T(8,128)(2,1)} %copy-done.67) | copy-start | bytes 2752516
  66.5 34.5 %all-to-all-start.1 = ((bf16[8,292,512]{2,1,0:T(8,128)(2,1)}), bf16[8,292,512]{2,1,0:T(8,128)(2,1)}, u32[]{:S(2)}, u32[]{:S(2)}) async-start(bf16[8,292,512]{2,1,0:T(8,128)(2,1)} %copy-done.53), calls=%async_computation.1 | async-start | bytes 4849664 | tf_op jit(solution)/shard_map/all_to_all | solution.py:968
  82.2 34.8 %copy-start.41 = (f32[256,1024]{1,0:T(8,128)}, f32[256,1024]{1,0:T(8,128)S(1)}, u32[]{:S(2)}) copy-start(f32[256,1024]{1,0:T(8,128)S(1)} %fusion.91) | copy-start | bytes 3145732
  82.2 28.5 %copy-start.98 = (f32[1024]{0:T(1024)S(1)}, f32[1024]{0:T(1024)}, u32[]{:S(2)}) copy-start(f32[1024]{0:T(1024)} %param.23) | copy-start | bytes 12292
  82.3 28.6 %copy-start.99 = (f32[1024]{0:T(1024)S(1)}, f32[1024]{0:T(1024)}, u32[]{:S(2)}) copy-start(f32[1024]{0:T(1024)} %param.24) | copy-start | bytes 12292
  82.3 28.7 %copy-start.100 = (f32[1024]{0:T(1024)S(1)}, f32[1024]{0:T(1024)}, u32[]{:S(2)}) copy-start(f32[1024]{0:T(1024)} %param.26) | copy-start | bytes 12292
  82.3 28.7 %copy-start.94 = (f32[1024,4]{0,1:T(4,128)S(1)}, f32[1024,4]{0,1:T(4,128)}, u32[]{:S(2)}) copy-start(f32[1024,4]{0,1:T(4,128)} %param.22) | copy-start | bytes 49156
  82.3 28.8 %copy-start.87 = (f32[1024,16]{0,1:T(8,128)S(1)}, f32[1024,16]{0,1:T(8,128)}, u32[]{:S(2)}) copy-start(f32[1024,16]{0,1:T(8,128)} %param.25) | copy-start | bytes 196612
  100.9 116.9 %all-to-all-start.2 = ((bf16[8,256,1792]{2,1,0:T(8,128)(2,1)}), bf16[8,256,1792]{2,1,0:T(8,128)(2,1)}, u32[]{:S(2)}, u32[]{:S(2)}) async-start(bf16[8,256,1792]{2,1,0:T(8,128)(2,1)} %bitcast_dynamic-update-slice_fusion), calls=%async_computation.2 | async-start | bytes 14680064 | tf_op jit(solution)/shard_map/all_to_all | solution.py:968
  109.3 6.2 collective-permute-start
  110.9 32.3 %copy-start.27 = (f32[512]{0:T(512)}, f32[512]{0:T(512)S(1)}, u32[]{:S(2)}) copy-start(f32[512]{0:T(512)S(1)} %dynamic_slice.23) | copy-start | bytes 6148
  111.0 32.3 %copy-start.28 = (f32[512]{0:T(512)}, f32[512]{0:T(512)S(1)}, u32[]{:S(2)}) copy-start(f32[512]{0:T(512)S(1)} %dynamic_slice.25) | copy-start | bytes 6148
  111.1 5.9 copy-start.79
  111.1 5.9 copy-start.81
  111.1 5.9 copy-start.83
  111.2 5.9 copy-start.85
  111.2 32.1 %copy-start.19 = (f32[16,512]{1,0:T(8,128)}, f32[16,512]{1,0:T(8,128)S(1)}, u32[]{:S(2)}) copy-start(f32[16,512]{1,0:T(8,128)S(1)} %negate_bitcast_fusion.rate_ref) | copy-start | bytes 98308
  119.4 23.9 %copy-start.2 = (bf16[256,512]{1,0:T(8,128)(2,1)}, bf16[256,512]{1,0:T(8,128)(2,1)S(1)}, u32[]{:S(2)}) copy-start(bf16[256,512]{1,0:T(8,128)(2,1)S(1)} %get-tuple-element.100.chan_ref) | copy-start | bytes 786436
  124.7 18.6 %copy-start.33 = (f32[256]{0:T(256)}, f32[256]{0:T(256)S(1)}, u32[]{:S(2)}) copy-start(f32[256]{0:T(256)S(1)} %subtract_bitcast_fusion.keep_ref) | copy-start | bytes 3076
  142.7 8.6 copy-start
  143.3 7.9 copy-start.1
  143.4 7.9 copy-start.51
  217.9 82.9 %all-to-all-start.3 = ((bf16[8,256,768]{2,1,0:T(8,128)(2,1)}), bf16[8,256,768]{2,1,0:T(8,128)(2,1)}, u32[]{:S(2)}, u32[]{:S(2)}) async-start(bf16[8,256,768]{2,1,0:T(8,128)(2,1)} %copy-done.48), calls=%async_computation.3 | async-start | bytes 6291456 | tf_op jit(solution)/shard_map/all_to_all | solution.py:968
  300.8 37.6 %copy-start.14 = (f32[32,2048]{1,0:T(8,128)}, f32[32,2048]{1,0:T(8,128)S(1)}, u32[]{:S(2)}) copy-start(f32[32,2048]{1,0:T(8,128)S(1)} %get-tuple-element.60.refs_1_) | copy-start | bytes 786436
  331.2 57.0 %collective-permute-start.2 = (bf16[4,128,2048]{2,1,0:T(8,128)(2,1)}, bf16[4,128,2048]{2,1,0:T(8,128)(2,1)}, u32[]{:S(2)}, u32[]{:S(2)}) collective-permute-start(bf16[4,128,2048]{2,1,0:T(8,128)(2,1)} %all_to_all.55), channel_id=1, source_target_pairs={{0,4},{4,0},{8,12},{12,8},{16,20},{20,16},{24,28},{28,24},{1,5},{5... | collective-permute-start | bytes 6291464 | tf_op jit(solution)/shard_map/ppermute | solution.py:1023
  382.6 5.5 copy-start.36
  399.3 4.2 collective-permute-start.1
  405.1 29.9 %all-to-all-start.4 = ((bf16[4,128,2048]{2,1,0:T(8,128)(2,1)}), bf16[4,128,2048]{2,1,0:T(8,128)(2,1)}, u32[]{:S(2)}, u32[]{:S(2)}) async-start(bf16[4,128,2048]{2,1,0:T(8,128)(2,1)} %fusion.10), calls=%async_computation.4 | async-start | bytes 4194304 | tf_op jit(solution)/shard_map/all_to_all | solution.py:1043
  437.9 64.7 %all-to-all-start.5 = ((bf16[4,32,2048]{2,1,0:T(8,128)(2,1)}), bf16[4,32,2048]{2,1,0:T(8,128)(2,1)}, u32[]{:S(2)}, u32[]{:S(2)}) async-start(bf16[4,32,2048]{2,1,0:T(8,128)(2,1)} %bitcast.326), calls=%async_computation.5 | async-start | bytes 1048576 | tf_op jit(solution)/shard_map/all_to_all | solution.py:1151
  502.6 85.0 %all-to-all-start.7 = ((bf16[8,256,768]{2,1,0:T(8,128)(2,1)}), bf16[8,256,768]{2,1,0:T(8,128)(2,1)}, u32[]{:S(2)}, u32[]{:S(2)}) async-start(bf16[8,256,768]{2,1,0:T(8,128)(2,1)} %pad_maximum_fusion.5), calls=%async_computation.7 | async-start | bytes 6291456 | tf_op jit(solution)/shard_map/all_to_all | solution.py:968
  507.0 98.0 %all-gather.2.cloned.1.call-start = ((), (), s32[]{:S(2)}) async-start(), calls=%async_computation.11 | async-start | bytes 1310720 | tf_op jit(solution)/shard_map/all_gather | solution.py:1153
  507.3 61.3 %copy-start.13 = (bf16[256,2048]{1,0:T(8,128)(2,1)S(1)}, bf16[256,2048]{1,0:T(8,128)(2,1)}, u32[]{:S(2)}) copy-start(bf16[256,2048]{1,0:T(8,128)(2,1)} %copy-done.12) | copy-start | bytes 3145732
  577.6 6.2 copy-start.35
  587.5 4.9 copy-start.50
  587.6 103.0 %all-to-all-start.8 = ((bf16[8,256,1024]{2,1,0:T(8,128)(2,1)}), bf16[8,256,1024]{2,1,0:T(8,128)(2,1)}, u32[]{:S(2)}, u32[]{:S(2)}) async-start(bf16[8,256,1024]{2,1,0:T(8,128)(2,1)} %pad_maximum_fusion.2), calls=%async_computation.8 | async-start | bytes 8388608 | tf_op jit(solution)/shard_map/all_to_all | solution.py:968
  596.2 8.9 %copy-start.21 = (f32[32,2048]{1,0:T(8,128)S(1)}, f32[32,2048]{1,0:T(8,128)}, u32[]{:S(2)}) copy-start(f32[32,2048]{1,0:T(8,128)} %copy-done.20) | copy-start | bytes 786436
  684.9 5.5 copy-start.77
  690.5 21.2 %copy-start.9 = (f32[256,256]{1,0:T(8,128)S(1)}, f32[256,256]{1,0:T(8,128)}, u32[]{:S(2)}) copy-start(f32[256,256]{1,0:T(8,128)} %copy-done.8) | copy-start | bytes 786436
  718.6 19.4 %copy-start.3 = (bf16[256,512]{1,0:T(8,128)(2,1)S(1)}, bf16[256,512]{1,0:T(8,128)(2,1)}, u32[]{:S(2)}) copy-start(bf16[256,512]{1,0:T(8,128)(2,1)} %copy-done.2) | copy-start | bytes 786436
  718.6 38.9 %all-to-all-start.9 = ((bf16[8,256,768]{2,1,0:T(8,128)(2,1)}), bf16[8,256,768]{2,1,0:T(8,128)(2,1)}, u32[]{:S(2)}, u32[]{:S(2)}) async-start(bf16[8,256,768]{2,1,0:T(8,128)(2,1)} %pad_maximum_fusion.6), calls=%async_computation.9 | async-start | bytes 6291456 | tf_op jit(solution)/shard_map/all_to_all | solution.py:968
  757.5 107.4 %all-to-all-start.10 = ((bf16[8,804,512]{2,1,0:T(8,128)(2,1)}), bf16[8,804,512]{2,1,0:T(8,128)(2,1)}, u32[]{:S(2)}, u32[]{:S(2)}) async-start(bf16[8,804,512]{2,1,0:T(8,128)(2,1)} %pad_maximum_fusion), calls=%async_computation.10 | async-start | bytes 13238272 | tf_op jit(solution)/shard_map/all_to_all | solution.py:968
  766.2 4.9 copy-start.75
  766.2 4.9 copy-start.95
  766.2 4.9 copy-start.96
  766.3 5.1 copy-start.74
  (70 other events, 171.0 us)
Sparse Core Ops, SparseCore 0:
  577.7 27.3 all-gather.1

commit v2 on v1

--- a/solution.py
+++ b/solution.py
@@ -127,7 +127,7 @@
         out_shape=jax.ShapeDtypeStruct((tokens, channels), jnp.bfloat16),
         scratch_shapes=[pltpu.VMEM((tokens, width), jnp.float32)] * 3,
         compiler_params=pltpu.CompilerParams(vmem_limit_bytes=48 << 20),
-        cost_estimate=pl.CostEstimate(flops=1, bytes_accessed=28 << 20, transcendentals=0),
+        cost_estimate=pl.CostEstimate(flops=1, bytes_accessed=1 << 34, transcendentals=0),
         name="scan_forward",
     )(keep, channel, step_raw, gate_half, step_bias[None], rates_t, skip_gain[None], in_wide, out_wide)
 
@@ -239,7 +239,7 @@
         scratch_shapes=[pltpu.VMEM((tokens, width), jnp.float32)] * 6
         + [pltpu.VMEM((tokens, STATE, width), jnp.float32)] * 2,
         compiler_params=pltpu.CompilerParams(vmem_limit_bytes=56 << 20),
-        cost_estimate=pl.CostEstimate(flops=1, bytes_accessed=75 << 20, transcendentals=0),
+        cost_estimate=pl.CostEstimate(flops=1, bytes_accessed=1 << 34, transcendentals=0),
         name="scan_backward",
     )(keep, channel, step_raw, gate_half, dmixed, step_bias[None], rates_t, skip_gain[None], in_wide, out_wide)
 
@@ -537,8 +537,8 @@
         value = lax.rem(self.spot // axis, 2)
         return 1 - value if turned & axis else value
 
-    def across(self, turned):
-        move = 0
+    def across(self, turned, swapped=False):
+        move = 1 - 2 * self.core if swapped else 0
         for axis in (2, 4):
             if turned & axis:
                 move = move + axis * (1 - 2 * self.bit(axis, 0))
@@ -566,10 +566,12 @@
     return copy
 
 
-def greet(place, ways):
+def greet(place, ways, both=False):
     barrier = pltpu.get_barrier_semaphore()
     peers = [(place.partner, place.depth)]
     peers += [(place.across(turned), place.depth) for turned in ways]
+    if both:
+        peers += [(place.across(turned, True), place.depth) for turned in ways]
     peers += [(place.spot, place.along(offset)) for offset in range(1, place.ways)]
     for peer in peers:
         pl.semaphore_signal(barrier, inc=1, device_id=peer, device_id_type=MESH)
@@ -580,102 +582,188 @@
     return pl.ds(pl.multiple_of(start * unit, unit), size)
 
 
-def reduce_stage(place, group, rows, parts, part_ref, near_s, sum_s, far_s, deep_s, sems):
-    share = rows // place.ways
-    step = part_ref.shape[1] // parts
-    ways = turns(group) + [0]
-    sides = len(ways)
-    near = {}
-    for part in range(parts):
-        lanes = pl.ds(part * step, step)
-        for at, turned in enumerate(ways):
-            side = place.side(group, turned)
-            near[part, turned] = send(
-                part_ref.at[rows_at(side * 2 + 1 - place.core, rows, rows), lanes],
-                near_s.at[rows_at(side, rows, rows), lanes],
-                sems["near"], part * sides + at, place.partner, place.depth,
-            )
-
-    def joined(side, lanes):
-        own = part_ref[rows_at(side * 2 + place.core, rows, rows), lanes].astype(jnp.float32)
-        return own + near_s[rows_at(side, rows, rows), lanes].astype(jnp.float32)
-
-    far = {}
-    for part in range(parts):
-        lanes = pl.ds(part * step, step)
-        for at, turned in enumerate(ways[:-1]):
-            side = place.side(group, turned)
-            near[part, turned].wait_recv()
-            sum_s[rows_at(side, rows, rows), lanes] = joined(side, lanes).astype(sum_s.dtype)
-            far[part, turned] = send(
-                sum_s.at[rows_at(side, rows, rows), lanes], far_s.at[at, :, lanes],
-                sems["far"], part * (sides - 1) + at, place.across(turned), place.depth,
-            )
-    deep = []
-    mine = place.side(group)
-    for part in range(parts):
-        lanes = pl.ds(part * step, step)
-        near[part, 0].wait_recv()
-        total = joined(mine, lanes)
-        for at, turned in enumerate(ways[:-1]):
-            far[part, turned].wait_recv()
-            total = total + far_s[at, :, lanes].astype(jnp.float32)
-        sum_s[rows_at(mine, rows, rows), lanes] = total.astype(sum_s.dtype)
-        for offset in range(1, place.ways):
-            deep.append(
-                send(
-                    sum_s.at[pl.ds(pl.multiple_of(mine * rows + place.along(offset) * share, share), share), lanes],
-                    deep_s.at[offset - 1, :, lanes],
-                    sems["deep"], part * (place.ways - 1) + offset - 1, place.spot, place.along(offset),
+class Reduction:
+    def __init__(self, place, group, rows, parts, part_ref, near_s, sum_s, far_s, sems, names):
+        self.place, self.group, self.rows, self.parts = place, group, rows, parts
+        self.part_ref, self.near_s, self.sum_s, self.far_s = part_ref, near_s, sum_s, far_s
+        self.sems = [sems[name] for name in names]
+        self.ways = turns(group) + [0]
+        self.step = part_ref.shape[1] // parts
+        self.near, self.far = {}, {}
+
+    def lanes(self, part):
+        return pl.ds(part * self.step, self.step)
+
+    def block(self, side):
+        return rows_at(side, self.rows, self.rows)
+
+    def send_near(self):
+        place = self.place
+        for part in range(self.parts):
+            for at, turned in enumerate(self.ways):
+                side = place.side(self.group, turned)
+                self.near[part, turned] = send(
+                    self.part_ref.at[self.block(side * 2 + 1 - place.core), self.lanes(part)],
+                    self.near_s.at[self.block(side), self.lanes(part)],
+                    self.sems[0], part * len(self.ways) + at, place.partner, place.depth,
                 )
-            )
-    for copy in deep:
+
+    def joined(self, part, turned):
+        self.near[part, turned].wait_recv()
+        side, lanes = self.place.side(self.group, turned), self.lanes(part)
+        own = self.part_ref[self.block(side * 2 + self.place.core), lanes].astype(jnp.float32)
+        return own + self.near_s[self.block(side), lanes].astype(jnp.float32)
+
+    def order(self):
+        half = self.parts // 2
+        return [at + first for at in range(half) for first in (0, half)]
+
+    def leg(self, part):
+        return (2, 4) if part < self.parts // 2 else (4, 2)
+
+    def push(self, part, turned, slot, to, value):
+        rows, lanes = self.block(self.place.side(self.group, turned)), self.lanes(part)
+        self.sum_s[rows, lanes] = value.astype(self.sum_s.dtype)
+        self.far[part, slot] = send(
+            self.sum_s.at[rows, lanes], self.far_s.at[slot, :, lanes],
+            self.sems[1], part * 3 + slot, self.place.across(to), self.place.depth,
+        )
+
+    def came(self, part, slot):
+        self.far[part, slot].wait_recv()
+        return self.far_s[slot, :, self.lanes(part)].astype(jnp.float32)
+
+    def send_far(self):
+        if self.group:
+            for part in self.order():
+                first, _ = self.leg(part)
+                self.push(part, 6, 1, first, self.joined(part, 6))
+                self.push(part, first, 0, first, self.joined(part, first))
+
+    def relay(self):
+        if self.group:
+            for part in self.order():
+                _, second = self.leg(part)
+                value = self.joined(part, second) + self.came(part, 1)
+                self.push(part, second, 2, second, value)
+
+    def chip_sum(self, part):
+        total = self.joined(part, 0)
+        if self.group:
+            total = total + self.came(part, 0) + self.came(part, 2)
+        return total
+
+    def sent(self):
+        return list(self.near.values()) + list(self.far.values())
+
+
+def deep_sends(place, share, source, start, deep_s, lanes, sems, at):
+    return [
+        send(
+            source.at[pl.ds(pl.multiple_of(start + place.along(offset) * share, share), share), lanes],
+            deep_s.at[offset - 1, :, lanes],
+            sems, at + offset - 1, place.spot, place.along(offset),
+        )
+        for offset in range(1, place.ways)
+    ]
+
+
+def deep_total(place, share, source, start, deep_s, copies):
+    for copy in copies:
         copy.wait_recv()
-    total = sum_s[pl.ds(pl.multiple_of(mine * rows + place.depth * share, share), share), :].astype(jnp.float32)
+    total = source[pl.ds(pl.multiple_of(start + place.depth * share, share), share), :].astype(jnp.float32)
     for offset in range(1, place.ways):
         total = total + deep_s[offset - 1].astype(jnp.float32)
-    return total, list(near.values()) + list(far.values()) + deep
-
-
-def gather_stage(place, group, rows, all_ref, sems):
+    return total
+
+
+def reduce_stage(first, deep_s, sems, between):
+    place, rows = first.place, first.rows
     share = rows // place.ways
-    ways = turns(group)
-    mine = place.side(group)
-
-    def piece(side, depth):
-        return all_ref.at[pl.ds(pl.multiple_of((side * 2 + place.core) * rows + depth * share, share), share), :]
-
-    own = piece(mine, place.depth)
+    first.send_near()
+    between(0)
+    first.send_far()
+    first.relay()
+    between(1)
+    deep = []
+    mine = place.side(first.group)
+    for part in first.order() if first.group else range(first.parts):
+        first.sum_s[first.block(mine), first.lanes(part)] = first.chip_sum(part).astype(first.sum_s.dtype)
+        deep += deep_sends(
+            place, share, first.sum_s, mine * rows, deep_s, first.lanes(part), sems["deep"], part * (place.ways - 1)
+        )
+    return deep_total(place, share, first.sum_s, mine * rows, deep_s, deep), first.sent() + deep
+
+
+def hand_on(place, group, rows_of, target, sems, base, far):
+    half = target.shape[1] // 2
+    for came, to, lanes in ((2, 4, pl.ds(0, half)), (4, 2, pl.ds(half, half))):
+        far[came].wait_recv()
+        block = target.at[rows_of(came), lanes]
+        far[came, to] = send(block, block, sems, base + to // 2 + 1, place.across(to), place.depth)
+
+
+def first_leg(place, block, sems, base):
+    return {turned: send(block, block, sems, base + turned // 2 - 1, place.across(turned), place.depth) for turned in (2, 4)}
+
+
+def gather_stage(place, group, rows, all_ref, sems, between):
+    share = rows // place.ways
+
+    def place_of(turned, offset):
+        depth = place.along(place.ways - offset) if offset else place.depth
+        return pl.ds(pl.multiple_of((place.side(group, turned) * 2 + place.core) * rows + depth * share, share), share)
+
+    def to_partner(turned, offset, at):
+        block = all_ref.at[place_of(turned, offset), :]
+        return send(block, block, sems["near_back"], at * place.ways + offset, place.partner, place.depth)
+
+    own = all_ref.at[place_of(0, 0), :]
     deep = [
         send(own, own, sems["deep_back"], offset - 1, place.spot, place.along(offset)) for offset in range(1, place.ways)
     ]
-    far, near = {}, []
+    far, near = [], []
     for offset in range(place.ways):
         if offset:
             deep[offset - 1].wait_recv()
-        came = piece(mine, place.along(place.ways - offset) if offset else place.depth)
-        for at, turned in enumerate(ways):
-            far[offset, turned] = send(
-                came, came, sems["far_back"], offset * len(ways) + at, place.across(turned), place.depth
+        if group:
+            far.append(first_leg(place, all_ref.at[place_of(0, offset), :], sems["far_back"], 4 * offset))
+        near.append(to_partner(0, offset, 0))
+        if offset == 0:
+            between()
+    if group:
+        for offset in range(place.ways):
+            hand_on(
+                place, group, lambda turned: place_of(turned, offset), all_ref, sems["far_back"], 4 * offset, far[offset]
             )
-        near.append(send(came, came, sems["near_back"], offset, place.partner, place.depth))
-    for offset in range(place.ways):
-        for at, turned in enumerate(ways):
-            far[offset, turned].wait_recv()
-            came = piece(place.side(group, turned), place.along(place.ways - offset) if offset else place.depth)
-            near.append(
-                send(came, came, sems["near_back"], (1 + at) * place.ways + offset, place.partner, place.depth)
-            )
+            near.append(to_partner(2, offset, 1))
+            near.append(to_partner(4, offset, 2))
+        for offset in range(place.ways):
+            far[offset][2, 4].wait_recv()
+            far[offset][4, 2].wait_recv()
+            near.append(to_partner(6, offset, 3))
     for copy in near:
         copy.wait_recv()
-    return deep + list(far.values()) + near
-
-
-def spread_stage(place, rows, all_ref, sems):
+    return deep + [copy for one in far for copy in one.values()] + near
+
+
+def exchange_start(place, source_ref, target_ref, sems):
+    copies = [
+        send(source_ref.at[spot], target_ref.at[place.spot], sems, at, spot, place.depth)
+        for at, spot in enumerate(
+            [place.across(turned, swapped) for turned in (6, 2, 4) for swapped in (False, True)] + [place.partner]
+        )
+    ]
+    own = pltpu.make_async_copy(source_ref.at[place.spot], target_ref.at[place.spot], sems[1].at[7])
+    own.start()
+    return copies, own
+
+
+def spread_stage(place, rows, all_ref, sems, name="deep_back"):
     share = rows // place.ways
     own = all_ref.at[pl.ds(pl.multiple_of(place.depth * share, share), share), :]
     deep = [
-        send(own, own, sems["deep_back"], offset - 1, place.spot, place.along(offset)) for offset in range(1, place.ways)
+        send(own, own, sems[name], offset - 1, place.spot, place.along(offset)) for offset in range(1, place.ways)
     ]
     return deep
 
@@ -732,36 +820,86 @@
     return {name: (refs[2 * at], refs[2 * at + 1]) for at, name in enumerate(names)}
 
 
-def edge_kernel(kind, ways, rows, parts, in_group, out_group, names, *refs):
+def edge_kernel(kind, extra, carrying, ways, rows, parts, in_group, out_group, names, counts, *refs):
     place = Place(ways)
     share = rows // ways
-    refs = list(refs)
-    part_ref = refs.pop(0)
+    ins, outs = list(refs[: counts[0]]), list(refs[counts[0] : counts[0] + counts[1]])
+    scratch = list(refs[counts[0] + counts[1] : counts[0] + counts[1] + counts[2]])
+    sems = sem_dict(names, refs[sum(counts) :])
+    part_ref = ins.pop(0)
+    near_s, sum_s, far_s, deep_s = [scratch.pop(0) for _ in range(4)]
     if kind == "forward":
-        stream_ref, gain_ref = refs.pop(0), refs.pop(0)
-        all_ref, fresh_ref = refs.pop(0), refs.pop(0)
-    elif kind in ("backward", "last"):
-        stream_ref, gain_ref, grad_ref = refs.pop(0), refs.pop(0), refs.pop(0)
-        small_ref = refs.pop(0) if kind == "last" else None
-        all_ref = refs.pop(0)
-        fresh_ref = refs.pop(0) if kind == "backward" else None
-        dgain_ref = refs.pop(0)
+        stream_ref, gain_ref = ins.pop(0), ins.pop(0)
+    elif kind != "sum":
+        stream_ref, gain_ref, grad_ref = ins.pop(0), ins.pop(0), ins.pop(0)
+    all_ref = outs.pop(0)
+    if kind != "sum" and kind != "last":
+        fresh_ref = outs.pop(0)
+    if kind == "backward":
+        dgain_ref = outs.pop(0)
+    if kind == "last":
+        small_ref, late_ref, three_ref = ins.pop(0), ins.pop(0), ins.pop(0)
+        dgain_ref, late_out_ref = outs.pop(0), outs.pop(0)
+        low_s, small_s, late_s, late_low_s = [scratch.pop(0) for _ in range(4)]
+    if carrying:
+        source_ref, target_ref = ins.pop(), outs.pop()
+    everyone = carrying or kind == "last"
+    greet(place, turns(6) if everyone else sorted({*turns(in_group), *turns(out_group)}), carrying)
+    first = Reduction(place, in_group, rows, parts, part_ref, near_s, sum_s, far_s, sems, ("near", "far"))
+    waiting = []
+    freight = {}
+    if extra == "gather":
+        load_ref, load_out_ref = ins.pop(0), outs.pop(0)
+
+        def load_rows(turned):
+            return rows_at(place.side(in_group, turned) * 2 + place.core, rows, rows)
+
+        def between(stage):
+            spot = rows_at(place.side(in_group) * 2 + place.core, rows, rows)
+            if stage == 0:
+                load_out_ref[spot, :] = load_ref[...]
+                return
+            own = load_out_ref.at[spot, :]
+            if stage == 1:
+                freight.update(first_leg(place, own, sems["load_far"], 0))
+                freight[0] = send(own, own, sems["load_near"], 0, place.partner, place.depth)
+            else:
+                hand_on(place, in_group, load_rows, load_out_ref, sems["load_far"], 0, freight)
+
+    elif extra == "reduce":
+        second = Reduction(
+            place, in_group, rows, parts, ins.pop(0), *[scratch.pop(0) for _ in range(3)], sems, ("load_near", "load_far")
+        )
+        load_out_ref = outs.pop(0)
+
+        def between(stage):
+            (second.send_near, second.send_far, second.relay)[stage]()
+
     else:
-        all_ref = refs.pop(0)
-    near_s, sum_s, far_s, deep_s = refs.pop(0), refs.pop(0), refs.pop(0), refs.pop(0)
+
+        def between(stage):
+            pass
+
+    carried = []
+
+    def on_the_way(stage):
+        between(stage)
+        if carrying and stage == (1 if in_group else 0):
+            carried.append(exchange_start(place, source_ref, target_ref, sems["exchange"]))
+
     if kind == "last":
-        low_s, small_s = refs.pop(0), refs.pop(0)
-    sems = sem_dict(names, refs)
-    greet(place, turns(6) if kind == "last" else sorted({*turns(in_group), *turns(out_group)}))
-    total, waiting = reduce_stage(
-        place, in_group, rows, parts, part_ref, near_s, sum_s, far_s, deep_s, sems
-    )
+        late = deep_sends(place, share, late_ref, 0, late_s, slice(None), sems["late"], 0)
+        waiting += late
+    total, copies = reduce_stage(first, deep_s, sems, on_the_way)
+    waiting += copies
     if kind == "forward":
         fresh = stream_ref[...] + total
         fresh_ref[...] = fresh
         scale = lax.rsqrt(jnp.mean(fresh * fresh, axis=-1, keepdims=True) + EPS)
         value = fresh * scale * gain_ref[...]
-    elif kind in ("backward", "last"):
+    elif kind == "sum":
+        value = total
+    else:
         stream = stream_ref[...]
         scale = lax.rsqrt(jnp.mean(stream * stream, axis=-1, keepdims=True) + EPS)
         leaned = total * gain_ref[...]
@@ -771,28 +909,50 @@
         if kind == "backward":
             dgain_ref[...] = dgain
             fresh_ref[...] = value
-    else:
-        value = total
     if kind == "last":
-        low_s[pl.ds(pl.multiple_of(place.depth * share, share), share), :] = value.astype(low_s.dtype)
+        own = pl.ds(pl.multiple_of(place.depth * share, share), share)
+        low_s[own, :] = value.astype(low_s.dtype)
+        spread = spread_stage(place, rows, low_s, sems)
+        late_total = three_ref[...] + deep_total(place, share, late_ref, 0, late_s, late)
+        late_low_s[own, :] = late_total.astype(late_low_s.dtype)
+        spread += spread_stage(place, rows, late_low_s, sems, "late_back")
         half, span = small_ref.shape[0] // 2, small_ref.shape[1]
         dgain_ref[...] = small_ref[...]
         for at in range(dgain.shape[1] // span):
             dgain_ref[pl.ds(2 * half - 8 + at, 1), :] = dgain[:, at * span : (at + 1) * span]
-        spread = spread_stage(place, rows, low_s, sems)
         waiting += spread + small_stage(place, half, dgain_ref, small_s, sems)
         for copy in spread:
             copy.wait_recv()
         all_ref[...] = low_s[...].astype(jnp.float32)
+        late_out_ref[...] = late_low_s[...].astype(jnp.float32)
     else:
         spot = pl.multiple_of((place.side(out_group) * 2 + place.core) * rows + place.depth * share, share)
         all_ref[pl.ds(spot, share), :] = value.astype(all_ref.dtype)
-        waiting += gather_stage(place, out_group, rows, all_ref, sems)
+        waiting += gather_stage(place, out_group, rows, all_ref, sems, partial(on_the_way, 2))
+    if extra == "gather":
+        last = []
+        for at, turned in enumerate((2, 4, 6)):
+            for key in ((2, 4), (4, 2)) if turned == 6 else ():
+                freight[key].wait_recv()
+            came = load_out_ref.at[load_rows(turned), :]
+            last.append(send(came, came, sems["load_near"], 1 + at, place.partner, place.depth))
+        for copy in last + [freight[0]]:
+            copy.wait_recv()
+        waiting += list(freight.values()) + last
+    elif extra == "reduce":
+        for part in range(parts):
+            load_out_ref[:, second.lanes(part)] = second.chip_sum(part).astype(load_out_ref.dtype)
+        waiting += second.sent()
+    for copies, own in carried:
+        for copy in copies:
+            copy.wait_recv()
+        own.wait()
+        waiting += copies
     for copy in waiting:
         copy.wait_send()
 
 
-def edge(kind, part, extras, ways, rows, parts, in_group, out_group, ident, name):
+def edge(kind, part, extras, ways, rows, parts, in_group, out_group, ident, name, extra=None, carried=None):
     width = part.shape[1]
     share = rows // ways
     in_far, out_far = len(turns(in_group)), len(turns(out_group or 0))
@@ -801,40 +961,56 @@
     line = jax.ShapeDtypeStruct((1, width), jnp.float32)
     strip = jax.ShapeDtypeStruct((share, width), jnp.float32)
     whole = jax.ShapeDtypeStruct((out_sides * 2 * rows, width), dtype)
+    block = jax.ShapeDtypeStruct((rows, width), jnp.float32)
     outs = {
         "forward": [whole, strip],
         "backward": [whole, strip, line],
-        "last": [jax.ShapeDtypeStruct((rows, width), jnp.float32)]
-        + [jax.ShapeDtypeStruct(extra.shape, extra.dtype) for extra in extras[3:]],
+        "last": [block] + [jax.ShapeDtypeStruct(one.shape, one.dtype) for one in extras[3:4]] + [block],
         "sum": [whole],
     }[kind]
-    names = {"near": parts * in_sides, "far": parts * in_far, "deep": parts * (ways - 1), "deep_back": ways - 1}
-    if kind == "last":
-        names["small"] = 5 + ways
-    else:
-        names.update({"far_back": ways * out_far, "near_back": ways * out_sides})
-    if not in_group:
-        del names["far"]
-    if kind != "last" and not out_group:
-        del names["far_back"]
-    scratch = [
+    names = {"near": parts * in_sides, "far": 3 * parts if in_far else 0, "deep": parts * (ways - 1), "deep_back": ways - 1}
+    reducing = [
         pltpu.VMEM((in_sides * rows, width), dtype),
         pltpu.VMEM((in_sides * rows, width), dtype),
         pltpu.VMEM((max(in_far, 1), rows if in_far else 16, width), dtype),
-        pltpu.VMEM((ways - 1, share, width), dtype),
     ]
+    deep = pltpu.VMEM((ways - 1, share, width), dtype)
+    scratch = reducing + [deep]
     if kind == "last":
-        scratch.append(pltpu.VMEM((rows, width), dtype))
-        scratch.append(pltpu.VMEM((8 + ways, extras[3].shape[0] // 2, extras[3].shape[1]), jnp.float32))
-    vmem = pl.BlockSpec(memory_space=pltpu.VMEM)
+        names.update({"small": 5 + ways, "late": ways - 1, "late_back": ways - 1})
+        small = pltpu.VMEM((8 + ways, extras[3].shape[0] // 2, extras[3].shape[1]), jnp.float32)
+        spread = pltpu.VMEM((rows, width), dtype)
+        scratch += [spread, small, deep, spread]
+    else:
+        names.update({"far_back": 4 * ways if out_far else 0, "near_back": ways * out_sides})
+    if extra == "gather":
+        names.update({"load_far": 4, "load_near": in_sides})
+        outs = outs + [jax.ShapeDtypeStruct((in_sides * 2 * rows, width), dtype)]
+    elif extra == "reduce":
+        names.update({"load_far": 3 * parts, "load_near": parts * in_sides})
+        outs = outs + [jax.ShapeDtypeStruct((rows, width), dtype)]
+        scratch = scratch + reducing
+    vmem, whole_memory = pl.BlockSpec(memory_space=pltpu.VMEM), pl.BlockSpec(memory_space=pl.ANY)
+    in_specs, out_specs = [vmem] * (1 + len(extras)), [vmem] * len(outs)
+    if carried is not None:
+        names["exchange"] = 8
+        extras = list(extras) + [carried]
+        outs = outs + [jax.ShapeDtypeStruct(carried.shape, carried.dtype)]
+        in_specs, out_specs = in_specs + [whole_memory], out_specs + [whole_memory]
+    names = {key: count for key, count in names.items() if count}
+    if not in_far:
+        names["far"] = 1
     return pl.pallas_call(
-        partial(edge_kernel, kind, ways, rows, parts, in_group, out_group, names),
-        in_specs=[vmem] * (1 + len(extras)),
-        out_specs=[vmem] * len(outs),
+        partial(
+            edge_kernel, kind, extra, carried is not None, ways, rows, parts, in_group, out_group, names,
+            (1 + len(extras), len(outs), len(scratch)),
+        ),
+        in_specs=in_specs,
+        out_specs=out_specs,
         out_shape=outs,
         scratch_shapes=scratch + sem_shapes(names),
         compiler_params=pltpu.CompilerParams(
-            collective_id=ident, has_side_effects=True, vmem_limit_bytes=40 << 20
+            collective_id=ident, has_side_effects=True, vmem_limit_bytes=48 << 20
         ),
         cost_estimate=pl.CostEstimate(flops=1, bytes_accessed=1, transcendentals=0),
         name=name,
@@ -978,10 +1154,6 @@
     return [
         jnp.concatenate([one[:, block * size : (block + 1) * size] for one in sums], axis=1) for block in range(blocks)
     ]
-
-
-def by_half(place, first, second):
-    return [jnp.where(place == 0, first, second), jnp.where(place == 0, second, first)]
 
 
 def after(value, *others):
@@ -1022,31 +1194,6 @@
     def swapped_core(value):
         return lax.ppermute(value, "dp", [(at, at ^ 1) for at in range(spots)])
 
-    same_core = [[2 * chip + at for chip in range(spots // 2)] for at in range(2)]
-
-    def whole_group(value, group):
-        if group == 6:
-            value = jnp.broadcast_to(value[None], (spots // 2,) + value.shape)
-            value = lax.all_to_all(value, "dp", 0, 0, tiled=True, axis_index_groups=same_core)
-        else:
-            value = value[None]
-        if group in (2, 4):
-            moved = lax.ppermute(value, "dp", [(at, at ^ group) for at in range(spots)])
-            value = jnp.concatenate(by_half((spot // group) % 2, value, moved))
-        return jnp.stack(by_half(core, value, swapped_core(value)), axis=1).reshape(-1, value.shape[-1])
-
-    def group_sum(part, group):
-        part = part.reshape(-1, 2, rows, width)
-        mine, other = by_half(core, part[:, 0], part[:, 1])
-        part = mine + swapped_core(other)
-        if group == 6:
-            part = lax.all_to_all(part, "dp", 0, 0, tiled=True, axis_index_groups=same_core)
-            return jnp.sum(part.astype(jnp.float32), axis=0).astype(low)
-        if group:
-            mine, other = by_half((spot // group) % 2, part[0], part[1])
-            return mine + lax.ppermute(other, "dp", [(at, at ^ group) for at in range(spots)])
-        return part[0]
-
     in_weights = swap(pull(spots, ([mixer_in[0], mixer_in[1]], 0)))
 
     other_lengths = swapped_core(seq_lengths)
@@ -1076,20 +1223,17 @@
     row_mat = row_weights.reshape(-1, channels)
     early_blocks = [early_gate_up[0], early_gate_up[1], early_down]
     focus_blocks = [attention_in[0], attention_in[1], attention_in[2], attention_out]
-    middle_weights = swap(
-        after(pull(spots, (early_blocks, early_group), (focus_blocks, focus_group)), row_weights, both)
-    ).reshape(width, -1)
-    units = 3 * early_down.shape[1] // subs_of(early_group)
-    early_mat, focus_mat = middle_weights[:, :units], middle_weights[:, units:]
+    early_weights = swap(after(pull(spots, (early_blocks, early_group)), row_weights, both))
     out_mat = row_mat[:width]
     select_mat = row_mat[width : width + PROJ_OUT]
     step_mat = row_mat[width + PROJ_OUT :]
 
-    def mixed_sum(part, ident, name):
+    def mixed_sum(part, ident, name, carried=None):
         padded = jnp.pad(part, ((0, 0), (0, 256 - PROJ_OUT)))
-        return edge("sum", padded, [], ways, rows, 1, 0, 0, ident, name)[0][:, :PROJ_OUT]
-
-    mix_rows = mixed_sum(project_t(channel_low, select_mat), 1, "mix_sum")
+        total, *came = edge("sum", padded, [], ways, rows, 1, 0, 0, ident, name, carried=carried)
+        return total[:, :PROJ_OUT], *came
+
+    mix_rows, = mixed_sum(project_t(channel_low, select_mat), 1, "mix_sum")
     rank_low = mix_rows[:, :DT_RANK].astype(low)
     step_raw = project(rank_low, step_mat)
     rates_t = -jnp.exp(decay).T
@@ -1099,13 +1243,12 @@
     mixer_low = scan_forward(
         keeping, channel_low, step_raw, gate_half, bias, rates_t, skip, in_wide, out_wide, groups, LANES
     )
+    focus_weights = swap(after(pull(spots, (focus_blocks, focus_group)), early_weights, mixer_low))
+    early_mat, focus_mat = [one.reshape(width, -1) for one in (early_weights, focus_weights)]
     second_low, stream_one = edge(
         "forward", project_t(mixer_low, out_mat).astype(low), [stream_zero, norm_gains[1:2]],
         ways, rows, 4, 0, early_group, 2, "edge_one",
     )
-
-    late_blocks = [late_gate_up[0], late_gate_up[1], late_down]
-    late_weights = swap(after(pull(spots, (late_blocks, late_group)), middle_weights, second_low))
 
     def ffn(normed, mat):
         units = mat.shape[1] // 3
@@ -1114,11 +1257,13 @@
         return project_t(hidden, mat[:, 2 * units :]).astype(low), both, hidden
 
     early_part, early_both, early_hidden = ffn(second_low, early_mat)
-    third_low, stream_two = edge(
-        "forward", early_part, [stream_one, norm_gains[2:3]], ways, rows, 4, early_group, 0, 3, "edge_two"
-    )
-
-    last_grad = whole_group(after(output_grad, late_weights, third_low), late_group)
+    third_low, stream_two, last_grad = edge(
+        "forward", early_part, [stream_one, norm_gains[2:3], output_grad], ways, rows, 4, early_group, 0, 3, "edge_two",
+        "gather",
+    )
+
+    late_blocks = [late_gate_up[0], late_gate_up[1], late_down]
+    late_weights = swap(after(pull(spots, (late_blocks, late_group)), focus_weights, third_low))
     heads_width = focus_mat.shape[1] // 4
     down, side = flat_segs[:, None], flat_segs.reshape(2, rows)
     joint_low, attended_low = attend(project(third_low, focus_mat[:, : 3 * heads_width]), down, side, rows)
@@ -1141,37 +1286,30 @@
 
     grad_fourth, late_joint = ffn_back(last_grad, fourth_low, late_both, late_hidden, late_mat)
     grad_zero = lax.dynamic_slice_in_dim(output_grad, depth * share, share, 0).astype(jnp.float32)
-    output_part = group_sum(late_part, late_group)
-    grad_low_three, grad_three, gain_four = edge(
-        "backward", after(grad_fourth, output_part), [stream_three, norm_gains[3:4], grad_zero],
-        ways, rows, 4, late_group, 0, 5, "edge_four",
-    )
-    late_swapped = swap(after(late_joint, grad_low_three))
-
-    output_rows = lax.all_to_all(output_part.reshape(ways, share, width), "tensor", 0, 0, tiled=True)
-    output_rows = stream_three + jnp.sum(output_rows.astype(jnp.float32), axis=0)
-    output = lax.all_gather(output_rows, "tensor", axis=0, tiled=True)
+    grad_low_three, grad_three, gain_four, output_part = edge(
+        "backward", grad_fourth, [stream_three, norm_gains[3:4], grad_zero, late_part],
+        ways, rows, 4, late_group, 0, 5, "edge_four", "reduce",
+    )
 
     grad_attended = project(grad_low_three, focus_mat[:, 3 * heads_width :])
     joint_grad = attend_back(joint_low, grad_attended, down, side, rows)
-    grad_low_two, grad_two, gain_three = edge(
+    grad_low_two, grad_two, gain_three, late_swapped = edge(
         "backward", project_t(joint_grad, focus_mat[:, : 3 * heads_width]).astype(low),
-        [stream_two, norm_gains[2:3], grad_three], ways, rows, 4, 0, early_group, 6, "edge_five",
+        [stream_two, norm_gains[2:3], grad_three], ways, rows, 4, 0, early_group, 6, "edge_five", carried=late_joint,
     )
     focus_joint = jnp.concatenate(
         [outer_rows(third_low, joint_grad), outer_rows(grad_low_three, attended_low)], axis=1
     ).astype(low)
-    focus_swapped = swap(after(focus_joint.reshape(spots, -1, 4 * heads_width), late_swapped, grad_low_two))
+    focus_joint = focus_joint.reshape(spots, -1, 4 * heads_width)
 
     grad_second, early_joint = ffn_back(grad_low_two, second_low, early_both, early_hidden, early_mat)
-    grad_low_one, grad_one, gain_two = edge(
-        "backward", after(grad_second, late_swapped), [stream_one, norm_gains[1:2], grad_two],
-        ways, rows, 4, early_group, 0, 7, "edge_six",
-    )
-
-    early_swapped = swap(after(early_joint, focus_swapped, grad_low_one))
-
-    grad_scanned = after(project(grad_low_one, out_mat), focus_swapped)
+    grad_low_one, grad_one, gain_two, focus_swapped = edge(
+        "backward", grad_second, [stream_one, norm_gains[1:2], grad_two],
+        ways, rows, 4, early_group, 0, 7, "edge_six", carried=focus_joint,
+    )
+    early_swapped = swap(after(early_joint, grad_low_one))
+
+    grad_scanned = project(grad_low_one, out_mat)
     (
         grad_channel,
         grad_step_low,
@@ -1185,9 +1323,14 @@
         keeping, channel_low, step_raw, gate_half, grad_scanned, bias, rates_t, skip, in_wide, out_wide,
         groups, LANES,
     )
+    grad_channel, grad_step_low, in_sums, out_sums, early_swapped = lax.optimization_barrier(
+        (grad_channel, grad_step_low, in_sums, out_sums, early_swapped)
+    )
     grad_rank = project_t(grad_step_low, step_mat)
-    grad_rows = mixed_sum(
-        jnp.concatenate([grad_rank, jnp.sum(in_sums, axis=-1), jnp.sum(out_sums, axis=-1)], axis=1), 8, "mix_grad_sum"
+    gate_joint = outer_rows(first_low, gate_low).astype(low).reshape(spots, -1, channels)
+    grad_rows, gate_swapped = mixed_sum(
+        jnp.concatenate([grad_rank, jnp.sum(in_sums, axis=-1), jnp.sum(out_sums, axis=-1)], axis=1), 8, "mix_grad_sum",
+        gate_joint,
     )
     grad_rows_low = grad_rows.astype(low)
     rows_joint = jnp.concatenate(
@@ -1201,37 +1344,35 @@
     grad_channel = grad_channel + project(grad_rows_low, select_mat)
     grad_conv_in, taps_grad, offset_grad = conv_back(grad_channel)
     conv_low = grad_conv_in.astype(low)
+    conv_joint = outer_rows(first_low, conv_low).astype(low).reshape(spots, -1, channels)
     in_grad = jnp.concatenate([conv_low, gate_low], axis=1)
     grad_first = project_t(in_grad, in_mat).astype(low)
-    in_joints = [outer_rows(first_low, grad).astype(low) for grad in (conv_low, gate_low)]
-    mixer_joint = jnp.concatenate(
-        [joint.reshape(spots, -1, channels) for joint in (in_joints[0], in_joints[1], rows_joint)], axis=1
-    )
-    mixer_swapped = swap(after(mixer_joint, early_swapped))
+    mixer_joint = jnp.concatenate([conv_joint, rows_joint.reshape(spots, -1, channels)], axis=1)
+    mixer_joint = jnp.pad(mixer_joint, ((0, 0), (0, -mixer_joint.shape[1] % 16), (0, 0)))
     lines = jnp.concatenate([taps_grad.T, offset_grad[None], bias_grad, skip_grad, decay_grad], axis=0)
     lines = jnp.pad(lines, ((0, 1), (0, 0)))
     blank = jnp.zeros_like(lines)
     lines = jnp.where(core == 0, jnp.concatenate([lines, blank], axis=1), jnp.concatenate([blank, lines], axis=1))
     gains = jnp.concatenate([jnp.zeros_like(gain_two), gain_two, gain_three, gain_four], axis=0)
     small = jnp.concatenate([lines, gains.reshape(8, -1)], axis=0)
-    input_grad, small = edge(
-        "last", grad_first, [stream_zero, norm_gains[0:1], grad_one, small],
-        ways, rows, 4, 0, None, 9, "edge_seven",
+    input_grad, small, output, mixer_swapped = edge(
+        "last", grad_first, [stream_zero, norm_gains[0:1], grad_one, small, output_part, stream_three],
+        ways, rows, 4, 0, None, 9, "edge_seven", carried=mixer_joint,
     )
     lines = small[: CONV + 3 + STATE]
     gains = small[-8:].reshape(norm_gains.shape)
-
     late_grads = settle(late_swapped, late_group, 3)
+    early_grads = settle(early_swapped, early_group, 3)
     focus_grads = settle(focus_swapped, focus_group, 4)
-    early_grads = settle(early_swapped, early_group, 3)
+    gate_grad = settle(gate_swapped, 0, 1)[0]
     mixer_grads = settle(mixer_swapped, 0, 1)[0]
     in_rows = mixer_in.shape[1]
     return (
         output,
         input_grad,
         gains,
-        mixer_grads[: 2 * in_rows].reshape(2, in_rows, -1),
-        mixer_grads[2 * in_rows :],
+        jnp.stack([mixer_grads[:in_rows], gate_grad]),
+        mixer_grads[in_rows : in_rows + mixer_rows.shape[0]],
         lines[:CONV].T,
         lines[CONV],
         lines[CONV + 1],

time: 890 us -> 785 us (0.88)
  blocking collectives: 29 us -> 0 us
  starting transfers between devices: 59.3 us -> 37.1 us
  waiting for transfers between devices: 69.2 us -> 48.4 us
  Pallas kernels: 499 us -> 484 us
  between operations: 16.6 us -> 3.09 us
    all_to_all x1 -> x0, blocking collectives: 29 us -> none  [whole_group(): lax.all_to_all(value, 'dp', 0, 0, tiled=True, axis_index_groups=same_core)]
    pallas_call x9, Pallas kernels: 465 us -> 450 us  [edge(): pl.pallas_call(partial(edge_kernel, kind, extra, carried is not None, way...]
    all_to_all x8 -> x6, starting transfers between devices: 48.8 us -> 36.9 us  [swap(): return lax.all_to_all(stacked, 'dp', 0, 0, tiled=True)]
    all_to_all x2 -> x0, starting transfers between devices: 9.13 us -> none  [the longest x1 4.94 us: group_sum(): lax.all_to_all(part, 'dp', 0, 0, tiled=True, axis_index_groups=same_core)]
    unnamed x244 -> x271, local copies, waits for them, and re-layouts: 25.6 us -> 34.5 us
    all_to_all x8 -> x6, waiting for transfers between devices: 54 us -> 48.4 us  [swap(): return lax.all_to_all(stacked, 'dp', 0, 0, tiled=True)]
  transfers between devices with their start and end apart: 14 -> 7, of which waited for: 6 -> 2; matrix products, arithmetic and copies ran while one was open for 17% -> 11% of each run, Pallas kernels for 54% -> 27%
where the time goes in v2:
time: 785 us; the launch traced here: 778 us
  Pallas kernels  484 us (62%)
  matrix products  85 us (11%)
  other arithmetic  62.1 us (8%)
  local copies, waits for them, and re-layouts  58.2 us (7%)
  waiting for transfers between devices  48.4 us (6%)
  starting transfers between devices  37.1 us (5%)
    pallas_call x9, Pallas kernels, edge(): pl.pallas_call(partial(edge_kernel, kind, extra, carried is not None, way...  450 us
    all_to_all x6, waiting for transfers between devices, swap(): return lax.all_to_all(stacked, 'dp', 0, 0, tiled=True)  48.4 us
    all_to_all x6, starting transfers between devices, swap(): return lax.all_to_all(stacked, 'dp', 0, 0, tiled=True)  36.9 us
    unnamed x271, local copies, waits for them, and re-layouts  34.5 us
    dot_general x10, matrix products, project_t(): lax.dot_general(left, right, (((1,), (1,)), ((), ())), preferred_element_...  33.9 us
    dot_general x10, matrix products, project(): return jnp.dot(left, right, preferred_element_type=jnp.float32)  32.3 us
    pallas_call x1, Pallas kernels, scan_backward(): pl.pallas_call(partial(scan_backward_kernel, groups, tokens // groups), g...  21.1 us
    dot_general x11, matrix products, outer_rows(): lax.dot_general(left, right, (((0,), (0,)), ((), ())), preferred_element_...  18.8 us
  transfers between devices with their start and end apart: 7, of which 2 were waited for; matrix products, arithmetic and copies ran while one was open for 11% of the time, Pallas kernels for 27%

profile of v2, /device:TPU:1, one launch (start us, length us, event | category | flops | bytes accessed | tf_op | source)
XLA Modules:
  0.0 778.4 jit_solution(1990530186553382036)
XLA Ops:
  9.0 5.4 all-to-all-start
  15.1 2.1 opening.1
  29.9 30.2 %all-to-all-done = bf16[8,256,1024]{2,1,0:T(8,128)(2,1)} async-done(((bf16[8,256,1024]{2,1,0:T(8,128)(2,1)}), bf16[8,256,1024]{2,1,0:T(8,128)(2,1)}, u32[]{:S(2)}, u32[]{:S(2)}) %all-to-all-start) | async-done | bytes 4194336 | tf_op jit(solution)/shard_map/all_to_all | solution.py:1144
  60.1 8.3 %all-to-all-start.1 = ((bf16[8,292,512]{2,1,0:T(8,128)(2,1)}), bf16[8,292,512]{2,1,0:T(8,128)(2,1)}, u32[]{:S(2)}, u32[]{:S(2)}) async-start(bf16[8,292,512]{2,1,0:T(8,128)(2,1)} %bitcast_dynamic-update-slice_fusion.3), calls=%async_computation.1 | async-start | bytes 4849664 | tf_op jit(solution)/shard_map/all_to_all | solution.py:1144
  73.4 3.4 fusion.88
  76.9 18.2 %all-to-all-done.1 = bf16[8,292,512]{2,1,0:T(8,128)(2,1)} async-done(((bf16[8,292,512]{2,1,0:T(8,128)(2,1)}), bf16[8,292,512]{2,1,0:T(8,128)(2,1)}, u32[]{:S(2)}, u32[]{:S(2)}) %all-to-all-start.1) | async-done | bytes 2392096 | tf_op jit(solution)/shard_map/all_to_all | solution.py:1144
  95.1 8.0 %all-to-all-start.2 = ((bf16[8,256,768]{2,1,0:T(8,128)(2,1)}), bf16[8,256,768]{2,1,0:T(8,128)(2,1)}, u32[]{:S(2)}, u32[]{:S(2)}) async-start(bf16[8,256,768]{2,1,0:T(8,128)(2,1)} %fusion.48), calls=%async_computation.2 | async-start | bytes 6291456 | tf_op jit(solution)/shard_map/all_to_all | solution.py:1144
  110.0 4.2 reshape.282
  115.4 15.2 %mix_sum.1 = f32[256,256]{1,0:T(8,128)S(1)} custom-call(f32[256,256]{1,0:T(8,128)S(1)} %pad.43.refs_0_), custom_call_target="tpu_custom_call" | custom-call | flops 1 | bytes 1 | tf_op jit(solution)/shard_map/mix_sum/pallas_call | solution.py:1003
  133.2 7.9 %scan_forward.1 = bf16[256,512]{1,0:T(8,128)(2,1)S(1)} custom-call(f32[256]{0:T(256)S(1)} %subtract_bitcast_fusion.keep_ref, bf16[256,512]{1,0:T(8,128)(2,1)S(1)} %get-tuple-element.114.chan_ref, f32[256,512]{1,0:T(8,128)S(1)} %fusion.62.raw_ref, f32[256,512]{1,0:T(8,128)S(1)} %copy-done.4, f32[1,512]{1,0:T(1,128)S(1)} %bitcast.288, ...), custom_call_target="tpu_custom_call" | custom-call | flops 1 | bytes 17179869184 | tf_op jit(solution)/shard_map/scan_forward/pallas_call | solution.py:119
  143.1 5.0 all-to-all-start.3
  155.4 59.8 %edge_one.1 = (bf16[1024,2048]{1,0:T(8,128)(2,1)S(1)}, f32[32,2048]{1,0:T(8,128)S(1)}) custom-call(bf16[256,2048]{1,0:T(8,128)(2,1)S(1)} %convolution_convert_fusion.10.refs_0_, f32[32,2048]{1,0:T(8,128)S(1)} %dynamic-slice_convert_fusion.1.refs_1_, f32[1,2048]{1,0:T(1,128)S(1)} %get-tuple-element.280.refs_2_), custom_call_target="tpu_custom_call" | custom-call | flops 1 | bytes 1 | tf_op jit(solution)/shard_map/edge_one/pallas_call | solution.py:1003
  215.2 5.5 fusion.14
  221.0 5.2 convolution_convert_fusion.3.refs_0_
  226.2 53.8 %edge_two.1 = (bf16[256,2048]{1,0:T(8,128)(2,1)S(1)}, f32[32,2048]{1,0:T(8,128)S(1)}, bf16[1024,2048]{1,0:T(8,128)(2,1)}) custom-call(bf16[1024,2048]{1,0:T(8,128)(2,1)} %convolution_convert_fusion.3.refs_0_, f32[32,2048]{1,0:T(8,128)S(1)} %get-tuple-element.64.refs_1_, f32[1,2048]{1,0:T(1,128)S(1)} %get-tuple-element.282.refs_2_, ...), custom_call_target="tpu_custom_call" | custom-call | flops 1 | bytes 1 | tf_op jit(solution)/shard_map/edge_two/pallas_call | solution.py:1003
  280.0 5.2 all-to-all-start.4
  287.0 2.9 fusion.5.joint_ref
  293.3 47.6 %edge_three.1 = (bf16[1024,2048]{1,0:T(8,128)(2,1)S(1)}, f32[32,2048]{1,0:T(8,128)S(1)}) custom-call(bf16[256,2048]{1,0:T(8,128)(2,1)S(1)} %convolution_convert_fusion.15.refs_0_, f32[32,2048]{1,0:T(8,128)S(1)} %get-tuple-element.71.refs_1_, f32[1,2048]{1,0:T(1,128)S(1)} %copy-done.30), custom_call_target="tpu_custom_call" | custom-call | flops 1 | bytes 1 | tf_op jit(solution)/shard_map/edge_three/pallas_call | solution.py:1003
  342.9 5.4 fusion.11
  348.3 3.1 fusion.21
  351.4 2.5 convolution_convert_fusion.9
  353.9 6.0 convolution_convert_fusion.2.refs_0_
  361.4 4.6 convolution_convert_fusion.1.refs_4_
  366.0 52.7 %edge_four.1 = (bf16[256,2048]{1,0:T(8,128)(2,1)S(1)}, f32[32,2048]{1,0:T(8,128)S(1)}, f32[1,2048]{1,0:T(1,128)S(1)}, bf16[128,2048]{1,0:T(8,128)(2,1)S(1)}) custom-call(bf16[1024,2048]{1,0:T(8,128)(2,1)} %convolution_convert_fusion.2.refs_0_, f32[32,2048]{1,0:T(8,128)S(1)} %get-tuple-element.73.refs_1_.refs_6_, f32[1,2048]{1,0:T(1,128)S(1)} %copy-done.31, ...), custom_call_target="tpu_custom_call" | custom-call | flops 1 | bytes 1 | tf_op jit(solution)/shard_map/edge_four/pallas_call | solution.py:1003
  424.1 2.9 fusion.7.refs_0_
  430.0 59.9 %edge_five.1 = (bf16[1024,2048]{1,0:T(8,128)(2,1)}, f32[32,2048]{1,0:T(8,128)S(1)}, f32[1,2048]{1,0:T(1,128)S(1)}, bf16[8,256,768]{2,1,0:T(8,128)(2,1)S(1)}) custom-call(bf16[256,2048]{1,0:T(8,128)(2,1)S(1)} %fusion.7.refs_0_, f32[32,2048]{1,0:T(8,128)S(1)} %get-tuple-element.71.refs_1_, f32[1,2048]{1,0:T(1,128)S(1)} %get-tuple-element.282.refs_2_, ...), custom_call_target="tpu_custom_call" | custom-call | flops 1 | bytes 1 | tf_op jit(solution)/shard_map/edge_five/pallas_call | solution.py:1003
  490.0 5.9 fusion.24
  495.9 4.0 convolution_convert_fusion.8
  499.8 6.2 convolution_convert_fusion.refs_0_
  507.4 2.6 pad_maximum_fusion.refs_4_
  510.0 71.3 %edge_six.1 = (bf16[256,2048]{1,0:T(8,128)(2,1)S(1)}, f32[32,2048]{1,0:T(8,128)S(1)}, f32[1,2048]{1,0:T(1,128)S(1)}, bf16[8,256,1024]{2,1,0:T(8,128)(2,1)S(1)}) custom-call(bf16[1024,2048]{1,0:T(8,128)(2,1)} %convolution_convert_fusion.refs_0_, f32[32,2048]{1,0:T(8,128)S(1)} %get-tuple-element.64.refs_1_, f32[1,2048]{1,0:T(1,128)S(1)} %get-tuple-element.280.refs_2_, ...), custom_call_target="tpu_custom_call" | custom-call | flops 1 | bytes 1 | tf_op jit(solution)/shard_map/edge_six/pallas_call | solution.py:1003
  587.4 5.0 all-to-all-start.5
  592.5 3.0 add_bitcast_fusion.3
  597.3 2.2 bitcast_convert_fusion
  602.9 21.1 %scan_backward.1 = (f32[256,512]{1,0:T(8,128)}, bf16[256,512]{1,0:T(8,128)(2,1)}, bf16[256,512]{1,0:T(8,128)(2,1)}, f32[256,16,128]{2,1,0:T(8,128)}, f32[256,16,...) custom-call(f32[256]{0:T(256)} %copy-done.40, bf16[256,512]{1,0:T(8,128)(2,1)} %copy-done.2, ...), custom_call_target="tpu_custom_call" | custom-call | flops 1 | bytes 17179869184 | tf_op jit(solution)/shard_map/scan_backward/pallas_call | solution.py:229
  624.7 2.2 slice_dynamic-update-slice_fusion.6
  626.8 2.1 slice_dynamic-update-slice_fusion.5
  637.9 2.3 pad_maximum_fusion.2
  643.9 2.2 reduce_sum.71
  646.1 2.9 reduce_sum.72
  650.3 27.3 %mix_grad_sum.1 = (f32[256,256]{1,0:T(8,128)S(1)}, bf16[8,256,512]{2,1,0:T(8,128)(2,1)S(1)}) custom-call(f32[256,256]{1,0:T(8,128)S(1)} %select_maximum_fusion.refs_0_, bf16[8,256,512]{2,1,0:T(8,128)(2,1)S(1)} %bitcast.287), custom_call_target="tpu_custom_call" | custom-call | flops 1 | bytes 1 | tf_op jit(solution)/shard_map/mix_grad_sum/pallas_call | solution.py:1003
  681.2 3.5 convolution_convert_fusion.11.refs_0_
  688.4 4.2 convert_element_type.303
  693.0 4.1 fusion.2.refs_7_
  697.1 62.4 %edge_seven.1 = (f32[128,2048]{1,0:T(8,128)S(1)}, f32[32,1024]{1,0:T(8,128)S(1)}, f32[128,2048]{1,0:T(8,128)S(1)}, bf16[8,560,512]{2,1,0:T(8,128)(2,1)}) custom-call(bf16[256,2048]{1,0:T(8,128)(2,1)S(1)} %convolution_convert_fusion.11.refs_0_, f32[32,2048]{1,0:T(8,128)S(1)} %copy-done.10, f32[1,2048]{1,0:T(1,128)S(1)} %copy-done.33, ...), custom_call_target="tpu_custom_call" | custom-call | flops 1 | bytes 1 | tf_op jit(solution)/shard_map/edge_seven/pallas_call | solution.py:1003
  761.3 2.8 add_bitcast_fusion.1
  768.2 2.5 bitcast_convert_fusion.8
  773.2 2.7 pad_maximum_fusion.1
  (403 shorter events, 108.1 us)
Async XLA Ops:
  0.6 106.2 %collective-permute-start = (s32[2,4]{1,0:T(2,128)}, s32[2,4]{1,0:T(2,128)S(1)}, u32[]{:S(2)}, u32[]{:S(2)}) collective-permute-start(s32[2,4]{1,0:T(2,128)} %param.18), channel_id=1, source_target_pairs={{0,4},{4,0},{8,12},{12,8},{16,20},{20,16},{24,28},{28,24},{1,5},{5... | collective-permute-start | bytes 104 | tf_op jit(solution)/shard_map/ppermute | solution.py:1195
  9.0 6.0 copy-start.19
  9.0 8.2 %copy-start.103 = (f32[1024,16]{0,1:T(8,128)S(1)}, f32[1024,16]{0,1:T(8,128)}, u32[]{:S(2)}) copy-start(f32[1024,16]{0,1:T(8,128)} %param.25) | copy-start | bytes 196612
  9.0 51.1 %all-to-all-start = ((bf16[8,256,1024]{2,1,0:T(8,128)(2,1)}), bf16[8,256,1024]{2,1,0:T(8,128)(2,1)}, u32[]{:S(2)}, u32[]{:S(2)}) async-start(bf16[8,256,1024]{2,1,0:T(8,128)(2,1)} %constant_dynamic-update-slice_fusion), calls=%async_computation | async-start | bytes 8388608 | tf_op jit(solution)/shard_map/all_to_all | solution.py:1144
  17.3 115.8 %copy-start.27 = (f32[16,512]{1,0:T(8,128)}, f32[16,512]{1,0:T(8,128)S(1)}, u32[]{:S(2)}) copy-start(f32[16,512]{1,0:T(8,128)S(1)} %negate_bitcast_fusion.rate_ref) | copy-start | bytes 98308
  29.9 38.6 %copy-start.114 = (f32[1024,4]{0,1:T(4,128)S(1)}, f32[1024,4]{0,1:T(4,128)}, u32[]{:S(2)}) copy-start(f32[1024,4]{0,1:T(4,128)} %param.22) | copy-start | bytes 49156
  29.9 38.7 %copy-start.79 = (bf16[256,256]{1,0:T(8,128)(2,1)S(1)}, bf16[256,256]{1,0:T(8,128)(2,1)}, u32[]{:S(2)}) copy-start(bf16[256,256]{1,0:T(8,128)(2,1)} %get-tuple-element.181) | copy-start | bytes 393220
  29.9 38.7 %copy-start.80 = (bf16[256,256]{1,0:T(8,128)(2,1)S(1)}, bf16[256,256]{1,0:T(8,128)(2,1)}, u32[]{:S(2)}) copy-start(bf16[256,256]{1,0:T(8,128)(2,1)} %get-tuple-element.298) | copy-start | bytes 393220
  29.9 39.6 %copy-start.77 = (bf16[256,256]{1,0:T(8,128)(2,1)S(1)}, bf16[256,256]{1,0:T(8,128)(2,1)}, u32[]{:S(2)}) copy-start(bf16[256,256]{1,0:T(8,128)(2,1)} %get-tuple-element.180) | copy-start | bytes 393220
  29.9 39.6 %copy-start.78 = (bf16[256,256]{1,0:T(8,128)(2,1)S(1)}, bf16[256,256]{1,0:T(8,128)(2,1)}, u32[]{:S(2)}) copy-start(bf16[256,256]{1,0:T(8,128)(2,1)} %get-tuple-element.299) | copy-start | bytes 393220
  29.9 41.1 %copy-start.76 = (bf16[3,256,512]{2,1,0:T(8,128)(2,1)S(1)}, bf16[3,256,512]{2,1,0:T(8,128)(2,1)}, u32[]{:S(2)}) copy-start(bf16[3,256,512]{2,1,0:T(8,128)(2,1)} %param.29) | copy-start | bytes 2359300
  60.1 35.0 %all-to-all-start.1 = ((bf16[8,292,512]{2,1,0:T(8,128)(2,1)}), bf16[8,292,512]{2,1,0:T(8,128)(2,1)}, u32[]{:S(2)}, u32[]{:S(2)}) async-start(bf16[8,292,512]{2,1,0:T(8,128)(2,1)} %bitcast_dynamic-update-slice_fusion.3), calls=%async_computation.1 | async-start | bytes 4849664 | tf_op jit(solution)/shard_map/all_to_all | solution.py:1144
  68.5 39.1 %copy-start.95 = (f32[512,1]{0,1:T(1,128)}, f32[512,1]{0,1:T(1,128)S(1)}, u32[]{:S(2)}) copy-start(f32[512,1]{0,1:T(1,128)S(1)} %get-tuple-element.283) | copy-start | bytes 6148
  68.5 39.1 %copy-start.97 = (f32[512,1]{0,1:T(1,128)}, f32[512,1]{0,1:T(1,128)S(1)}, u32[]{:S(2)}) copy-start(f32[512,1]{0,1:T(1,128)S(1)} %get-tuple-element.284) | copy-start | bytes 6148
  68.5 39.1 %copy-start.99 = (f32[512,1]{0,1:T(1,128)}, f32[512,1]{0,1:T(1,128)S(1)}, u32[]{:S(2)}) copy-start(f32[512,1]{0,1:T(1,128)S(1)} %get-tuple-element.285) | copy-start | bytes 6148
  68.6 39.1 %copy-start.101 = (f32[512,1]{0,1:T(1,128)}, f32[512,1]{0,1:T(1,128)S(1)}, u32[]{:S(2)}) copy-start(f32[512,1]{0,1:T(1,128)S(1)} %get-tuple-element.286) | copy-start | bytes 6148
  76.9 30.8 %copy-start.48 = (f32[256,1024]{1,0:T(8,128)}, f32[256,1024]{1,0:T(8,128)S(1)}, u32[]{:S(2)}) copy-start(f32[256,1024]{1,0:T(8,128)S(1)} %fusion.88) | copy-start | bytes 3145732
  76.9 26.2 %copy-start.123 = (s32[2,4]{1,0:T(2,128)S(1)}, s32[2,4]{1,0:T(2,128)}, u32[]{:S(2)}) copy-start(s32[2,4]{1,0:T(2,128)} %param.18) | copy-start | bytes 100
  76.9 26.3 %copy-start.117 = (f32[1024]{0:T(1024)S(1)}, f32[1024]{0:T(1024)}, u32[]{:S(2)}) copy-start(f32[1024]{0:T(1024)} %param.23) | copy-start | bytes 12292
  76.9 26.4 %copy-start.118 = (f32[1024]{0:T(1024)S(1)}, f32[1024]{0:T(1024)}, u32[]{:S(2)}) copy-start(f32[1024]{0:T(1024)} %param.24) | copy-start | bytes 12292
  76.9 26.4 %copy-start.119 = (f32[1024]{0:T(1024)S(1)}, f32[1024]{0:T(1024)}, u32[]{:S(2)}) copy-start(f32[1024]{0:T(1024)} %param.26) | copy-start | bytes 12292
  95.1 48.0 %all-to-all-start.2 = ((bf16[8,256,768]{2,1,0:T(8,128)(2,1)}), bf16[8,256,768]{2,1,0:T(8,128)(2,1)}, u32[]{:S(2)}, u32[]{:S(2)}) async-start(bf16[8,256,768]{2,1,0:T(8,128)(2,1)} %fusion.48), calls=%async_computation.2 | async-start | bytes 6291456 | tf_op jit(solution)/shard_map/all_to_all | solution.py:1144
  103.3 29.8 %copy-start.34 = (f32[512]{0:T(512)}, f32[512]{0:T(512)S(1)}, u32[]{:S(2)}) copy-start(f32[512]{0:T(512)S(1)} %dynamic_slice.23) | copy-start | bytes 6148
  103.4 29.7 %copy-start.35 = (f32[512]{0:T(512)}, f32[512]{0:T(512)S(1)}, u32[]{:S(2)}) copy-start(f32[512]{0:T(512)S(1)} %dynamic_slice.25) | copy-start | bytes 6148
  110.0 23.2 %copy-start.2 = (bf16[256,512]{1,0:T(8,128)(2,1)}, bf16[256,512]{1,0:T(8,128)(2,1)S(1)}, u32[]{:S(2)}) copy-start(bf16[256,512]{1,0:T(8,128)(2,1)S(1)} %get-tuple-element.114.chan_ref) | copy-start | bytes 786436
  115.4 17.8 %copy-start.40 = (f32[256]{0:T(256)}, f32[256]{0:T(256)S(1)}, u32[]{:S(2)}) copy-start(f32[256]{0:T(256)S(1)} %subtract_bitcast_fusion.keep_ref) | copy-start | bytes 3076
  132.5 8.5 %copy-start = (f32[256,16,128]{2,1,0:T(8,128)}, f32[256,16,128]{2,1,0:T(8,128)S(1)}, u32[]{:S(2)}) copy-start(f32[256,16,128]{2,1,0:T(8,128)S(1)} %broadcast_in_dim.21.out_ref) | copy-start | bytes 6291460
  143.1 136.9 %all-to-all-start.3 = ((bf16[8,256,1024]{2,1,0:T(8,128)(2,1)}), bf16[8,256,1024]{2,1,0:T(8,128)(2,1)}, u32[]{:S(2)}, u32[]{:S(2)}) async-start(bf16[8,256,1024]{2,1,0:T(8,128)(2,1)} %constant_dynamic-update-slice_fusion.8), calls=%async_computation.3 | async-start | bytes 8388608 | tf_op jit(solution)/shard_map/all_to_all | solution.py:1144
  154.6 60.6 %copy-start.9 = (f32[32,2048]{1,0:T(8,128)}, f32[32,2048]{1,0:T(8,128)S(1)}, u32[]{:S(2)}) copy-start(f32[32,2048]{1,0:T(8,128)S(1)} %dynamic-slice_convert_fusion.1.refs_1_) | copy-start | bytes 786436
  280.0 6.8 copy-start.105
  280.0 6.8 copy-start.113
  280.0 62.8 %all-to-all-start.4 = ((bf16[8,256,768]{2,1,0:T(8,128)(2,1)}), bf16[8,256,768]{2,1,0:T(8,128)(2,1)}, u32[]{:S(2)}, u32[]{:S(2)}) async-start(bf16[8,256,768]{2,1,0:T(8,128)(2,1)} %copy-done.58), calls=%async_computation.4 | async-start | bytes 6291456 | tf_op jit(solution)/shard_map/all_to_all | solution.py:1144
  342.9 23.1 %copy-start.17 = (f32[32,2048]{1,0:T(8,128)}, f32[32,2048]{1,0:T(8,128)S(1)}, u32[]{:S(2)}) copy-start(f32[32,2048]{1,0:T(8,128)S(1)} %get-tuple-element.73.refs_1_.refs_6_) | copy-start | bytes 786436
  489.9 5.9 copy-start.7
  489.9 5.9 copy-start.42
  499.8 6.2 copy-start.60
  499.8 6.2 copy-start.122
  510.0 74.0 %copy-start.62 = (bf16[2336,512]{1,0:T(8,128)(2,1)S(1)}, bf16[2336,512]{1,0:T(8,128)(2,1)}, u32[]{:S(2)}) copy-start(bf16[2336,512]{1,0:T(8,128)(2,1)} %reshape.282) | copy-start | bytes 7176196
  587.4 52.8 %all-to-all-start.5 = ((bf16[8,256,768]{2,1,0:T(8,128)(2,1)}), bf16[8,256,768]{2,1,0:T(8,128)(2,1)}, u32[]{:S(2)}, u32[]{:S(2)}) async-start(bf16[8,256,768]{2,1,0:T(8,128)(2,1)} %pad_maximum_fusion.4), calls=%async_computation.5 | async-start | bytes 6291456 | tf_op jit(solution)/shard_map/all_to_all | solution.py:1144
  646.1 31.5 %copy-start.3 = (bf16[256,512]{1,0:T(8,128)(2,1)S(1)}, bf16[256,512]{1,0:T(8,128)(2,1)}, u32[]{:S(2)}) copy-start(bf16[256,512]{1,0:T(8,128)(2,1)} %copy-done.2) | copy-start | bytes 786436
  646.1 31.7 %copy-start.107 = (f32[256]{0:T(256)S(1)}, f32[256]{0:T(256)}, u32[]{:S(2)}) copy-start(f32[256]{0:T(256)} %copy-done.106) | copy-start | bytes 3076
  646.1 31.7 %copy-start.109 = (f32[256]{0:T(256)S(1)}, f32[256]{0:T(256)}, u32[]{:S(2)}) copy-start(f32[256]{0:T(256)} %copy-done.108) | copy-start | bytes 3076
  646.1 31.7 %copy-start.111 = (f32[256]{0:T(256)S(1)}, f32[256]{0:T(256)}, u32[]{:S(2)}) copy-start(f32[256]{0:T(256)} %copy-done.110) | copy-start | bytes 3076
  649.0 28.8 %copy-start.52 = (f32[253,512]{1,0:T(8,128)S(1)}, f32[253,512]{1,0:T(8,128)}, u32[]{:S(2)}) copy-start(f32[253,512]{1,0:T(8,128)} %copy-done.51) | copy-start | bytes 1554436
  649.0 28.8 %copy-start.54 = (f32[254,512]{1,0:T(8,128)S(1)}, f32[254,512]{1,0:T(8,128)}, u32[]{:S(2)}) copy-start(f32[254,512]{1,0:T(8,128)} %copy-done.53) | copy-start | bytes 1560580
  649.0 28.8 %copy-start.56 = (f32[255,512]{1,0:T(8,128)S(1)}, f32[255,512]{1,0:T(8,128)}, u32[]{:S(2)}) copy-start(f32[255,512]{1,0:T(8,128)} %copy-done.55) | copy-start | bytes 1566724
  649.0 28.9 %copy-start.71 = (f32[256,512]{1,0:T(8,128)S(1)}, f32[256,512]{1,0:T(8,128)}, u32[]{:S(2)}) copy-start(f32[256,512]{1,0:T(8,128)} %get-tuple-element.115) | copy-start | bytes 1572868
  649.0 28.9 %copy-start.87 = (f32[256,512]{1,0:T(8,128)S(1)}, f32[256,512]{1,0:T(8,128)}, u32[]{:S(2)}) copy-start(f32[256,512]{1,0:T(8,128)} %get-tuple-element.84) | copy-start | bytes 1572868
  (83 other events, 229.8 us)

commit v3 on v2

--- a/solution.py
+++ b/solution.py
@@ -5,6 +5,7 @@
 import jax.numpy as jnp
 from jax import lax
 from jax.experimental import pallas as pl
+from jax.experimental.layout import Layout, with_layout_constraint
 from jax.experimental.pallas import tpu as pltpu
 from jax.sharding import PartitionSpec as P
 
@@ -747,16 +748,104 @@
     return deep + [copy for one in far for copy in one.values()] + near
 
 
-def exchange_start(place, source_ref, target_ref, sems):
-    copies = [
-        send(source_ref.at[spot], target_ref.at[place.spot], sems, at, spot, place.depth)
-        for at, spot in enumerate(
-            [place.across(turned, swapped) for turned in (6, 2, 4) for swapped in (False, True)] + [place.partner]
+class Exchange:
+    def __init__(self, place, items, sems):
+        self.place, self.items, self.sems = place, items, sems
+        self.copies, self.own = [], []
+
+    def start(self):
+        place = self.place
+        spots = [place.across(turned, swapped) for turned in (6, 2, 4) for swapped in (False, True)] + [place.partner]
+        for at, (source, target) in enumerate(self.items):
+            for slot, spot in enumerate(spots):
+                self.copies.append(
+                    send(source(spot), target(place.spot), self.sems, at * 8 + slot, spot, place.depth)
+                )
+            own = pltpu.make_async_copy(source(place.spot), target(place.spot), self.sems[1].at[at * 8 + 7])
+            own.start()
+            self.own.append(own)
+
+    def close(self):
+        for copy in self.own + self.copies:
+            copy.wait()
+
+
+def columns_at(half, size):
+    return pl.ds(pl.multiple_of(half * size, size), size)
+
+
+def blocks_of(refs, size):
+    return [(ref, at) for ref in refs for at in range(ref.shape[2] // size)]
+
+
+def spread_items(size, refs, out):
+    return [
+        (
+            lambda spot, ref=ref, at=at: ref.at[spot, :, pl.ds(at * size, size)],
+            lambda spot, to=to: out.at[to, :, columns_at(spot, size)],
         )
+        for to, (ref, at) in enumerate(blocks_of(refs, size))
     ]
-    own = pltpu.make_async_copy(source_ref.at[place.spot], target_ref.at[place.spot], sems[1].at[7])
-    own.start()
-    return copies, own
+
+
+def chip_items(size, refs, out):
+    return [
+        (
+            lambda spot, ref=ref, at=at: ref.at[spot, :, pl.ds(at * size, size)],
+            lambda spot, to=to: out.at[spot // 2, to, :, columns_at(spot % 2, size)],
+        )
+        for to, (ref, at) in enumerate(blocks_of(refs, size))
+    ]
+
+
+def layers(refs):
+    return [ref.at[at] if len(ref.shape) == 3 else ref for ref in refs for at in range(ref.shape[0] if len(ref.shape) == 3 else 1)]
+
+
+def plane_items(spots, refs, out):
+    blocks = layers(refs)
+    size = blocks[0].shape[1] // spots
+    return [
+        (
+            lambda spot, block=block: block.at[:, columns_at(spot, size)],
+            lambda spot, at=at: out.at[spot, :, pl.ds(at * size, size)],
+        )
+        for at, block in enumerate(blocks)
+    ]
+
+
+def core_items(refs, out):
+    blocks = layers(refs)
+    size = blocks[0].shape[1] // 2
+    return [
+        (
+            lambda half, block=block: block.at[:, columns_at(half, size)],
+            lambda spot, at=at: out.at[spot, :, pl.ds(at * size, size)],
+        )
+        for at, block in enumerate(blocks)
+    ]
+
+
+def handed_items(out):
+    return [(None, lambda spot: out.at[spot])]
+
+
+class Load:
+    def __init__(self, mode, arrays, out, items, count, stage):
+        self.mode, self.arrays, self.items, self.count, self.stage = mode, arrays, items, count, stage
+        self.out = jax.ShapeDtypeStruct(out, arrays[0].dtype)
+
+    def begin(self, place, refs, out, sems):
+        if self.mode == "second":
+            mover = Pull(place, self.items(out), sems)
+            mover.second(False)
+        elif self.mode == "first":
+            mover = Pull(place, self.items(refs, out), sems)
+            mover.first()
+        else:
+            mover = Exchange(place, self.items(refs, out), sems)
+            mover.start()
+        return mover
 
 
 def spread_stage(place, rows, all_ref, sems, name="deep_back"):
@@ -820,7 +909,7 @@
     return {name: (refs[2 * at], refs[2 * at + 1]) for at, name in enumerate(names)}
 
 
-def edge_kernel(kind, extra, carrying, ways, rows, parts, in_group, out_group, names, counts, *refs):
+def edge_kernel(kind, extra, loads, ways, rows, parts, in_group, out_group, names, counts, *refs):
     place = Place(ways)
     share = rows // ways
     ins, outs = list(refs[: counts[0]]), list(refs[counts[0] : counts[0] + counts[1]])
@@ -841,10 +930,12 @@
         small_ref, late_ref, three_ref = ins.pop(0), ins.pop(0), ins.pop(0)
         dgain_ref, late_out_ref = outs.pop(0), outs.pop(0)
         low_s, small_s, late_s, late_low_s = [scratch.pop(0) for _ in range(4)]
-    if carrying:
-        source_ref, target_ref = ins.pop(), outs.pop()
-    everyone = carrying or kind == "last"
-    greet(place, turns(6) if everyone else sorted({*turns(in_group), *turns(out_group)}), carrying)
+    moving = []
+    for load in reversed(loads):
+        moving.append(([ins.pop() for _ in load.arrays][::-1], outs.pop()))
+    moving = moving[::-1]
+    everyone = loads or kind == "last"
+    greet(place, turns(6) if everyone else sorted({*turns(in_group), *turns(out_group)}), bool(loads))
     first = Reduction(place, in_group, rows, parts, part_ref, near_s, sum_s, far_s, sems, ("near", "far"))
     waiting = []
     freight = {}
@@ -884,8 +975,9 @@
 
     def on_the_way(stage):
         between(stage)
-        if carrying and stage == (1 if in_group else 0):
-            carried.append(exchange_start(place, source_ref, target_ref, sems["exchange"]))
+        for at, load in enumerate(loads):
+            if load.stage == stage:
+                carried.append(load.begin(place, *moving[at], sems[f"load{at}"]))
 
     if kind == "last":
         late = deep_sends(place, share, late_ref, 0, late_s, slice(None), sems["late"], 0)
@@ -943,16 +1035,13 @@
         for part in range(parts):
             load_out_ref[:, second.lanes(part)] = second.chip_sum(part).astype(load_out_ref.dtype)
         waiting += second.sent()
-    for copies, own in carried:
-        for copy in copies:
-            copy.wait_recv()
-        own.wait()
-        waiting += copies
+    for mover in carried:
+        mover.close()
     for copy in waiting:
         copy.wait_send()
 
 
-def edge(kind, part, extras, ways, rows, parts, in_group, out_group, ident, name, extra=None, carried=None):
+def edge(kind, part, extras, ways, rows, parts, in_group, out_group, ident, name, extra=None, loads=()):
     width = part.shape[1]
     share = rows // ways
     in_far, out_far = len(turns(in_group)), len(turns(out_group or 0))
@@ -992,23 +1081,28 @@
         scratch = scratch + reducing
     vmem, whole_memory = pl.BlockSpec(memory_space=pltpu.VMEM), pl.BlockSpec(memory_space=pl.ANY)
     in_specs, out_specs = [vmem] * (1 + len(extras)), [vmem] * len(outs)
-    if carried is not None:
-        names["exchange"] = 8
-        extras = list(extras) + [carried]
-        outs = outs + [jax.ShapeDtypeStruct(carried.shape, carried.dtype)]
-        in_specs, out_specs = in_specs + [whole_memory], out_specs + [whole_memory]
+    aliases, extras, outs = {}, list(extras), list(outs)
+    for at, load in enumerate(loads):
+        names[f"load{at}"] = 8 * load.count
+        if load.mode == "second":
+            aliases[1 + len(extras)] = len(outs)
+        extras += load.arrays
+        outs.append(load.out)
+        in_specs += [whole_memory] * len(load.arrays)
+        out_specs.append(whole_memory)
     names = {key: count for key, count in names.items() if count}
     if not in_far:
         names["far"] = 1
     return pl.pallas_call(
         partial(
-            edge_kernel, kind, extra, carried is not None, ways, rows, parts, in_group, out_group, names,
+            edge_kernel, kind, extra, loads, ways, rows, parts, in_group, out_group, names,
             (1 + len(extras), len(outs), len(scratch)),
         ),
         in_specs=in_specs,
         out_specs=out_specs,
         out_shape=outs,
         scratch_shapes=scratch + sem_shapes(names),
+        input_output_aliases=aliases,
         compiler_params=pltpu.CompilerParams(
             collective_id=ident, has_side_effects=True, vmem_limit_bytes=48 << 20
         ),
@@ -1017,33 +1111,99 @@
     )(part, *extras)
 
 
-def opening_kernel(ways, rows, hidden_ref, gain_ref, first_ref, send_sem, recv_sem):
+class Pull:
+    def __init__(self, place, items, sems):
+        self.place, self.items, self.sems = place, items, sems
+        self.copies, self.handed = {}, set()
+
+    def go(self, at, key, slot, source, spot, target):
+        self.copies[at, key] = send(source, target, self.sems, at * 8 + slot, spot, self.place.depth)
+
+    def first(self):
+        place = self.place
+        for at, (source, target) in enumerate(self.items):
+            mine = target(place.spot)
+            for turned in (2, 4):
+                self.go(at, (turned, False), turned - 2, source(place.core), place.across(turned), mine)
+                self.go(at, (turned, True), turned - 1, source(1 - place.core), place.across(turned, True), mine)
+            self.go(at, "near", 4, source(1 - place.core), place.partner, mine)
+            own = pltpu.make_async_copy(source(place.core), mine, self.sems[1].at[at * 8 + 7])
+            own.start()
+            self.copies[at, "own"] = own
+
+    def second(self, fresh=True):
+        place = self.place
+        for at, (_, target) in enumerate(self.items):
+            for slot, turned, swapped, to in ((5, 2, False, 4), (6, 4, True, 2)):
+                if fresh:
+                    self.copies[at, (turned, swapped)].wait_recv()
+                    self.handed.add((at, (turned, swapped)))
+                block = target(place.across(turned, swapped))
+                self.go(at, ("on", turned), slot, block, place.across(to), block)
+
+    def close(self):
+        for (at, key), copy in self.copies.items():
+            if key == "own":
+                copy.wait()
+            else:
+                if (at, key) not in self.handed:
+                    copy.wait_recv()
+                copy.wait_send()
+
+
+def opening_kernel(ways, rows, hidden_ref, gain_ref, in_ref, rows_ref, first_ref, in_out, rows_out, *sems):
     place = Place(ways)
-    barrier = pltpu.get_barrier_semaphore()
-    pl.semaphore_signal(barrier, inc=1, device_id=(place.partner, place.depth), device_id_type=MESH)
-    pl.semaphore_wait(barrier, 1)
+    greet_plane(place)
+    size = rows_out.shape[2]
+    items = [
+        (
+            lambda half, at=at: in_ref.at[at, :, columns_at(half, size)],
+            lambda spot, at=at: in_out.at[spot, :, pl.ds(at * size, size)],
+        )
+        for at in range(in_ref.shape[0])
+    ]
+    items.append((lambda half: rows_ref.at[:, columns_at(half, size)], lambda spot: rows_out.at[spot]))
+    pull = Pull(place, items, sems[2:])
+    pull.first()
     stream = hidden_ref[...].astype(jnp.float32)
     scale = lax.rsqrt(jnp.mean(stream * stream, axis=-1, keepdims=True) + EPS)
     first_ref[rows_at(place.core, rows, rows), :] = (stream * scale * gain_ref[...]).astype(jnp.bfloat16)
     mine = first_ref.at[rows_at(place.core, rows, rows), :]
-    send(mine, mine, (send_sem, recv_sem), 0, place.partner, place.depth).wait()
-
-
-def opening(hidden, gain, ways, ident):
+    copy = send(mine, mine, sems[:2], 0, place.partner, place.depth)
+    pull.second()
+    copy.wait()
+    pull.close()
+
+
+def greet_plane(place):
+    barrier = pltpu.get_barrier_semaphore()
+    peers = [place.partner] + [place.across(turned, swapped) for turned in (2, 4) for swapped in (False, True)]
+    for peer in peers:
+        pl.semaphore_signal(barrier, inc=1, device_id=(peer, place.depth), device_id_type=MESH)
+    pl.semaphore_wait(barrier, len(peers))
+
+
+def opening(hidden, gain, in_weights, row_weights, spots, ways, ident):
     rows, width = hidden.shape
-    vmem = pl.BlockSpec(memory_space=pltpu.VMEM)
+    vmem, whole_memory = pl.BlockSpec(memory_space=pltpu.VMEM), pl.BlockSpec(memory_space=pl.ANY)
+    kinds, depth, columns = in_weights.shape
+    low = jnp.bfloat16
     return pl.pallas_call(
         partial(opening_kernel, ways, rows),
-        in_specs=[vmem] * 2,
-        out_specs=vmem,
-        out_shape=jax.ShapeDtypeStruct((2 * rows, width), jnp.bfloat16),
-        scratch_shapes=[pltpu.SemaphoreType.DMA((1,))] * 2,
+        in_specs=[vmem] * 2 + [whole_memory] * 2,
+        out_specs=[vmem] + [whole_memory] * 2,
+        out_shape=[
+            jax.ShapeDtypeStruct((2 * rows, width), low),
+            jax.ShapeDtypeStruct((spots, depth, kinds * columns // 2), low),
+            jax.ShapeDtypeStruct((spots, row_weights.shape[0], columns // 2), low),
+        ],
+        scratch_shapes=[pltpu.SemaphoreType.DMA((1,))] * 2 + [pltpu.SemaphoreType.DMA((8 * (kinds + 1),))] * 2,
         compiler_params=pltpu.CompilerParams(
             collective_id=ident, has_side_effects=True, vmem_limit_bytes=40 << 20
         ),
         cost_estimate=pl.CostEstimate(flops=1, bytes_accessed=1, transcendentals=0),
         name="opening",
-    )(hidden, gain)
+    )(hidden, gain, in_weights, row_weights)
 
 
 def probs_of(query, keys, allowed):
@@ -1140,20 +1300,42 @@
     )
 
 
+def in_order(value):
+    return with_layout_constraint(value, Layout(major_to_minor=tuple(range(value.ndim))))
+
+
 def swap(stacked):
     return lax.all_to_all(stacked, "dp", 0, 0, tiled=True)
 
 
-def settle(swapped, group, blocks):
-    subs = subs_of(group)
-    count = swapped.shape[0]
-    size = swapped.shape[2] // blocks
-    sums = []
-    for sub in range(subs):
-        sums.append(sum(swapped[spot].astype(jnp.float32) for spot in range(count) if sub_of(spot, group) == sub))
-    return [
-        jnp.concatenate([one[:, block * size : (block + 1) * size] for one in sums], axis=1) for block in range(blocks)
-    ]
+def spread_out_kernel(came_ref, pair_ref, last_ref):
+    size = last_ref.shape[1]
+    for at in range(2):
+        pair_ref[at] = came_ref[0, :, at * size : (at + 1) * size].astype(jnp.float32)
+    last_ref[...] = came_ref[0, :, 2 * size :].astype(jnp.float32)
+
+
+def spread_out(came):
+    spots, rows, columns = came.shape
+    size = columns // 3
+    return pl.pallas_call(
+        spread_out_kernel,
+        grid=(spots,),
+        in_specs=[pl.BlockSpec((1, rows, columns), lambda i: (i, 0, 0))],
+        out_specs=[
+            pl.BlockSpec((2, rows, size), lambda i: (0, 0, i)),
+            pl.BlockSpec((rows, size), lambda i: (0, i)),
+        ],
+        out_shape=[
+            jax.ShapeDtypeStruct((2, rows, spots * size), jnp.float32),
+            jax.ShapeDtypeStruct((rows, spots * size), jnp.float32),
+        ],
+        name="spread_out",
+    )(came)
+
+
+def chip_total(came):
+    return jnp.sum(came.astype(jnp.float32), axis=0)
 
 
 def after(value, *others):
@@ -1194,7 +1376,12 @@
     def swapped_core(value):
         return lax.ppermute(value, "dp", [(at, at ^ 1) for at in range(spots)])
 
-    in_weights = swap(pull(spots, ([mixer_in[0], mixer_in[1]], 0)))
+    own_rows = mixer_rows.shape[0]
+    padded_rows = jnp.pad(mixer_rows, ((0, -own_rows % 16), (0, 0)))
+    first_low, in_weights, row_weights = opening(
+        hidden_in, norm_gains[0:1], mixer_in, padded_rows, spots, ways, 20
+    )
+    row_weights = row_weights[:, :own_rows]
 
     other_lengths = swapped_core(seq_lengths)
     lengths = jnp.where(
@@ -1205,8 +1392,6 @@
     keeping = 1.0 - starts.reshape(-1).astype(jnp.float32)
     groups = 2 * seq_lengths.shape[0]
 
-    first_low = opening(hidden_in, norm_gains[0:1], ways, 20)
-    row_weights = swap(after(pull(spots, ([mixer_rows], 0)), in_weights, first_low))
     stream_zero = lax.dynamic_slice_in_dim(hidden_in, depth * share, share, 0).astype(jnp.float32)
 
     channels = conv_weight.shape[0] // 2
@@ -1222,15 +1407,28 @@
     channel_low = channel_full.astype(low)
     row_mat = row_weights.reshape(-1, channels)
     early_blocks = [early_gate_up[0], early_gate_up[1], early_down]
-    focus_blocks = [attention_in[0], attention_in[1], attention_in[2], attention_out]
-    early_weights = swap(after(pull(spots, (early_blocks, early_group)), row_weights, both))
+    early_weights = swap(after(pull(spots, (early_blocks, early_group)), first_low))
     out_mat = row_mat[:width]
     select_mat = row_mat[width : width + PROJ_OUT]
     step_mat = row_mat[width + PROJ_OUT :]
 
-    def mixed_sum(part, ident, name, carried=None):
+    def spread_load(joints, size, stage):
+        count = sum(one.shape[2] // size for one in joints)
+        return Load(
+            "exchange", joints, (count, joints[0].shape[1], spots * size), partial(spread_items, size), count, stage
+        )
+
+    def chip_load(joints, size, stage):
+        count = sum(one.shape[2] // size for one in joints)
+        out = (spots // 2, count, joints[0].shape[1], 2 * size)
+        return Load("exchange", joints, out, partial(chip_items, size), count, stage)
+
+    def by_spot(joint):
+        return joint.astype(low).reshape(spots, -1, joint.shape[1])
+
+    def mixed_sum(part, ident, name, loads=()):
         padded = jnp.pad(part, ((0, 0), (0, 256 - PROJ_OUT)))
-        total, *came = edge("sum", padded, [], ways, rows, 1, 0, 0, ident, name, carried=carried)
+        total, *came = edge("sum", padded, [], ways, rows, 1, 0, 0, ident, name, loads=loads)
         return total[:, :PROJ_OUT], *came
 
     mix_rows, = mixed_sum(project_t(channel_low, select_mat), 1, "mix_sum")
@@ -1243,11 +1441,13 @@
     mixer_low = scan_forward(
         keeping, channel_low, step_raw, gate_half, bias, rates_t, skip, in_wide, out_wide, groups, LANES
     )
-    focus_weights = swap(after(pull(spots, (focus_blocks, focus_group)), early_weights, mixer_low))
-    early_mat, focus_mat = [one.reshape(width, -1) for one in (early_weights, focus_weights)]
-    second_low, stream_one = edge(
+    early_mat = early_weights.reshape(width, -1)
+    focus_blocks = [attention_in, attention_out]
+    heads_width = attention_out.shape[1] // 2
+    focus_pull = Load("first", focus_blocks, (spots, width // spots, 4 * heads_width), core_items, 4, 0)
+    second_low, stream_one, focus_half = edge(
         "forward", project_t(mixer_low, out_mat).astype(low), [stream_zero, norm_gains[1:2]],
-        ways, rows, 4, 0, early_group, 2, "edge_one",
+        ways, rows, 4, 0, early_group, 2, "edge_one", loads=[focus_pull],
     )
 
     def ffn(normed, mat):
@@ -1257,19 +1457,21 @@
         return project_t(hidden, mat[:, 2 * units :]).astype(low), both, hidden
 
     early_part, early_both, early_hidden = ffn(second_low, early_mat)
-    third_low, stream_two, last_grad = edge(
+    third_low, stream_two, last_grad, focus_weights = edge(
         "forward", early_part, [stream_one, norm_gains[2:3], output_grad], ways, rows, 4, early_group, 0, 3, "edge_two",
-        "gather",
-    )
-
-    late_blocks = [late_gate_up[0], late_gate_up[1], late_down]
-    late_weights = swap(after(pull(spots, (late_blocks, late_group)), focus_weights, third_low))
-    heads_width = focus_mat.shape[1] // 4
+        "gather", [Load("second", [focus_half], focus_half.shape, handed_items, 1, 1)],
+    )
+    focus_mat = focus_weights.reshape(width, -1)
+
+    late_pull = Load(
+        "exchange", [late_gate_up, late_down], (spots, width // spots, 3 * late_down.shape[1] // spots),
+        partial(plane_items, spots), 3, 0,
+    )
     down, side = flat_segs[:, None], flat_segs.reshape(2, rows)
     joint_low, attended_low = attend(project(third_low, focus_mat[:, : 3 * heads_width]), down, side, rows)
-    fourth_low, stream_three = edge(
+    fourth_low, stream_three, late_weights = edge(
         "forward", project_t(attended_low, focus_mat[:, 3 * heads_width :]).astype(low),
-        [stream_two, norm_gains[3:4]], ways, rows, 4, 0, late_group, 4, "edge_three",
+        [stream_two, norm_gains[3:4]], ways, rows, 4, 0, late_group, 4, "edge_three", loads=[late_pull],
     )
 
     late_mat = late_weights.reshape(width, -1)
@@ -1281,10 +1483,9 @@
         _, unit_back = jax.vjp(gated_unit, both[:, :units], both[:, units:])
         both_low = jnp.concatenate(unit_back(grad_hidden), axis=1).astype(low)
         grad_normed = project_t(both_low, mat[:, : 2 * units]).astype(low)
-        joint = jnp.concatenate([outer_rows(normed, both_low), outer_rows(grad_low, hidden)], axis=1)
-        return grad_normed, joint.astype(low).reshape(spots, -1, 3 * units)
-
-    grad_fourth, late_joint = ffn_back(last_grad, fourth_low, late_both, late_hidden, late_mat)
+        return grad_normed, [by_spot(outer_rows(normed, both_low)), by_spot(outer_rows(grad_low, hidden))]
+
+    grad_fourth, late_joints = ffn_back(last_grad, fourth_low, late_both, late_hidden, late_mat)
     grad_zero = lax.dynamic_slice_in_dim(output_grad, depth * share, share, 0).astype(jnp.float32)
     grad_low_three, grad_three, gain_four, output_part = edge(
         "backward", grad_fourth, [stream_three, norm_gains[3:4], grad_zero, late_part],
@@ -1295,19 +1496,19 @@
     joint_grad = attend_back(joint_low, grad_attended, down, side, rows)
     grad_low_two, grad_two, gain_three, late_swapped = edge(
         "backward", project_t(joint_grad, focus_mat[:, : 3 * heads_width]).astype(low),
-        [stream_two, norm_gains[2:3], grad_three], ways, rows, 4, 0, early_group, 6, "edge_five", carried=late_joint,
-    )
-    focus_joint = jnp.concatenate(
-        [outer_rows(third_low, joint_grad), outer_rows(grad_low_three, attended_low)], axis=1
-    ).astype(low)
-    focus_joint = focus_joint.reshape(spots, -1, 4 * heads_width)
-
-    grad_second, early_joint = ffn_back(grad_low_two, second_low, early_both, early_hidden, early_mat)
+        [stream_two, norm_gains[2:3], grad_three], ways, rows, 4, 0, early_group, 6, "edge_five",
+        loads=[spread_load(late_joints, late_joints[1].shape[2], 0)],
+    )
+    focus_joints = [by_spot(outer_rows(third_low, joint_grad)), by_spot(outer_rows(grad_low_three, attended_low))]
+
+    grad_second, early_joints = ffn_back(grad_low_two, second_low, early_both, early_hidden, early_mat)
     grad_low_one, grad_one, gain_two, focus_swapped = edge(
         "backward", grad_second, [stream_one, norm_gains[1:2], grad_two],
-        ways, rows, 4, early_group, 0, 7, "edge_six", carried=focus_joint,
-    )
-    early_swapped = swap(after(early_joint, grad_low_one))
+        ways, rows, 4, early_group, 0, 7, "edge_six",
+        loads=[chip_load(focus_joints, heads_width, 1)],
+    )
+    early_joints = [in_order(one) for one in early_joints]
+    early_swapped = swap(after(in_order(jnp.concatenate(early_joints, axis=2)), grad_low_one))
 
     grad_scanned = project(grad_low_one, out_mat)
     (
@@ -1330,7 +1531,7 @@
     gate_joint = outer_rows(first_low, gate_low).astype(low).reshape(spots, -1, channels)
     grad_rows, gate_swapped = mixed_sum(
         jnp.concatenate([grad_rank, jnp.sum(in_sums, axis=-1), jnp.sum(out_sums, axis=-1)], axis=1), 8, "mix_grad_sum",
-        gate_joint,
+        [chip_load([gate_joint], channels, 0)],
     )
     grad_rows_low = grad_rows.astype(low)
     rows_joint = jnp.concatenate(
@@ -1347,43 +1548,39 @@
     conv_joint = outer_rows(first_low, conv_low).astype(low).reshape(spots, -1, channels)
     in_grad = jnp.concatenate([conv_low, gate_low], axis=1)
     grad_first = project_t(in_grad, in_mat).astype(low)
-    mixer_joint = jnp.concatenate([conv_joint, rows_joint.reshape(spots, -1, channels)], axis=1)
-    mixer_joint = jnp.pad(mixer_joint, ((0, 0), (0, -mixer_joint.shape[1] % 16), (0, 0)))
+    rows_joint = rows_joint.reshape(spots, -1, channels)
+    rows_joint = jnp.pad(rows_joint, ((0, 0), (0, -own_rows % 16), (0, 0)))
     lines = jnp.concatenate([taps_grad.T, offset_grad[None], bias_grad, skip_grad, decay_grad], axis=0)
     lines = jnp.pad(lines, ((0, 1), (0, 0)))
     blank = jnp.zeros_like(lines)
     lines = jnp.where(core == 0, jnp.concatenate([lines, blank], axis=1), jnp.concatenate([blank, lines], axis=1))
     gains = jnp.concatenate([jnp.zeros_like(gain_two), gain_two, gain_three, gain_four], axis=0)
     small = jnp.concatenate([lines, gains.reshape(8, -1)], axis=0)
-    input_grad, small, output, mixer_swapped = edge(
+    input_grad, small, output, conv_swapped, rows_swapped = edge(
         "last", grad_first, [stream_zero, norm_gains[0:1], grad_one, small, output_part, stream_three],
-        ways, rows, 4, 0, None, 9, "edge_seven", carried=mixer_joint,
+        ways, rows, 4, 0, None, 9, "edge_seven",
+        loads=[chip_load([conv_joint], channels, 0), chip_load([rows_joint], channels, 0)],
     )
     lines = small[: CONV + 3 + STATE]
     gains = small[-8:].reshape(norm_gains.shape)
-    late_grads = settle(late_swapped, late_group, 3)
-    early_grads = settle(early_swapped, early_group, 3)
-    focus_grads = settle(focus_swapped, focus_group, 4)
-    gate_grad = settle(gate_swapped, 0, 1)[0]
-    mixer_grads = settle(mixer_swapped, 0, 1)[0]
-    in_rows = mixer_in.shape[1]
+    early_gate_up_grad, early_down_grad = spread_out(early_swapped)
     return (
         output,
         input_grad,
         gains,
-        jnp.stack([mixer_grads[:in_rows], gate_grad]),
-        mixer_grads[in_rows : in_rows + mixer_rows.shape[0]],
+        jnp.stack([chip_total(conv_swapped[:, 0]), chip_total(gate_swapped[:, 0])]),
+        chip_total(rows_swapped[:, 0, :own_rows]),
         lines[:CONV].T,
         lines[CONV],
         lines[CONV + 1],
         lines[CONV + 3 :].T,
         lines[CONV + 2],
-        jnp.stack(early_grads[:2]),
-        early_grads[2],
-        jnp.stack(focus_grads[:3]),
-        focus_grads[3],
-        jnp.stack(late_grads[:2]),
-        late_grads[2],
+        early_gate_up_grad,
+        early_down_grad,
+        chip_total(focus_swapped[:, :3]),
+        chip_total(focus_swapped[:, 3]),
+        late_swapped[:2].astype(jnp.float32),
+        late_swapped[2].astype(jnp.float32),
     )
 
 

time: 785 us -> 716 us (0.912)
  Pallas kernels: 484 us -> 553 us
  waiting for transfers between devices: 48.4 us -> 0.01 us
  other arithmetic: 62.1 us -> 33.5 us
  starting transfers between devices: 37.1 us -> 10.1 us
  local copies, waits for them, and re-layouts: 58.2 us -> 37.5 us
  matrix products: 85 us -> 73.9 us
    pallas_call x10 -> x11, Pallas kernels: 452 us -> 520 us  [the longest x9 454 us: edge(): pl.pallas_call(partial(edge_kernel, kind, extra, loads, ways, rows, parts...]
    all_to_all x6 -> x2, waiting for transfers between devices: 48.4 us -> 0.01 us  [swap(): return lax.all_to_all(stacked, 'dp', 0, 0, tiled=True)]
    all_to_all x6 -> x2, starting transfers between devices: 36.9 us -> 10 us  [swap(): return lax.all_to_all(stacked, 'dp', 0, 0, tiled=True)]
    unnamed x271 -> x170, local copies, waits for them, and re-layouts: 34.5 us -> 10.2 us
    unnamed x28 -> x7, other arithmetic: 14.6 us -> 0.2 us
    reduce_sum x0 -> x5, other arithmetic: none -> 10.9 us  [chip_total(): return jnp.sum(came.astype(jnp.float32), axis=0)]
    concatenate x6 -> x1, other arithmetic: 12.4 us -> 1.86 us  [grouped_body(): jnp.concatenate(early_joints, axis=2)]
  transfers between devices with their start and end apart: 7 -> 3, of which waited for: 2 -> 0; matrix products, arithmetic and copies ran while one was open for 11% -> 6% of each run, Pallas kernels for 27% -> 21%
where the time goes in v3:
time: 716 us; the launch traced here: 710 us
  Pallas kernels  553 us (77%)
  matrix products  73.9 us (10%)
  local copies, waits for them, and re-layouts  37.5 us (5%)
  other arithmetic  33.5 us (5%)
  starting transfers between devices  10.1 us (1%)
    pallas_call x9, Pallas kernels, edge(): pl.pallas_call(partial(edge_kernel, kind, extra, loads, ways, rows, parts...  454 us
    pallas_call x1, Pallas kernels, opening(): pl.pallas_call(partial(opening_kernel, ways, rows), in_specs=[vmem] * 2 +...  58.8 us
    dot_general x10, matrix products, project(): return jnp.dot(left, right, preferred_element_type=jnp.float32)  30.7 us
    dot_general x10, matrix products, project_t(): lax.dot_general(left, right, (((1,), (1,)), ((), ())), preferred_element_...  27 us
    pallas_call x1, Pallas kernels, scan_backward(): pl.pallas_call(partial(scan_backward_kernel, groups, tokens // groups), g...  21.1 us
    dot_general x11, matrix products, outer_rows(): lax.dot_general(left, right, (((0,), (0,)), ((), ())), preferred_element_...  16.2 us
  transfers between devices with their start and end apart: 3, of which 0 were waited for; matrix products, arithmetic and copies ran while one was open for 6% of the time, Pallas kernels for 21%

profile of v3, /device:TPU:1, one launch (start us, length us, event | category | flops | bytes accessed | tf_op | source)
XLA Modules:
  0.0 710.1 jit_solution(18037123468411658371)
XLA Ops:
  6.2 58.8 %opening.1 = (bf16[256,2048]{1,0:T(8,128)(2,1)S(1)}, bf16[8,256,1024]{2,1,0:T(8,128)(2,1)S(1)}, bf16[8,304,512]{2,1,0:T(8,128)(2,1)S(1)}) custom-call(bf16[128,2048]{1,0:T(8,128)(2,1)S(1)} %copy-done.18, f32[1,2048]{1,0:T(1,128)S(1)} %get-tuple-element.172.gain_ref.refs_2_, bf16[2,256,1024]{2,1,0:T(8,128)(2,1)S(1)} %copy-done.14, ...), custom_call_target="tpu_custom_call" | custom-call | flops 1 | bytes 1 | tf_op jit(solution)/shard_map/opening/pallas_call | solution.py:1191
  65.0 2.0 copy-done.33
  67.0 5.3 all-to-all-start
  74.1 3.4 fusion.66
  85.8 4.2 reshape.217
  92.4 2.8 multiply_convert_fusion.4
  95.5 15.1 %mix_sum.1 = f32[256,256]{1,0:T(8,128)S(1)} custom-call(f32[256,256]{1,0:T(8,128)S(1)} %pad.48.refs_0_), custom_call_target="tpu_custom_call" | custom-call | flops 1 | bytes 1 | tf_op jit(solution)/shard_map/mix_sum/pallas_call | solution.py:1096
  112.4 8.4 %scan_forward.1 = bf16[256,512]{1,0:T(8,128)(2,1)S(1)} custom-call(f32[256]{0:T(256)S(1)} %subtract_bitcast_fusion.keep_ref, bf16[256,512]{1,0:T(8,128)(2,1)S(1)} %get-tuple-element.126.chan_ref, f32[256,512]{1,0:T(8,128)S(1)} %fusion.51.raw_ref, f32[256,512]{1,0:T(8,128)S(1)} %get-tuple-element.159.gate_ref, f32[1,512]{1,0:T(1,128)S(1)} %bitcast.128, ...), custom_call_target="tpu_custom_call" | custom-call | flops 1 | bytes 17179869184 | tf_op jit(solution)/shard_map/scan_forward/pallas_call | solution.py:120
  122.0 48.8 %edge_one.1 = (bf16[1024,2048]{1,0:T(8,128)(2,1)}, f32[32,2048]{1,0:T(8,128)S(1)}, bf16[8,256,1024]{2,1,0:T(8,128)(2,1)}) custom-call(bf16[256,2048]{1,0:T(8,128)(2,1)S(1)} %convolution_convert_fusion.10.refs_0_, f32[32,2048]{1,0:T(8,128)S(1)} %get-tuple-element.191.refs_1_, f32[1,2048]{1,0:T(1,128)S(1)} %get-tuple-element.171.refs_2_, ...), custom_call_target="tpu_custom_call" | custom-call | flops 1 | bytes 1 | tf_op jit(solution)/shard_map/edge_one/pallas_call | solution.py:1096
  171.0 5.2 fusion.11
  176.6 5.0 convolution_convert_fusion.3.refs_0_
  181.5 58.9 %edge_two.1 = (bf16[256,2048]{1,0:T(8,128)(2,1)S(1)}, f32[32,2048]{1,0:T(8,128)S(1)}, bf16[1024,2048]{1,0:T(8,128)(2,1)}, bf16[8,256,1024]{2,1,0:T(8,128)(2,1)}) custom-call(bf16[1024,2048]{1,0:T(8,128)(2,1)} %convolution_convert_fusion.3.refs_0_, f32[32,2048]{1,0:T(8,128)S(1)} %get-tuple-element.72.refs_1_, ...), custom_call_target="tpu_custom_call", output_to_operand_aliasing={{3}: (4, {})} | custom-call | flops 1 | bytes 1 | tf_op jit(solution)/shard_map/edge_two/pallas_call | solution.py:1096
  240.4 2.9 fusion.2.joint_ref
  246.5 58.6 %edge_three.1 = (bf16[1024,2048]{1,0:T(8,128)(2,1)}, f32[32,2048]{1,0:T(8,128)S(1)}, bf16[8,256,768]{2,1,0:T(8,128)(2,1)}) custom-call(bf16[256,2048]{1,0:T(8,128)(2,1)S(1)} %convolution_convert_fusion.15.refs_0_, f32[32,2048]{1,0:T(8,128)S(1)} %get-tuple-element.79.refs_1_, f32[1,2048]{1,0:T(1,128)S(1)} %get-tuple-element.170.refs_2_, ...), custom_call_target="tpu_custom_call" | custom-call | flops 1 | bytes 1 | tf_op jit(solution)/shard_map/edge_three/pallas_call | solution.py:1096
  305.2 5.6 fusion.8
  313.0 2.5 convolution_convert_fusion.9
  315.5 4.4 convolution_convert_fusion.2.refs_0_
  321.3 3.3 convolution_convert_fusion.1.refs_4_
  324.6 50.9 %edge_four.1 = (bf16[256,2048]{1,0:T(8,128)(2,1)S(1)}, f32[32,2048]{1,0:T(8,128)S(1)}, f32[1,2048]{1,0:T(1,128)S(1)}, bf16[128,2048]{1,0:T(8,128)(2,1)S(1)}) custom-call(bf16[1024,2048]{1,0:T(8,128)(2,1)} %convolution_convert_fusion.2.refs_0_, f32[32,2048]{1,0:T(8,128)S(1)} %get-tuple-element.82.refs_1_.refs_6_, f32[1,2048]{1,0:T(1,128)S(1)} %get-tuple-element.170.refs_2_, ...), custom_call_target="tpu_custom_call" | custom-call | flops 1 | bytes 1 | tf_op jit(solution)/shard_map/edge_four/pallas_call | solution.py:1096
  375.6 1.9 fusion.27.grad_ref
  378.0 1.9 attend_back.1
  382.1 60.6 %edge_five.1 = (bf16[1024,2048]{1,0:T(8,128)(2,1)}, f32[32,2048]{1,0:T(8,128)S(1)}, f32[1,2048]{1,0:T(1,128)S(1)}, bf16[3,256,2048]{2,1,0:T(8,128)(2,1)}) custom-call(bf16[256,2048]{1,0:T(8,128)(2,1)S(1)} %fusion.4.refs_0_, f32[32,2048]{1,0:T(8,128)S(1)} %get-tuple-element.79.refs_1_, f32[1,2048]{1,0:T(1,128)S(1)} %copy-done.29, ...), custom_call_target="tpu_custom_call" | custom-call | flops 1 | bytes 1 | tf_op jit(solution)/shard_map/edge_five/pallas_call | solution.py:1096
  442.7 4.8 fusion.21
  447.5 2.5 convolution_convert_fusion.8
  450.0 6.3 convolution_convert_fusion.refs_0_
  457.8 1.9 pad_maximum_fusion
  459.6 71.8 %edge_six.1 = (bf16[256,2048]{1,0:T(8,128)(2,1)S(1)}, f32[32,2048]{1,0:T(8,128)S(1)}, f32[1,2048]{1,0:T(1,128)S(1)}, bf16[4,4,256,512]{3,2,1,0:T(8,128)(2,1)}) custom-call(bf16[1024,2048]{1,0:T(8,128)(2,1)} %convolution_convert_fusion.refs_0_, f32[32,2048]{1,0:T(8,128)S(1)} %get-tuple-element.72.refs_1_, f32[1,2048]{1,0:T(1,128)S(1)} %get-tuple-element.171.refs_2_, ...), custom_call_target="tpu_custom_call" | custom-call | flops 1 | bytes 1 | tf_op jit(solution)/shard_map/edge_six/pallas_call | solution.py:1096
  532.1 4.7 all-to-all-start.1
  536.9 3.1 fusion.13.dmix_ref
  540.0 21.1 %scan_backward.1 = (f32[256,512]{1,0:T(8,128)}, bf16[256,512]{1,0:T(8,128)(2,1)}, bf16[256,512]{1,0:T(8,128)(2,1)}, f32[256,16,128]{2,1,0:T(8,128)}, f32[256,16,...) custom-call(f32[256]{0:T(256)} %copy-done.32, bf16[256,512]{1,0:T(8,128)(2,1)} %copy-done.2, ...), custom_call_target="tpu_custom_call" | custom-call | flops 1 | bytes 17179869184 | tf_op jit(solution)/shard_map/scan_backward/pallas_call | solution.py:230
  561.8 2.2 convert_reduce_fusion.4
  564.0 3.7 convert_reduce_fusion
  567.7 2.1 convolution_convert_fusion.5
  573.2 2.5 slice_convert_fusion
  575.7 1.8 convolution_convert_fusion.17
  577.5 1.9 fusion.49
  579.4 2.2 reduce_sum.114
  581.6 2.9 reduce_sum.118
  585.8 27.2 %mix_grad_sum.1 = (f32[256,256]{1,0:T(8,128)S(1)}, bf16[4,1,256,1024]{3,2,1,0:T(8,128)(2,1)S(1)}) custom-call(f32[256,256]{1,0:T(8,128)S(1)} %select_maximum_fusion.refs_0_, bf16[8,256,512]{2,1,0:T(8,128)(2,1)S(1)} %bitcast.123), custom_call_target="tpu_custom_call" | custom-call | flops 1 | bytes 1 | tf_op jit(solution)/shard_map/mix_grad_sum/pallas_call | solution.py:1096
  613.4 1.8 multiply_reduce_fusion.3
  617.4 2.3 convolution_convert_fusion.11.refs_0_
  619.7 2.1 convolution_convert_fusion.6
  621.9 2.1 convert_element_type.159
  624.1 3.5 pad.58.refs_8_
  628.2 62.7 %edge_seven.1 = (f32[128,2048]{1,0:T(8,128)S(1)}, f32[32,1024]{1,0:T(8,128)S(1)}, f32[128,2048]{1,0:T(8,128)S(1)}, bf16[4,1,256,1024]{3,2,1,0:T(8,128)(2,1)}, bf16[4,1,304,1024]{3,2,1,0:T(8,128)(2,1)}) custom-call(bf16[256,2048]{1,0:T(8,128)(2,1)S(1)} %copy-done.17, f32[32,2048]{1,0:T(8,128)S(1)} %copy-done.7, f32[1,2048]{1,0:T(1,128)S(1)} %copy-done.28, ...), custom_call_target="tpu_custom_call" | custom-call | flops 1 | bytes 1 | tf_op jit(solution)/shard_map/edge_seven/pallas_call | solution.py:1096
  693.8 3.2 convert_reduce_fusion.3
  698.5 6.7 spread_out.1
  705.2 2.7 pad_maximum_fusion.2
  (249 shorter events, 47.5 us)
Async XLA Ops:
  0.7 90.5 %collective-permute-start = (s32[2,4]{1,0:T(2,128)}, s32[2,4]{1,0:T(2,128)}, u32[]{:S(2)}, u32[]{:S(2)}) collective-permute-start(s32[2,4]{1,0:T(2,128)} %param.18), channel_id=1, source_target_pairs={{0,4},{4,0},{8,12},{12,8},{16,20},{20,16},{24,28},{28,24},{1,5},{5... | collective-permute-start | bytes 104 | tf_op jit(solution)/shard_map/ppermute | solution.py:1377
  67.0 103.9 %all-to-all-start = ((bf16[8,256,768]{2,1,0:T(8,128)(2,1)}), bf16[8,256,768]{2,1,0:T(8,128)(2,1)}, u32[]{:S(2)}, u32[]{:S(2)}) async-start(bf16[8,256,768]{2,1,0:T(8,128)(2,1)} %copy-done.44), calls=%async_computation | async-start | bytes 6291456 | tf_op jit(solution)/shard_map/all_to_all | solution.py:1308
  85.8 4.2 copy-start.19
  85.8 5.2 copy-start.75
  85.8 6.1 copy-start.78
  85.8 6.4 copy-start.74
  85.8 6.5 copy-start.39
  85.8 6.5 copy-start.41
  85.8 6.5 copy-start.73
  90.0 5.4 copy-start.79
  91.0 30.6 %copy-start.6 = (f32[32,2048]{1,0:T(8,128)}, f32[32,2048]{1,0:T(8,128)S(1)}, u32[]{:S(2)}) copy-start(f32[32,2048]{1,0:T(8,128)S(1)} %get-tuple-element.191.refs_1_) | copy-start | bytes 786436
  91.1 19.9 %copy-start.59 = (f32[512,1]{0,1:T(1,128)}, f32[512,1]{0,1:T(1,128)S(1)}, u32[]{:S(2)}) copy-start(f32[512,1]{0,1:T(1,128)S(1)} %get-tuple-element.174) | copy-start | bytes 6148
  91.1 19.9 %copy-start.61 = (f32[512,1]{0,1:T(1,128)}, f32[512,1]{0,1:T(1,128)S(1)}, u32[]{:S(2)}) copy-start(f32[512,1]{0,1:T(1,128)S(1)} %get-tuple-element.175) | copy-start | bytes 6148
  91.1 19.9 %copy-start.63 = (f32[512,1]{0,1:T(1,128)}, f32[512,1]{0,1:T(1,128)S(1)}, u32[]{:S(2)}) copy-start(f32[512,1]{0,1:T(1,128)S(1)} %get-tuple-element.176) | copy-start | bytes 6148
  91.1 19.9 %copy-start.65 = (f32[512,1]{0,1:T(1,128)}, f32[512,1]{0,1:T(1,128)S(1)}, u32[]{:S(2)}) copy-start(f32[512,1]{0,1:T(1,128)S(1)} %get-tuple-element.177) | copy-start | bytes 6148
  95.1 17.2 %copy-start.2 = (bf16[256,512]{1,0:T(8,128)(2,1)}, bf16[256,512]{1,0:T(8,128)(2,1)S(1)}, u32[]{:S(2)}) copy-start(bf16[256,512]{1,0:T(8,128)(2,1)S(1)} %get-tuple-element.126.chan_ref) | copy-start | bytes 786436
  95.2 17.2 %copy-start.4 = (f32[256,512]{1,0:T(8,128)}, f32[256,512]{1,0:T(8,128)S(1)}, u32[]{:S(2)}) copy-start(f32[256,512]{1,0:T(8,128)S(1)} %get-tuple-element.159.gate_ref) | copy-start | bytes 1572868
  95.5 16.8 %copy-start.31 = (f32[512]{0:T(512)}, f32[512]{0:T(512)S(1)}, u32[]{:S(2)}) copy-start(f32[512]{0:T(512)S(1)} %dynamic_slice.25) | copy-start | bytes 6148
  95.5 16.8 %copy-start.23 = (f32[16,512]{1,0:T(8,128)S(1)}, f32[16,512]{1,0:T(8,128)}, u32[]{:S(2)}) copy-start(f32[16,512]{1,0:T(8,128)} %negate_bitcast_fusion.rate_ref) | copy-start | bytes 98308
  95.5 16.8 %copy-start.30 = (f32[512]{0:T(512)S(1)}, f32[512]{0:T(512)}, u32[]{:S(2)}) copy-start(f32[512]{0:T(512)} %dynamic_slice.23) | copy-start | bytes 6148
  110.7 10.0 %copy-start.32 = (f32[256]{0:T(256)}, f32[256]{0:T(256)S(1)}, u32[]{:S(2)}) copy-start(f32[256]{0:T(256)S(1)} %subtract_bitcast_fusion.keep_ref) | copy-start | bytes 3076
  111.1 9.7 %copy-start.5 = (f32[256,512]{1,0:T(8,128)}, f32[256,512]{1,0:T(8,128)S(1)}, u32[]{:S(2)}) copy-start(f32[256,512]{1,0:T(8,128)S(1)} %fusion.51.raw_ref) | copy-start | bytes 1572868
  111.7 9.1 %copy-start = (f32[256,16,128]{2,1,0:T(8,128)}, f32[256,16,128]{2,1,0:T(8,128)S(1)}, u32[]{:S(2)}) copy-start(f32[256,16,128]{2,1,0:T(8,128)S(1)} %broadcast_in_dim.21.out_ref) | copy-start | bytes 6291460
  112.3 9.2 %copy-start.1 = (f32[256,16,128]{2,1,0:T(8,128)}, f32[256,16,128]{2,1,0:T(8,128)S(1)}, u32[]{:S(2)}) copy-start(f32[256,16,128]{2,1,0:T(8,128)S(1)} %broadcast_in_dim.20.in_ref) | copy-start | bytes 6291460
  176.2 5.3 copy-start.48
  176.5 5.0 copy-start.29
  305.1 19.5 %copy-start.12 = (f32[32,2048]{1,0:T(8,128)}, f32[32,2048]{1,0:T(8,128)S(1)}, u32[]{:S(2)}) copy-start(f32[32,2048]{1,0:T(8,128)S(1)} %get-tuple-element.82.refs_1_.refs_6_) | copy-start | bytes 786436
  305.2 5.6 copy-start.54
  305.2 5.6 copy-start.81
  375.6 5.5 copy-start.21
  375.6 4.4 copy-start.38
  442.7 4.9 copy-start.80
  450.0 6.4 copy-start.82
  532.1 43.6 %all-to-all-start.1 = ((bf16[8,256,768]{2,1,0:T(8,128)(2,1)}), bf16[8,256,768]{2,1,0:T(8,128)(2,1)}, u32[]{:S(2)}, u32[]{:S(2)}) async-start(bf16[8,256,768]{2,1,0:T(8,128)(2,1)} %pad_maximum_fusion), calls=%async_computation.1 | async-start | bytes 6291456 | tf_op jit(solution)/shard_map/all_to_all | solution.py:1308
  581.6 31.4 %copy-start.3 = (bf16[256,512]{1,0:T(8,128)(2,1)S(1)}, bf16[256,512]{1,0:T(8,128)(2,1)}, u32[]{:S(2)}) copy-start(bf16[256,512]{1,0:T(8,128)(2,1)} %copy-done.2) | copy-start | bytes 786436
  584.6 28.7 %copy-start.40 = (f32[253,512]{1,0:T(8,128)S(1)}, f32[253,512]{1,0:T(8,128)}, u32[]{:S(2)}) copy-start(f32[253,512]{1,0:T(8,128)} %slice.316) | copy-start | bytes 1554436
  584.6 28.7 %copy-start.42 = (f32[254,512]{1,0:T(8,128)S(1)}, f32[254,512]{1,0:T(8,128)}, u32[]{:S(2)}) copy-start(f32[254,512]{1,0:T(8,128)} %slice.315) | copy-start | bytes 1560580
  584.6 28.7 %copy-start.43 = (f32[255,512]{1,0:T(8,128)S(1)}, f32[255,512]{1,0:T(8,128)}, u32[]{:S(2)}) copy-start(f32[255,512]{1,0:T(8,128)} %slice.314) | copy-start | bytes 1566724
  584.6 28.7 %copy-start.50 = (f32[256,512]{1,0:T(8,128)S(1)}, f32[256,512]{1,0:T(8,128)}, u32[]{:S(2)}) copy-start(f32[256,512]{1,0:T(8,128)} %get-tuple-element.127) | copy-start | bytes 1572868
  584.6 28.7 %copy-start.53 = (f32[256,512]{1,0:T(8,128)S(1)}, f32[256,512]{1,0:T(8,128)}, u32[]{:S(2)}) copy-start(f32[256,512]{1,0:T(8,128)} %get-tuple-element.93) | copy-start | bytes 1572868
  584.6 28.7 %copy-start.68 = (f32[256]{0:T(256)S(1)}, f32[256]{0:T(256)}, u32[]{:S(2)}) copy-start(f32[256]{0:T(256)} %copy-done.67) | copy-start | bytes 3076
  584.6 28.7 %copy-start.70 = (f32[256]{0:T(256)S(1)}, f32[256]{0:T(256)}, u32[]{:S(2)}) copy-start(f32[256]{0:T(256)} %copy-done.69) | copy-start | bytes 3076
  584.6 28.7 %copy-start.72 = (f32[256]{0:T(256)S(1)}, f32[256]{0:T(256)}, u32[]{:S(2)}) copy-start(f32[256]{0:T(256)} %copy-done.71) | copy-start | bytes 3076
  624.0 4.1 copy-start.7
  624.0 4.1 copy-start.13
  624.1 4.1 copy-start.17
  628.2 64.6 %copy-start.9 = (bf16[4,1,256,1024]{3,2,1,0:T(8,128)(2,1)S(1)}, bf16[4,1,256,1024]{3,2,1,0:T(8,128)(2,1)}, u32[]{:S(2)}) copy-start(bf16[4,1,256,1024]{3,2,1,0:T(8,128)(2,1)} %copy-done.8) | copy-start | bytes 6291460
  698.5 9.4 %copy-start.16 = (f32[128,2048]{1,0:T(8,128)S(1)}, f32[128,2048]{1,0:T(8,128)}, u32[]{:S(2)}) copy-start(f32[128,2048]{1,0:T(8,128)} %copy-done.15) | copy-start | bytes 3145732
  (39 other events, 99.1 us)

commit v4 on v3

--- a/solution.py
+++ b/solution.py
@@ -1277,6 +1277,101 @@
     )(low, grad, down, side)
 
 
+def conv_total(stream, age_ref, taps_ref, offset_ref):
+    moved = [stream] + [
+        jnp.where(age_ref[...] >= lag, pltpu.roll(stream, lag, 0), 0.0) for lag in range(1, CONV)
+    ]
+    total = offset_ref[...]
+    for lag in range(CONV):
+        total = total + moved[lag] * taps_ref[lag : lag + 1, :]
+    return total, moved
+
+
+def front_kernel(first_ref, conv_mat_ref, gate_mat_ref, age_ref, taps_ref, offset_ref, select_ref, conv_ref, gate_ref,
+                 channel_ref, mix_ref):
+    stream = project(first_ref[...], conv_mat_ref[...])
+    conv_ref[...] = stream
+    gate_ref[...] = project(first_ref[...], gate_mat_ref[...])
+    total, _ = conv_total(stream, age_ref, taps_ref, offset_ref)
+    channel = (total / (1.0 + jnp.exp(-total))).astype(jnp.bfloat16)
+    channel_ref[...] = channel
+
+    @pl.when(pl.program_id(0) == 0)
+    def _():
+        mix_ref[...] = jnp.zeros_like(mix_ref)
+
+    mix_ref[...] += project_t(channel, select_ref[...])
+
+
+def front(first_low, in_mat, age, taps_t, offset, select):
+    count, width = first_low.shape
+    channels = in_mat.shape[1] // 2
+    size = channels // 2
+    column = pl.BlockSpec((count, size), lambda i: (0, i))
+    sheet = jax.ShapeDtypeStruct((count, channels), jnp.float32)
+    return pl.pallas_call(
+        front_kernel,
+        grid=(2,),
+        in_specs=[
+            pl.BlockSpec((count, width), lambda i: (0, 0)),
+            pl.BlockSpec((width, size), lambda i: (0, i)),
+            pl.BlockSpec((width, size), lambda i: (0, i + 2)),
+            pl.BlockSpec((count, 1), lambda i: (0, 0)),
+            pl.BlockSpec((CONV, size), lambda i: (0, i)),
+            pl.BlockSpec((1, size), lambda i: (0, i)),
+            pl.BlockSpec((select.shape[0], size), lambda i: (0, i)),
+        ],
+        out_specs=[column, column, column, pl.BlockSpec((count, select.shape[0]), lambda i: (0, 0))],
+        out_shape=[
+            sheet, sheet, jax.ShapeDtypeStruct((count, channels), jnp.bfloat16),
+            jax.ShapeDtypeStruct((count, select.shape[0]), jnp.float32),
+        ],
+        compiler_params=pltpu.CompilerParams(vmem_limit_bytes=40 << 20),
+        name="front",
+    )(first_low, in_mat, in_mat, age, taps_t, offset, select)
+
+
+def front_back_kernel(conv_ref, age_ref, left_ref, taps_ref, offset_ref, scan_ref, mix_ref, select_ref, low_ref, grads_ref):
+    total, moved = conv_total(conv_ref[...], age_ref, taps_ref, offset_ref)
+    sig = 1.0 / (1.0 + jnp.exp(-total))
+    grad = (scan_ref[...] + project(mix_ref[...], select_ref[...])) * (sig * (1.0 + total * (1.0 - sig)))
+    count = grad.shape[0]
+    back = grad * taps_ref[0:1, :]
+    for lag in range(1, CONV):
+        back = back + jnp.where(left_ref[...] >= lag, pltpu.roll(grad, count - lag, 0), 0.0) * taps_ref[lag : lag + 1, :]
+    low_ref[...] = back.astype(jnp.bfloat16)
+    for lag in range(CONV):
+        grads_ref[lag : lag + 1, :] = jnp.sum(grad * moved[lag], axis=0, keepdims=True)
+    grads_ref[CONV : CONV + 1, :] = jnp.sum(grad, axis=0, keepdims=True)
+    grads_ref[CONV + 1 :, :] = jnp.zeros((3, grad.shape[1]), jnp.float32)
+
+
+def front_back(conv_in, age, left, taps_t, offset, grad_scan, grad_mix, select):
+    count, channels = conv_in.shape
+    size = channels // 2
+    column = pl.BlockSpec((count, size), lambda i: (0, i))
+    place = pl.BlockSpec((count, 1), lambda i: (0, 0))
+    return pl.pallas_call(
+        front_back_kernel,
+        grid=(2,),
+        in_specs=[
+            column, place, place,
+            pl.BlockSpec((CONV, size), lambda i: (0, i)),
+            pl.BlockSpec((1, size), lambda i: (0, i)),
+            column,
+            pl.BlockSpec((count, select.shape[0]), lambda i: (0, 0)),
+            pl.BlockSpec((select.shape[0], size), lambda i: (0, i)),
+        ],
+        out_specs=[column, pl.BlockSpec((8, size), lambda i: (0, i))],
+        out_shape=[
+            jax.ShapeDtypeStruct((count, channels), jnp.bfloat16),
+            jax.ShapeDtypeStruct((8, channels), jnp.float32),
+        ],
+        compiler_params=pltpu.CompilerParams(vmem_limit_bytes=40 << 20),
+        name="front_back",
+    )(conv_in, age, left, taps_t, offset, grad_scan, grad_mix, select)
+
+
 def sub_of(spot, group):
     if group == 6:
         return spot
@@ -1308,27 +1403,42 @@
     return lax.all_to_all(stacked, "dp", 0, 0, tiled=True)
 
 
-def spread_out_kernel(came_ref, pair_ref, last_ref):
+def spread_out_kernel(came_ref, pair_ref, last_ref, sum_ref):
     size = last_ref.shape[1]
+    half = came_ref.shape[2] - 3 * size
+    spot = pl.program_id(0)
     for at in range(2):
         pair_ref[at] = came_ref[0, :, at * size : (at + 1) * size].astype(jnp.float32)
-    last_ref[...] = came_ref[0, :, 2 * size :].astype(jnp.float32)
-
-
-def spread_out(came):
-    spots, rows, columns = came.shape
-    size = columns // 3
+    last_ref[...] = came_ref[0, :, 2 * size : 3 * size].astype(jnp.float32)
+    piece = came_ref[0, :, 3 * size :].astype(jnp.float32)
+    for core in range(2):
+        lanes = slice(core * half, (core + 1) * half)
+
+        @pl.when(spot == core)
+        def _():
+            sum_ref[:, lanes] = piece
+
+        @pl.when((spot > 1) & (lax.rem(spot, 2) == core))
+        def _():
+            sum_ref[:, lanes] += piece
+
+
+def spread_out(came, columns):
+    spots, rows, _ = came.shape
+    size, half = columns // 3, came.shape[2] - columns
     return pl.pallas_call(
         spread_out_kernel,
         grid=(spots,),
-        in_specs=[pl.BlockSpec((1, rows, columns), lambda i: (i, 0, 0))],
+        in_specs=[pl.BlockSpec((1, rows, came.shape[2]), lambda i: (i, 0, 0))],
         out_specs=[
             pl.BlockSpec((2, rows, size), lambda i: (0, 0, i)),
             pl.BlockSpec((rows, size), lambda i: (0, i)),
+            pl.BlockSpec((rows, 2 * half), lambda i: (0, 0)),
         ],
         out_shape=[
             jax.ShapeDtypeStruct((2, rows, spots * size), jnp.float32),
             jax.ShapeDtypeStruct((rows, spots * size), jnp.float32),
+            jax.ShapeDtypeStruct((rows, 2 * half), jnp.float32),
         ],
         name="spread_out",
     )(came)
@@ -1391,6 +1501,13 @@
     flat_segs = (segs + jnp.arange(2, dtype=jnp.int32)[:, None] * rows).reshape(-1)
     keeping = 1.0 - starts.reshape(-1).astype(jnp.float32)
     groups = 2 * seq_lengths.shape[0]
+    flat_lengths = lengths.reshape(2, -1)
+    ends = jnp.cumsum(flat_lengths, axis=1) + jnp.arange(2, dtype=jnp.int32)[:, None] * rows
+    firsts = (ends - flat_lengths).reshape(1, -1)
+    ends = ends.reshape(1, -1)
+    places = jnp.arange(2 * rows, dtype=jnp.int32)[:, None]
+    age = places - jnp.max(jnp.where(firsts <= places, firsts, 0), axis=1, keepdims=True)
+    left = jnp.min(jnp.where(ends > places, ends, 2 * rows), axis=1, keepdims=True) - 1 - places
 
     stream_zero = lax.dynamic_slice_in_dim(hidden_in, depth * share, share, 0).astype(jnp.float32)
 
@@ -1401,10 +1518,7 @@
 
     taps, offset, bias, decay, skip = [half(v) for v in (conv_weight, conv_bias, step_bias, decay_log, skip_gain)]
     in_mat = in_weights.reshape(width, 2 * channels)
-    both = project(first_low, in_mat)
-    conv_in, gate_half = both[:, :channels], both[:, channels:]
-    channel_full, conv_back = jax.vjp(partial(causal_conv, flat_segs), conv_in, taps, offset)
-    channel_low = channel_full.astype(low)
+    taps_t = taps.T
     row_mat = row_weights.reshape(-1, channels)
     early_blocks = [early_gate_up[0], early_gate_up[1], early_down]
     early_weights = swap(after(pull(spots, (early_blocks, early_group)), first_low))
@@ -1427,11 +1541,12 @@
         return joint.astype(low).reshape(spots, -1, joint.shape[1])
 
     def mixed_sum(part, ident, name, loads=()):
-        padded = jnp.pad(part, ((0, 0), (0, 256 - PROJ_OUT)))
-        total, *came = edge("sum", padded, [], ways, rows, 1, 0, 0, ident, name, loads=loads)
+        total, *came = edge("sum", part, [], ways, rows, 1, 0, 0, ident, name, loads=loads)
         return total[:, :PROJ_OUT], *came
 
-    mix_rows, = mixed_sum(project_t(channel_low, select_mat), 1, "mix_sum")
+    wide_select = jnp.pad(select_mat, ((0, 256 - PROJ_OUT), (0, 0)))
+    conv_in, gate_half, channel_low, mix_part = front(first_low, in_mat, age, taps_t, offset[None], wide_select)
+    mix_rows, = mixed_sum(mix_part, 1, "mix_sum")
     rank_low = mix_rows[:, :DT_RANK].astype(low)
     step_raw = project(rank_low, step_mat)
     rates_t = -jnp.exp(decay).T
@@ -1487,9 +1602,10 @@
 
     grad_fourth, late_joints = ffn_back(last_grad, fourth_low, late_both, late_hidden, late_mat)
     grad_zero = lax.dynamic_slice_in_dim(output_grad, depth * share, share, 0).astype(jnp.float32)
-    grad_low_three, grad_three, gain_four, output_part = edge(
+    grad_low_three, grad_three, gain_four, output_part, late_down_swapped = edge(
         "backward", grad_fourth, [stream_three, norm_gains[3:4], grad_zero, late_part],
         ways, rows, 4, late_group, 0, 5, "edge_four", "reduce",
+        [spread_load(late_joints[1:], late_joints[1].shape[2], 1)],
     )
 
     grad_attended = project(grad_low_three, focus_mat[:, 3 * heads_width :])
@@ -1497,7 +1613,7 @@
     grad_low_two, grad_two, gain_three, late_swapped = edge(
         "backward", project_t(joint_grad, focus_mat[:, : 3 * heads_width]).astype(low),
         [stream_two, norm_gains[2:3], grad_three], ways, rows, 4, 0, early_group, 6, "edge_five",
-        loads=[spread_load(late_joints, late_joints[1].shape[2], 0)],
+        loads=[spread_load(late_joints[:1], late_joints[1].shape[2], 0)],
     )
     focus_joints = [by_spot(outer_rows(third_low, joint_grad)), by_spot(outer_rows(grad_low_three, attended_low))]
 
@@ -1505,9 +1621,9 @@
     grad_low_one, grad_one, gain_two, focus_swapped = edge(
         "backward", grad_second, [stream_one, norm_gains[1:2], grad_two],
         ways, rows, 4, early_group, 0, 7, "edge_six",
-        loads=[chip_load(focus_joints, heads_width, 1)],
-    )
-    early_joints = [in_order(one) for one in early_joints]
+        loads=[chip_load(focus_joints[:1], heads_width, 1)],
+    )
+    early_joints = [in_order(one) for one in early_joints + focus_joints[1:]]
     early_swapped = swap(after(in_order(jnp.concatenate(early_joints, axis=2)), grad_low_one))
 
     grad_scanned = project(grad_low_one, out_mat)
@@ -1524,13 +1640,17 @@
         keeping, channel_low, step_raw, gate_half, grad_scanned, bias, rates_t, skip, in_wide, out_wide,
         groups, LANES,
     )
-    grad_channel, grad_step_low, in_sums, out_sums, early_swapped = lax.optimization_barrier(
-        (grad_channel, grad_step_low, in_sums, out_sums, early_swapped)
-    )
     grad_rank = project_t(grad_step_low, step_mat)
     gate_joint = outer_rows(first_low, gate_low).astype(low).reshape(spots, -1, channels)
+    rest = mix_part[:, PROJ_OUT:]
     grad_rows, gate_swapped = mixed_sum(
-        jnp.concatenate([grad_rank, jnp.sum(in_sums, axis=-1), jnp.sum(out_sums, axis=-1)], axis=1), 8, "mix_grad_sum",
+        after(
+            jnp.concatenate(
+                [grad_rank, jnp.sum(in_sums, axis=-1), jnp.sum(out_sums, axis=-1), jnp.zeros_like(rest)], axis=1
+            ),
+            early_swapped,
+        ),
+        8, "mix_grad_sum",
         [chip_load([gate_joint], channels, 0)],
     )
     grad_rows_low = grad_rows.astype(low)
@@ -1542,15 +1662,16 @@
         ],
         axis=0,
     ).astype(low)
-    grad_channel = grad_channel + project(grad_rows_low, select_mat)
-    grad_conv_in, taps_grad, offset_grad = conv_back(grad_channel)
-    conv_low = grad_conv_in.astype(low)
+    grad_wide_low = jnp.pad(grad_rows_low, ((0, 0), (0, 256 - PROJ_OUT)))
+    conv_low, conv_grads = front_back(
+        conv_in, age, left, taps_t, offset[None], grad_channel, grad_wide_low, wide_select
+    )
     conv_joint = outer_rows(first_low, conv_low).astype(low).reshape(spots, -1, channels)
     in_grad = jnp.concatenate([conv_low, gate_low], axis=1)
     grad_first = project_t(in_grad, in_mat).astype(low)
     rows_joint = rows_joint.reshape(spots, -1, channels)
     rows_joint = jnp.pad(rows_joint, ((0, 0), (0, -own_rows % 16), (0, 0)))
-    lines = jnp.concatenate([taps_grad.T, offset_grad[None], bias_grad, skip_grad, decay_grad], axis=0)
+    lines = jnp.concatenate([conv_grads[: CONV + 1], bias_grad, skip_grad, decay_grad], axis=0)
     lines = jnp.pad(lines, ((0, 1), (0, 0)))
     blank = jnp.zeros_like(lines)
     lines = jnp.where(core == 0, jnp.concatenate([lines, blank], axis=1), jnp.concatenate([blank, lines], axis=1))
@@ -1563,7 +1684,7 @@
     )
     lines = small[: CONV + 3 + STATE]
     gains = small[-8:].reshape(norm_gains.shape)
-    early_gate_up_grad, early_down_grad = spread_out(early_swapped)
+    early_gate_up_grad, early_down_grad, focus_out_grad = spread_out(early_swapped, 3 * early_down.shape[1] // spots)
     return (
         output,
         input_grad,
@@ -1577,10 +1698,10 @@
         lines[CONV + 2],
         early_gate_up_grad,
         early_down_grad,
-        chip_total(focus_swapped[:, :3]),
-        chip_total(focus_swapped[:, 3]),
-        late_swapped[:2].astype(jnp.float32),
-        late_swapped[2].astype(jnp.float32),
+        chip_total(focus_swapped),
+        focus_out_grad,
+        late_swapped.astype(jnp.float32),
+        late_down_swapped[0].astype(jnp.float32),
     )
 
 

time: 716 us -> 703 us (0.982)
  Pallas kernels: 553 us -> 541 us
  local copies, waits for them, and re-layouts: 37.5 us -> 46.5 us
    pallas_call x9, Pallas kernels: 454 us -> 438 us  [edge(): pl.pallas_call(partial(edge_kernel, kind, extra, loads, ways, rows, parts...]
    unnamed x170 -> x176, local copies, waits for them, and re-layouts: 10.2 us -> 20.7 us
    dot_general x10 -> x8, matrix products: 30.7 us -> 24.4 us  [project(): return jnp.dot(left, right, preferred_element_type=jnp.float32)]
    dot_general x10 -> x9, matrix products: 27 us -> 24.5 us  [project_t(): lax.dot_general(left, right, (((1,), (1,)), ((), ())), preferred_element_...]
  transfers between devices with their start and end apart: 3 -> 3, of which waited for: 0 -> 1; matrix products, arithmetic and copies ran while one was open for 6% -> 6% of each run, Pallas kernels for 21% -> 22%
where the time goes in v4:
time: 703 us; the launch traced here: 698 us
  Pallas kernels  541 us (77%)
  matrix products  66.8 us (10%)
  local copies, waits for them, and re-layouts  46.5 us (7%)
  other arithmetic  28.2 us (4%)
  starting transfers between devices  10.5 us (1%)
    pallas_call x9, Pallas kernels, edge(): pl.pallas_call(partial(edge_kernel, kind, extra, loads, ways, rows, parts...  438 us
    pallas_call x1, Pallas kernels, opening(): pl.pallas_call(partial(opening_kernel, ways, rows), in_specs=[vmem] * 2 +...  58.8 us
    dot_general x9, matrix products, project_t(): lax.dot_general(left, right, (((1,), (1,)), ((), ())), preferred_element_...  24.5 us
    dot_general x8, matrix products, project(): return jnp.dot(left, right, preferred_element_type=jnp.float32)  24.4 us
    pallas_call x1, Pallas kernels, scan_backward(): pl.pallas_call(partial(scan_backward_kernel, groups, tokens // groups), g...  21.1 us
    unnamed x176, local copies, waits for them, and re-layouts  20.7 us
    dot_general x11, matrix products, outer_rows(): lax.dot_general(left, right, (((0,), (0,)), ((), ())), preferred_element_...  17.9 us
  transfers between devices with their start and end apart: 3, of which 1 were waited for; matrix products, arithmetic and copies ran while one was open for 6% of the time, Pallas kernels for 22%

profile of v4, /device:TPU:1, one launch (start us, length us, event | category | flops | bytes accessed | tf_op | source)
XLA Modules:
  0.0 697.5 jit_solution(5220455152428042677)
XLA Ops:
  4.6 1.7 copy-done.64
  6.2 58.8 %opening.1 = (bf16[256,2048]{1,0:T(8,128)(2,1)S(1)}, bf16[8,256,1024]{2,1,0:T(8,128)(2,1)S(1)}, bf16[8,304,512]{2,1,0:T(8,128)(2,1)S(1)}) custom-call(bf16[128,2048]{1,0:T(8,128)(2,1)S(1)} %copy-done.35, f32[1,2048]{1,0:T(1,128)S(1)} %get-tuple-element.166.gain_ref.refs_2_, bf16[2,256,1024]{2,1,0:T(8,128)(2,1)S(1)} %copy-done.28, ...), custom_call_target="tpu_custom_call" | custom-call | flops 1 | bytes 1 | tf_op jit(solution)/shard_map/opening/pallas_call | solution.py:1191
  65.0 2.0 copy-done.4
  67.1 5.3 all-to-all-start
  79.0 1.6 slice.196
  80.6 2.7 reshape.228
  84.8 1.8 dynamic-slice_convert_fusion
  88.9 2.2 copy-done.5
  91.1 2.9 front.1
  94.8 15.1 %mix_sum.1 = f32[256,256]{1,0:T(8,128)S(1)} custom-call(f32[256,256]{1,0:T(8,128)S(1)} %get-tuple-element.76.refs_0_), custom_call_target="tpu_custom_call" | custom-call | flops 1 | bytes 1 | tf_op jit(solution)/shard_map/mix_sum/pallas_call | solution.py:1096
  111.7 8.0 %scan_forward.1 = bf16[256,512]{1,0:T(8,128)(2,1)S(1)} custom-call(f32[256]{0:T(256)S(1)} %subtract_bitcast_fusion.keep_ref, bf16[256,512]{1,0:T(8,128)(2,1)S(1)} %get-tuple-element.75.chan_ref, f32[256,512]{1,0:T(8,128)S(1)} %fusion.47.raw_ref, f32[256,512]{1,0:T(8,128)S(1)} %get-tuple-element.77.gate_ref, f32[1,512]{1,0:T(1,128)S(1)} %bitcast.114, ...), custom_call_target="tpu_custom_call" | custom-call | flops 1 | bytes 17179869184 | tf_op jit(solution)/shard_map/scan_forward/pallas_call | solution.py:120
  121.0 48.8 %edge_one.1 = (bf16[1024,2048]{1,0:T(8,128)(2,1)}, f32[32,2048]{1,0:T(8,128)S(1)}, bf16[8,256,1024]{2,1,0:T(8,128)(2,1)}) custom-call(bf16[256,2048]{1,0:T(8,128)(2,1)S(1)} %convolution_convert_fusion.10.refs_0_, f32[32,2048]{1,0:T(8,128)S(1)} %copy-done.12, f32[1,2048]{1,0:T(1,128)S(1)} %copy-done.50, bf16[3,256,512]{2,1,0:T(8,128)(2,1)S(1)} %copy-done.37, ...), custom_call_target="tpu_custom_call" | custom-call | flops 1 | bytes 1 | tf_op jit(solution)/shard_map/edge_one/pallas_call | solution.py:1096
  170.1 5.2 fusion.11
  175.7 5.0 convolution_convert_fusion.3.refs_0_
  180.7 58.9 %edge_two.1 = (bf16[256,2048]{1,0:T(8,128)(2,1)S(1)}, f32[32,2048]{1,0:T(8,128)S(1)}, bf16[1024,2048]{1,0:T(8,128)(2,1)}, bf16[8,256,1024]{2,1,0:T(8,128)(2,1)}) custom-call(bf16[1024,2048]{1,0:T(8,128)(2,1)} %convolution_convert_fusion.3.refs_0_, f32[32,2048]{1,0:T(8,128)S(1)} %get-tuple-element.80.refs_1_, ...), custom_call_target="tpu_custom_call", output_to_operand_aliasing={{3}: (4, {})} | custom-call | flops 1 | bytes 1 | tf_op jit(solution)/shard_map/edge_two/pallas_call | solution.py:1096
  239.7 3.0 fusion.2.joint_ref
  244.7 58.8 %edge_three.1 = (bf16[1024,2048]{1,0:T(8,128)(2,1)}, f32[32,2048]{1,0:T(8,128)S(1)}, bf16[8,256,768]{2,1,0:T(8,128)(2,1)}) custom-call(bf16[256,2048]{1,0:T(8,128)(2,1)S(1)} %convolution_convert_fusion.15.refs_0_, f32[32,2048]{1,0:T(8,128)S(1)} %get-tuple-element.87.refs_1_, f32[1,2048]{1,0:T(1,128)S(1)} %copy-done.55, bf16[2,256,2048]{2,1,0:T(8,128)(2,1)S(1)} %copy-done.20, ...), custom_call_target="tpu_custom_call" | custom-call | flops 1 | bytes 1 | tf_op jit(solution)/shard_map/edge_three/pallas_call | solution.py:1096
  303.5 5.8 fusion.8
  309.4 1.7 fusion.18
  311.5 2.5 convolution_convert_fusion.9
  314.1 4.4 convolution_convert_fusion.2.refs_0_
  319.9 3.4 convolution_convert_fusion.1.refs_4_
  323.2 56.7 %edge_four.1 = (bf16[256,2048]{1,0:T(8,128)(2,1)S(1)}, f32[32,2048]{1,0:T(8,128)S(1)}, f32[1,2048]{1,0:T(1,128)S(1)}, bf16[128,2048]{1,0:T(8,128)(2,1)S(1)}, bf16[1,256,2048]{2,1,0:T(8,128)(2,1)S(1)}) custom-call(bf16[1024,2048]{1,0:T(8,128)(2,1)} %convolution_convert_fusion.2.refs_0_, f32[32,2048]{1,0:T(8,128)S(1)} %get-tuple-element.90.refs_1_.refs_6_, ...), custom_call_target="tpu_custom_call" | custom-call | flops 1 | bytes 1 | tf_op jit(solution)/shard_map/edge_four/pallas_call | solution.py:1096
  381.9 1.9 attend_back.1
  384.8 2.7 convolution_convert_fusion.4
  387.5 47.4 %edge_five.1 = (bf16[1024,2048]{1,0:T(8,128)(2,1)}, f32[32,2048]{1,0:T(8,128)S(1)}, f32[1,2048]{1,0:T(1,128)S(1)}, bf16[2,256,2048]{2,1,0:T(8,128)(2,1)S(1)}) custom-call(bf16[256,2048]{1,0:T(8,128)(2,1)S(1)} %fusion.4.refs_0_, f32[32,2048]{1,0:T(8,128)S(1)} %get-tuple-element.87.refs_1_, f32[1,2048]{1,0:T(1,128)S(1)} %copy-done.54, ...), custom_call_target="tpu_custom_call" | custom-call | flops 1 | bytes 1 | tf_op jit(solution)/shard_map/edge_five/pallas_call | solution.py:1096
  435.0 4.9 fusion.21
  439.9 2.5 convolution_convert_fusion.8
  442.4 6.2 convolution_convert_fusion.refs_0_
  450.0 60.6 %edge_six.1 = (bf16[256,2048]{1,0:T(8,128)(2,1)S(1)}, f32[32,2048]{1,0:T(8,128)S(1)}, f32[1,2048]{1,0:T(1,128)S(1)}, bf16[4,3,256,512]{3,2,1,0:T(8,128)(2,1)S(1)}) custom-call(bf16[1024,2048]{1,0:T(8,128)(2,1)} %convolution_convert_fusion.refs_0_, f32[32,2048]{1,0:T(8,128)S(1)} %copy-done.34, f32[1,2048]{1,0:T(1,128)S(1)} %copy-done.51, ...), custom_call_target="tpu_custom_call" | custom-call | flops 1 | bytes 1 | tf_op jit(solution)/shard_map/edge_six/pallas_call | solution.py:1096
  510.7 2.6 pad_maximum_fusion
  513.6 5.1 all-to-all-start.1
  518.7 3.1 fusion.13.dmix_ref
  521.9 21.1 %scan_backward.1 = (f32[256,512]{1,0:T(8,128)}, bf16[256,512]{1,0:T(8,128)(2,1)}, bf16[256,512]{1,0:T(8,128)(2,1)}, f32[256,16,128]{2,1,0:T(8,128)}, f32[256,16,...) custom-call(f32[256]{0:T(256)} %copy-done.60, bf16[256,512]{1,0:T(8,128)(2,1)} %copy-done.10, ...), custom_call_target="tpu_custom_call" | custom-call | flops 1 | bytes 17179869184 | tf_op jit(solution)/shard_map/scan_backward/pallas_call | solution.py:230
  543.7 2.2 reduce_sum.64
  545.9 2.2 reduce_sum.65
  548.2 4.3 convert_element_type.137
  555.3 1.7 convert_reduce_fusion
  556.9 2.1 convolution_convert_fusion.5
  561.8 2.5 all-to-all-done.1.came_ref
  565.4 28.9 %mix_grad_sum.1 = (f32[256,256]{1,0:T(8,128)S(1)}, bf16[4,1,256,1024]{3,2,1,0:T(8,128)(2,1)S(1)}) custom-call(f32[256,256]{1,0:T(8,128)S(1)} %copy-done.27, bf16[8,256,512]{2,1,0:T(8,128)(2,1)S(1)} %bitcast.106), custom_call_target="tpu_custom_call" | custom-call | flops 1 | bytes 1 | tf_op jit(solution)/shard_map/mix_grad_sum/pallas_call | solution.py:1096
  601.2 2.2 convolution_convert_fusion.11.refs_0_
  603.5 2.1 convolution_convert_fusion.6
  607.4 4.1 convert_element_type.132
  611.6 3.5 pad.26.refs_8_
  615.1 62.7 %edge_seven.1 = (f32[128,2048]{1,0:T(8,128)S(1)}, f32[32,1024]{1,0:T(8,128)S(1)}, f32[128,2048]{1,0:T(8,128)S(1)}, bf16[4,1,256,1024]{3,2,1,0:T(8,128)(2,1)}, bf16[4,1,304,1024]{3,2,1,0:T(8,128)(2,1)}) custom-call(bf16[256,2048]{1,0:T(8,128)(2,1)S(1)} %convolution_convert_fusion.11.refs_0_, f32[32,2048]{1,0:T(8,128)S(1)} %copy-done.12, ...), custom_call_target="tpu_custom_call" | custom-call | flops 1 | bytes 1 | tf_op jit(solution)/shard_map/edge_seven/pallas_call | solution.py:1096
  682.3 2.2 convert_reduce_fusion.3
  687.9 7.5 %spread_out.1 = (f32[2,256,2048]{2,1,0:T(8,128)}, f32[256,2048]{1,0:T(8,128)}, f32[256,512]{1,0:T(8,128)}) custom-call(bf16[8,256,1024]{2,1,0:T(8,128)(2,1)} %all-to-all-done.1.came_ref), custom_call_target="tpu_custom_call" | custom-call | tf_op jit(solution)/shard_map/spread_out/pallas_call | solution.py:1429
  (254 shorter events, 53.0 us)
Async XLA Ops:
  0.6 71.7 %copy-start = (f32[1024,4]{0,1:T(4,128)S(1)}, f32[1024,4]{0,1:T(4,128)}, u32[]{:S(2)}) copy-start(f32[1024,4]{0,1:T(4,128)} %param.22) | copy-start | bytes 49156
  0.7 85.9 %collective-permute-start = (s32[2,4]{1,0:T(2,128)}, s32[2,4]{1,0:T(2,128)}, u32[]{:S(2)}, u32[]{:S(2)}) collective-permute-start(s32[2,4]{1,0:T(2,128)} %param.18), channel_id=1, source_target_pairs={{0,4},{4,0},{8,12},{12,8},{16,20},{20,16},{24,28},{28,24},{1,5},{5... | collective-permute-start | bytes 104 | tf_op jit(solution)/shard_map/ppermute | solution.py:1487
  2.4 3.9 copy-start.52
  67.1 103.1 %all-to-all-start = ((bf16[8,256,768]{2,1,0:T(8,128)(2,1)}), bf16[8,256,768]{2,1,0:T(8,128)(2,1)}, u32[]{:S(2)}, u32[]{:S(2)}) async-start(bf16[8,256,768]{2,1,0:T(8,128)(2,1)} %copy-done.64), calls=%async_computation | async-start | bytes 6291456 | tf_op jit(solution)/shard_map/all_to_all | solution.py:1403
  76.9 12.0 %copy-start.56 = (f32[512]{0:T(512)}, f32[512]{0:T(512)S(1)}, u32[]{:S(2)}) copy-start(f32[512]{0:T(512)S(1)} %dynamic_slice.22) | copy-start | bytes 6148
  77.6 34.0 %copy-start.58 = (f32[512]{0:T(512)}, f32[512]{0:T(512)S(1)}, u32[]{:S(2)}) copy-start(f32[512]{0:T(512)S(1)} %dynamic_slice.23) | copy-start | bytes 6148
  80.6 6.7 copy-start.81
  80.6 7.0 %copy-start.80 = (s32[2]{0:T(128)S(1)}, s32[2]{0:T(128)}, u32[]{:S(2)}) copy-start(s32[2]{0:T(128)} %iota_multiply_fusion) | copy-start | bytes 28
  80.6 8.3 %copy-start.48 = (f32[4,512]{1,0:T(4,128)S(1)}, f32[4,512]{1,0:T(4,128)}, u32[]{:S(2)}) copy-start(f32[4,512]{1,0:T(4,128)} %dynamic-slice_bitcast_fusion.taps_ref) | copy-start | bytes 24580
  84.7 9.3 %copy-start.13 = (bf16[256,512]{1,0:T(8,128)(2,1)}, bf16[256,512]{1,0:T(8,128)(2,1)S(1)}, u32[]{:S(2)}) copy-start(bf16[256,512]{1,0:T(8,128)(2,1)S(1)} %pad.23.select_ref) | copy-start | bytes 786436
  91.1 19.1 %copy-start.66 = (bf16[2336,512]{1,0:T(8,128)(2,1)S(1)}, bf16[2336,512]{1,0:T(8,128)(2,1)}, u32[]{:S(2)}) copy-start(bf16[2336,512]{1,0:T(8,128)(2,1)} %copy-done.65) | copy-start | bytes 7176196
  94.8 16.8 %copy-start.10 = (bf16[256,512]{1,0:T(8,128)(2,1)}, bf16[256,512]{1,0:T(8,128)(2,1)S(1)}, u32[]{:S(2)}) copy-start(bf16[256,512]{1,0:T(8,128)(2,1)S(1)} %get-tuple-element.75.chan_ref) | copy-start | bytes 786436
  94.8 16.8 %copy-start.21 = (f32[256,512]{1,0:T(8,128)}, f32[256,512]{1,0:T(8,128)S(1)}, u32[]{:S(2)}) copy-start(f32[256,512]{1,0:T(8,128)S(1)} %get-tuple-element.77.gate_ref) | copy-start | bytes 1572868
  94.8 16.8 %copy-start.44 = (f32[16,512]{1,0:T(8,128)S(1)}, f32[16,512]{1,0:T(8,128)}, u32[]{:S(2)}) copy-start(f32[16,512]{1,0:T(8,128)} %negate_bitcast_fusion.rate_ref) | copy-start | bytes 98308
  94.8 16.8 %copy-start.59 = (f32[512]{0:T(512)S(1)}, f32[512]{0:T(512)}, u32[]{:S(2)}) copy-start(f32[512]{0:T(512)} %dynamic_slice.25) | copy-start | bytes 6148
  110.4 9.3 %copy-start.7 = (f32[256,512]{1,0:T(8,128)}, f32[256,512]{1,0:T(8,128)S(1)}, u32[]{:S(2)}) copy-start(f32[256,512]{1,0:T(8,128)S(1)} %fusion.47.raw_ref) | copy-start | bytes 1572868
  111.0 8.7 %copy-start.2 = (f32[256,16,128]{2,1,0:T(8,128)}, f32[256,16,128]{2,1,0:T(8,128)S(1)}, u32[]{:S(2)}) copy-start(f32[256,16,128]{2,1,0:T(8,128)S(1)} %broadcast_in_dim.62.out_ref) | copy-start | bytes 6291460
  111.7 8.9 %copy-start.3 = (f32[256,16,128]{2,1,0:T(8,128)}, f32[256,16,128]{2,1,0:T(8,128)S(1)}, u32[]{:S(2)}) copy-start(f32[256,16,128]{2,1,0:T(8,128)S(1)} %broadcast_in_dim.61.in_ref) | copy-start | bytes 6291460
  169.8 10.9 %copy-start.33 = (f32[32,2048]{1,0:T(8,128)}, f32[32,2048]{1,0:T(8,128)S(1)}, u32[]{:S(2)}) copy-start(f32[32,2048]{1,0:T(8,128)S(1)} %get-tuple-element.80.refs_1_) | copy-start | bytes 786436
  175.4 5.3 copy-start.68
  175.7 5.0 copy-start.36
  175.7 5.0 copy-start.54
  239.7 4.5 copy-start.62
  239.7 5.0 copy-start.55
  303.5 19.7 %copy-start.25 = (f32[32,2048]{1,0:T(8,128)}, f32[32,2048]{1,0:T(8,128)S(1)}, u32[]{:S(2)}) copy-start(f32[32,2048]{1,0:T(8,128)S(1)} %get-tuple-element.90.refs_1_.refs_6_) | copy-start | bytes 786436
  303.5 5.8 copy-start.74
  303.5 5.8 copy-start.84
  379.9 4.9 copy-start.23
  387.5 47.4 %copy-start.69 = (f32[1024,512]{0,1:T(8,128)S(1)}, f32[1024,512]{0,1:T(8,128)}, u32[]{:S(2)}) copy-start(f32[1024,512]{0,1:T(8,128)} %copy-done.68) | copy-start | bytes 6291460
  434.9 5.0 copy-start.17
  435.0 4.9 copy-start.83
  442.4 6.2 copy-start.85
  450.0 60.6 %copy-start.63 = (bf16[2048,256]{1,0:T(8,128)(2,1)S(1)}, bf16[2048,256]{1,0:T(8,128)(2,1)}, u32[]{:S(2)}) copy-start(bf16[2048,256]{1,0:T(8,128)(2,1)} %convolution_convert_fusion.12) | copy-start | bytes 3145732
  513.6 50.7 %all-to-all-start.1 = ((bf16[8,256,1024]{2,1,0:T(8,128)(2,1)}), bf16[8,256,1024]{2,1,0:T(8,128)(2,1)}, u32[]{:S(2)}, u32[]{:S(2)}) async-start(bf16[8,256,1024]{2,1,0:T(8,128)(2,1)} %pad_maximum_fusion), calls=%async_computation.1 | async-start | bytes 8388608 | tf_op jit(solution)/shard_map/all_to_all | solution.py:1403
  548.1 4.3 copy-start.71
  548.2 6.2 copy-start.16
  548.2 7.1 %copy-start.9 = (bf16[4,3,256,512]{3,2,1,0:T(8,128)(2,1)S(1)}, bf16[4,3,256,512]{3,2,1,0:T(8,128)(2,1)}, u32[]{:S(2)}) copy-start(bf16[4,3,256,512]{3,2,1,0:T(8,128)(2,1)} %copy-done.8) | copy-start | bytes 9437188
  559.8 34.5 %copy-start.82 = (pred[256]{0:T(512)(128)(4,1)S(1)}, pred[256]{0:T(512)(128)(4,1)}, u32[]{:S(2)}) copy-start(pred[256]{0:T(512)(128)(4,1)} %constant.64.clone.1) | copy-start | bytes 772
  564.3 36.9 %copy-start.6 = (bf16[8,256,1024]{2,1,0:T(8,128)(2,1)S(1)}, bf16[8,256,1024]{2,1,0:T(8,128)(2,1)}, u32[]{:S(2)}) copy-start(bf16[8,256,1024]{2,1,0:T(8,128)(2,1)} %copy-done.4) | copy-start | bytes 12582916
  594.3 9.1 %copy-start.18 = (bf16[4,1,256,1024]{3,2,1,0:T(8,128)(2,1)}, bf16[4,1,256,1024]{3,2,1,0:T(8,128)(2,1)S(1)}, u32[]{:S(2)}) copy-start(bf16[4,1,256,1024]{3,2,1,0:T(8,128)(2,1)S(1)} %get-tuple-element.118) | copy-start | bytes 6291460
  607.4 4.1 copy-start.77
  607.4 4.1 copy-start.78
  607.4 4.1 copy-start.79
  611.5 3.6 copy-start.53
  679.8 4.7 copy-start.19
  687.9 7.5 %copy-start.32 = (f32[128,2048]{1,0:T(8,128)S(1)}, f32[128,2048]{1,0:T(8,128)}, u32[]{:S(2)}) copy-start(f32[128,2048]{1,0:T(8,128)} %copy-done.31) | copy-start | bytes 3145732
  687.9 8.5 %copy-start.30 = (f32[128,2048]{1,0:T(8,128)S(1)}, f32[128,2048]{1,0:T(8,128)}, u32[]{:S(2)}) copy-start(f32[128,2048]{1,0:T(8,128)} %copy-done.29) | copy-start | bytes 3145732
  687.9 9.4 %copy-start.1 = (f32[1024,4]{0,1:T(4,128)S(1)}, f32[1024,4]{0,1:T(4,128)}, u32[]{:S(2)}) copy-start(f32[1024,4]{0,1:T(4,128)} %param.22) | copy-start | bytes 49156
  (42 other events, 76.5 us)

commit v5 on v4

--- a/solution.py
+++ b/solution.py
@@ -1565,42 +1565,45 @@
         ways, rows, 4, 0, early_group, 2, "edge_one", loads=[focus_pull],
     )
 
-    def ffn(normed, mat):
-        units = mat.shape[1] // 3
-        both = project(normed, mat[:, : 2 * units])
+    def ffn(normed, pair_mat, down_mat):
+        units = down_mat.shape[1]
+        both = project(normed, pair_mat)
         hidden = gated_unit(both[:, :units], both[:, units:]).astype(low)
-        return project_t(hidden, mat[:, 2 * units :]).astype(low), both, hidden
-
-    early_part, early_both, early_hidden = ffn(second_low, early_mat)
-    third_low, stream_two, last_grad, focus_weights = edge(
+        return project_t(hidden, down_mat).astype(low), both, hidden
+
+    units = early_mat.shape[1] // 3
+    early_mats = (early_mat[:, : 2 * units], early_mat[:, 2 * units :])
+    late_size = late_down.shape[1] // spots
+    late_pulls = [
+        Load("exchange", [one], (spots, width // spots, blocks * late_size), partial(plane_items, spots), blocks, stage)
+        for one, blocks, stage in ((late_gate_up, 2, 0), (late_down, 1, 2))
+    ]
+    early_part, early_both, early_hidden = ffn(second_low, *early_mats)
+    third_low, stream_two, last_grad, focus_weights, late_down_weights = edge(
         "forward", early_part, [stream_one, norm_gains[2:3], output_grad], ways, rows, 4, early_group, 0, 3, "edge_two",
-        "gather", [Load("second", [focus_half], focus_half.shape, handed_items, 1, 1)],
+        "gather", [Load("second", [focus_half], focus_half.shape, handed_items, 1, 1), late_pulls[1]],
     )
     focus_mat = focus_weights.reshape(width, -1)
 
-    late_pull = Load(
-        "exchange", [late_gate_up, late_down], (spots, width // spots, 3 * late_down.shape[1] // spots),
-        partial(plane_items, spots), 3, 0,
-    )
     down, side = flat_segs[:, None], flat_segs.reshape(2, rows)
     joint_low, attended_low = attend(project(third_low, focus_mat[:, : 3 * heads_width]), down, side, rows)
-    fourth_low, stream_three, late_weights = edge(
+    fourth_low, stream_three, late_pair_weights = edge(
         "forward", project_t(attended_low, focus_mat[:, 3 * heads_width :]).astype(low),
-        [stream_two, norm_gains[3:4]], ways, rows, 4, 0, late_group, 4, "edge_three", loads=[late_pull],
-    )
-
-    late_mat = late_weights.reshape(width, -1)
-    late_part, late_both, late_hidden = ffn(fourth_low, late_mat)
-
-    def ffn_back(grad_low, normed, both, hidden, mat):
-        units = mat.shape[1] // 3
-        grad_hidden = project(grad_low, mat[:, 2 * units :])
+        [stream_two, norm_gains[3:4]], ways, rows, 4, 0, late_group, 4, "edge_three", loads=late_pulls[:1],
+    )
+
+    late_mats = (late_pair_weights.reshape(width, -1), late_down_weights.reshape(width, -1))
+    late_part, late_both, late_hidden = ffn(fourth_low, *late_mats)
+
+    def ffn_back(grad_low, normed, both, hidden, pair_mat, down_mat):
+        units = down_mat.shape[1]
+        grad_hidden = project(grad_low, down_mat)
         _, unit_back = jax.vjp(gated_unit, both[:, :units], both[:, units:])
         both_low = jnp.concatenate(unit_back(grad_hidden), axis=1).astype(low)
-        grad_normed = project_t(both_low, mat[:, : 2 * units]).astype(low)
+        grad_normed = project_t(both_low, pair_mat).astype(low)
         return grad_normed, [by_spot(outer_rows(normed, both_low)), by_spot(outer_rows(grad_low, hidden))]
 
-    grad_fourth, late_joints = ffn_back(last_grad, fourth_low, late_both, late_hidden, late_mat)
+    grad_fourth, late_joints = ffn_back(last_grad, fourth_low, late_both, late_hidden, *late_mats)
     grad_zero = lax.dynamic_slice_in_dim(output_grad, depth * share, share, 0).astype(jnp.float32)
     grad_low_three, grad_three, gain_four, output_part, late_down_swapped = edge(
         "backward", grad_fourth, [stream_three, norm_gains[3:4], grad_zero, late_part],
@@ -1617,7 +1620,7 @@
     )
     focus_joints = [by_spot(outer_rows(third_low, joint_grad)), by_spot(outer_rows(grad_low_three, attended_low))]
 
-    grad_second, early_joints = ffn_back(grad_low_two, second_low, early_both, early_hidden, early_mat)
+    grad_second, early_joints = ffn_back(grad_low_two, second_low, early_both, early_hidden, *early_mats)
     grad_low_one, grad_one, gain_two, focus_swapped = edge(
         "backward", grad_second, [stream_one, norm_gains[1:2], grad_two],
         ways, rows, 4, early_group, 0, 7, "edge_six",

time: 703 us -> 704 us (level)
    unnamed x176 -> x172, local copies, waits for them, and re-layouts: 20.7 us -> 20 us
where the time goes in v5:
time: 704 us; the launch traced here: 694 us
  Pallas kernels  539 us (77%)
  matrix products  66.1 us (9%)
  local copies, waits for them, and re-layouts  45.7 us (6%)
  other arithmetic  28.3 us (4%)
  starting transfers between devices  10.5 us (1%)
    pallas_call x9, Pallas kernels, edge(): pl.pallas_call(partial(edge_kernel, kind, extra, loads, ways, rows, parts...  436 us
    pallas_call x1, Pallas kernels, opening(): pl.pallas_call(partial(opening_kernel, ways, rows), in_specs=[vmem] * 2 +...  58.8 us
    dot_general x9, matrix products, project_t(): lax.dot_general(left, right, (((1,), (1,)), ((), ())), preferred_element_...  24.9 us
    dot_general x8, matrix products, project(): return jnp.dot(left, right, preferred_element_type=jnp.float32)  23.3 us
    pallas_call x1, Pallas kernels, scan_backward(): pl.pallas_call(partial(scan_backward_kernel, groups, tokens // groups), g...  21.1 us
    unnamed x172, local copies, waits for them, and re-layouts  20 us
    dot_general x11, matrix products, outer_rows(): lax.dot_general(left, right, (((0,), (0,)), ((), ())), preferred_element_...  17.9 us
  transfers between devices with their start and end apart: 3, of which 1 were waited for; matrix products, arithmetic and copies ran while one was open for 6% of the time, Pallas kernels for 22%

profile of v5, /device:TPU:1, one launch (start us, length us, event | category | flops | bytes accessed | tf_op | source)
XLA Modules:
  0.0 694.0 jit_solution(12675123710793404764)
XLA Ops:
  4.6 1.7 copy-done.63
  6.2 58.8 %opening.1 = (bf16[256,2048]{1,0:T(8,128)(2,1)S(1)}, bf16[8,256,1024]{2,1,0:T(8,128)(2,1)S(1)}, bf16[8,304,512]{2,1,0:T(8,128)(2,1)S(1)}) custom-call(bf16[128,2048]{1,0:T(8,128)(2,1)S(1)} %copy-done.35, f32[1,2048]{1,0:T(1,128)S(1)} %get-tuple-element.168.gain_ref.refs_2_, bf16[2,256,1024]{2,1,0:T(8,128)(2,1)S(1)} %copy-done.28, ...), custom_call_target="tpu_custom_call" | custom-call | flops 1 | bytes 1 | tf_op jit(solution)/shard_map/opening/pallas_call | solution.py:1191
  65.0 2.0 copy-done.4
  67.1 5.3 all-to-all-start
  79.0 1.6 slice.186
  80.6 2.7 reshape.231
  84.7 1.9 dynamic-slice_convert_fusion
  89.0 2.2 copy-done.5
  91.2 2.9 front.1
  94.2 15.1 %mix_sum.1 = f32[256,256]{1,0:T(8,128)S(1)} custom-call(f32[256,256]{1,0:T(8,128)S(1)} %get-tuple-element.77.refs_0_), custom_call_target="tpu_custom_call" | custom-call | flops 1 | bytes 1 | tf_op jit(solution)/shard_map/mix_sum/pallas_call | solution.py:1096
  111.0 7.9 %scan_forward.1 = bf16[256,512]{1,0:T(8,128)(2,1)S(1)} custom-call(f32[256]{0:T(256)S(1)} %subtract_bitcast_fusion.keep_ref, bf16[256,512]{1,0:T(8,128)(2,1)S(1)} %get-tuple-element.76.chan_ref, f32[256,512]{1,0:T(8,128)S(1)} %fusion.41.raw_ref, f32[256,512]{1,0:T(8,128)S(1)} %get-tuple-element.78.gate_ref, f32[1,512]{1,0:T(1,128)S(1)} %bitcast.121, ...), custom_call_target="tpu_custom_call" | custom-call | flops 1 | bytes 17179869184 | tf_op jit(solution)/shard_map/scan_forward/pallas_call | solution.py:120
  120.2 48.7 %edge_one.1 = (bf16[1024,2048]{1,0:T(8,128)(2,1)}, f32[32,2048]{1,0:T(8,128)S(1)}, bf16[8,256,1024]{2,1,0:T(8,128)(2,1)}) custom-call(bf16[256,2048]{1,0:T(8,128)(2,1)S(1)} %convolution_convert_fusion.10.refs_0_, f32[32,2048]{1,0:T(8,128)S(1)} %copy-done.12, f32[1,2048]{1,0:T(1,128)S(1)} %copy-done.49, bf16[3,256,512]{2,1,0:T(8,128)(2,1)S(1)} %copy-done.36, ...), custom_call_target="tpu_custom_call" | custom-call | flops 1 | bytes 1 | tf_op jit(solution)/shard_map/edge_one/pallas_call | solution.py:1096
  169.2 5.2 fusion.8
  174.9 5.0 convolution_convert_fusion.3.refs_0_
  179.9 68.2 %edge_two.1 = (bf16[256,2048]{1,0:T(8,128)(2,1)S(1)}, f32[32,2048]{1,0:T(8,128)S(1)}, bf16[1024,2048]{1,0:T(8,128)(2,1)}, bf16[8,256,1024]{2,1,0:T(8,128)(2,1)}, bf16[8,256,256]{2,1,0:T(8,128)(2,1)S(1)}) custom-call(bf16[1024,2048]{1,0:T(8,128)(2,1)} %convolution_convert_fusion.3.refs_0_, ...), custom_call_target="tpu_custom_call", output_to_operand_aliasing={{3}: (4, {})} | custom-call | flops 1 | bytes 1 | tf_op jit(solution)/shard_map/edge_two/pallas_call | solution.py:1096
  248.1 3.0 fusion.2.joint_ref
  253.1 47.3 %edge_three.1 = (bf16[1024,2048]{1,0:T(8,128)(2,1)}, f32[32,2048]{1,0:T(8,128)S(1)}, bf16[8,256,512]{2,1,0:T(8,128)(2,1)S(1)}) custom-call(bf16[256,2048]{1,0:T(8,128)(2,1)S(1)} %convolution_convert_fusion.15.refs_0_, f32[32,2048]{1,0:T(8,128)S(1)} %get-tuple-element.89.refs_1_, f32[1,2048]{1,0:T(1,128)S(1)} %copy-done.54, bf16[2,256,2048]{2,1,0:T(8,128)(2,1)S(1)} %copy-done.20), custom_call_target="tpu_custom_call" | custom-call | flops 1 | bytes 1 | tf_op jit(solution)/shard_map/edge_three/pallas_call | solution.py:1096
  300.5 4.7 fusion.55
  305.2 1.7 fusion.15
  307.4 2.5 convolution_convert_fusion.9
  309.9 4.4 convolution_convert_fusion.2.refs_0_
  315.8 3.8 convolution_convert_fusion.1.refs_4_
  319.5 56.7 %edge_four.1 = (bf16[256,2048]{1,0:T(8,128)(2,1)S(1)}, f32[32,2048]{1,0:T(8,128)S(1)}, f32[1,2048]{1,0:T(1,128)S(1)}, bf16[128,2048]{1,0:T(8,128)(2,1)S(1)}, bf16[1,256,2048]{2,1,0:T(8,128)(2,1)S(1)}) custom-call(bf16[1024,2048]{1,0:T(8,128)(2,1)} %convolution_convert_fusion.2.refs_0_, f32[32,2048]{1,0:T(8,128)S(1)} %get-tuple-element.92.refs_1_.refs_6_, ...), custom_call_target="tpu_custom_call" | custom-call | flops 1 | bytes 1 | tf_op jit(solution)/shard_map/edge_four/pallas_call | solution.py:1096
  378.2 1.9 attend_back.1
  381.2 2.7 convolution_convert_fusion.4
  383.9 47.4 %edge_five.1 = (bf16[1024,2048]{1,0:T(8,128)(2,1)}, f32[32,2048]{1,0:T(8,128)S(1)}, f32[1,2048]{1,0:T(1,128)S(1)}, bf16[2,256,2048]{2,1,0:T(8,128)(2,1)S(1)}) custom-call(bf16[256,2048]{1,0:T(8,128)(2,1)S(1)} %fusion.4.refs_0_, f32[32,2048]{1,0:T(8,128)S(1)} %get-tuple-element.89.refs_1_, f32[1,2048]{1,0:T(1,128)S(1)} %copy-done.53, ...), custom_call_target="tpu_custom_call" | custom-call | flops 1 | bytes 1 | tf_op jit(solution)/shard_map/edge_five/pallas_call | solution.py:1096
  431.3 4.9 fusion.18
  436.2 2.5 convolution_convert_fusion.8
  438.7 6.2 convolution_convert_fusion.refs_0_
  446.3 60.6 %edge_six.1 = (bf16[256,2048]{1,0:T(8,128)(2,1)S(1)}, f32[32,2048]{1,0:T(8,128)S(1)}, f32[1,2048]{1,0:T(1,128)S(1)}, bf16[4,3,256,512]{3,2,1,0:T(8,128)(2,1)S(1)}) custom-call(bf16[1024,2048]{1,0:T(8,128)(2,1)} %convolution_convert_fusion.refs_0_, f32[32,2048]{1,0:T(8,128)S(1)} %get-tuple-element.81.refs_1_, f32[1,2048]{1,0:T(1,128)S(1)} %copy-done.50, ...), custom_call_target="tpu_custom_call" | custom-call | flops 1 | bytes 1 | tf_op jit(solution)/shard_map/edge_six/pallas_call | solution.py:1096
  506.9 2.6 pad_maximum_fusion
  509.9 5.1 all-to-all-start.1
  515.1 3.1 fusion.10.dmix_ref
  518.2 21.1 %scan_backward.1 = (f32[256,512]{1,0:T(8,128)}, bf16[256,512]{1,0:T(8,128)(2,1)}, bf16[256,512]{1,0:T(8,128)(2,1)}, f32[256,16,128]{2,1,0:T(8,128)}, f32[256,16,...) custom-call(f32[256]{0:T(256)} %copy-done.59, bf16[256,512]{1,0:T(8,128)(2,1)} %copy-done.10, ...), custom_call_target="tpu_custom_call" | custom-call | flops 1 | bytes 17179869184 | tf_op jit(solution)/shard_map/scan_backward/pallas_call | solution.py:230
  540.0 2.2 reduce_sum.64
  542.2 2.2 reduce_sum.65
  544.5 4.3 convert_element_type.137
  551.6 1.7 convert_reduce_fusion
  553.3 2.1 convolution_convert_fusion.5
  558.1 2.5 all-to-all-done.1.came_ref
  561.7 28.9 %mix_grad_sum.1 = (f32[256,256]{1,0:T(8,128)S(1)}, bf16[4,1,256,1024]{3,2,1,0:T(8,128)(2,1)S(1)}) custom-call(f32[256,256]{1,0:T(8,128)S(1)} %copy-done.27, bf16[8,256,512]{2,1,0:T(8,128)(2,1)S(1)} %bitcast.111), custom_call_target="tpu_custom_call" | custom-call | flops 1 | bytes 1 | tf_op jit(solution)/shard_map/mix_grad_sum/pallas_call | solution.py:1096
  597.5 2.2 convolution_convert_fusion.11.refs_0_
  599.8 2.1 convolution_convert_fusion.6
  603.7 4.1 convert_element_type.132
  607.9 3.5 pad.26.refs_8_
  611.4 62.7 %edge_seven.1 = (f32[128,2048]{1,0:T(8,128)S(1)}, f32[32,1024]{1,0:T(8,128)S(1)}, f32[128,2048]{1,0:T(8,128)S(1)}, bf16[4,1,256,1024]{3,2,1,0:T(8,128)(2,1)}, bf16[4,1,304,1024]{3,2,1,0:T(8,128)(2,1)}) custom-call(bf16[256,2048]{1,0:T(8,128)(2,1)S(1)} %convolution_convert_fusion.11.refs_0_, f32[32,2048]{1,0:T(8,128)S(1)} %copy-done.12, ...), custom_call_target="tpu_custom_call" | custom-call | flops 1 | bytes 1 | tf_op jit(solution)/shard_map/edge_seven/pallas_call | solution.py:1096
  678.6 2.2 convert_reduce_fusion.3
  684.2 7.5 %spread_out.1 = (f32[2,256,2048]{2,1,0:T(8,128)}, f32[256,2048]{1,0:T(8,128)}, f32[256,512]{1,0:T(8,128)}) custom-call(bf16[8,256,1024]{2,1,0:T(8,128)(2,1)} %all-to-all-done.1.came_ref), custom_call_target="tpu_custom_call" | custom-call | tf_op jit(solution)/shard_map/spread_out/pallas_call | solution.py:1429
  (250 shorter events, 52.2 us)
Async XLA Ops:
  0.6 71.7 %copy-start = (f32[1024,4]{0,1:T(4,128)S(1)}, f32[1024,4]{0,1:T(4,128)}, u32[]{:S(2)}) copy-start(f32[1024,4]{0,1:T(4,128)} %param.22) | copy-start | bytes 49156
  0.7 85.9 %collective-permute-start = (s32[2,4]{1,0:T(2,128)}, s32[2,4]{1,0:T(2,128)}, u32[]{:S(2)}, u32[]{:S(2)}) collective-permute-start(s32[2,4]{1,0:T(2,128)} %param.18), channel_id=1, source_target_pairs={{0,4},{4,0},{8,12},{12,8},{16,20},{20,16},{24,28},{28,24},{1,5},{5... | collective-permute-start | bytes 104 | tf_op jit(solution)/shard_map/ppermute | solution.py:1487
  2.4 3.9 copy-start.51
  67.1 102.2 %all-to-all-start = ((bf16[8,256,768]{2,1,0:T(8,128)(2,1)}), bf16[8,256,768]{2,1,0:T(8,128)(2,1)}, u32[]{:S(2)}, u32[]{:S(2)}) async-start(bf16[8,256,768]{2,1,0:T(8,128)(2,1)} %copy-done.63), calls=%async_computation | async-start | bytes 6291456 | tf_op jit(solution)/shard_map/all_to_all | solution.py:1403
  76.9 12.1 %copy-start.55 = (f32[512]{0:T(512)}, f32[512]{0:T(512)S(1)}, u32[]{:S(2)}) copy-start(f32[512]{0:T(512)S(1)} %dynamic_slice.22) | copy-start | bytes 6148
  77.6 33.3 %copy-start.57 = (f32[512]{0:T(512)}, f32[512]{0:T(512)S(1)}, u32[]{:S(2)}) copy-start(f32[512]{0:T(512)S(1)} %dynamic_slice.23) | copy-start | bytes 6148
  80.6 6.8 copy-start.79
  80.6 7.1 %copy-start.78 = (s32[2]{0:T(128)S(1)}, s32[2]{0:T(128)}, u32[]{:S(2)}) copy-start(s32[2]{0:T(128)} %iota_multiply_fusion) | copy-start | bytes 28
  80.6 8.4 %copy-start.47 = (f32[4,512]{1,0:T(4,128)S(1)}, f32[4,512]{1,0:T(4,128)}, u32[]{:S(2)}) copy-start(f32[4,512]{1,0:T(4,128)} %dynamic-slice_bitcast_fusion.taps_ref) | copy-start | bytes 24580
  84.7 9.4 %copy-start.13 = (bf16[256,512]{1,0:T(8,128)(2,1)}, bf16[256,512]{1,0:T(8,128)(2,1)S(1)}, u32[]{:S(2)}) copy-start(bf16[256,512]{1,0:T(8,128)(2,1)S(1)} %pad.23.select_ref) | copy-start | bytes 786436
  91.2 18.3 %copy-start.65 = (bf16[2336,512]{1,0:T(8,128)(2,1)S(1)}, bf16[2336,512]{1,0:T(8,128)(2,1)}, u32[]{:S(2)}) copy-start(bf16[2336,512]{1,0:T(8,128)(2,1)} %copy-done.64) | copy-start | bytes 7176196
  94.1 16.2 %copy-start.37 = (f32[256,512]{1,0:T(8,128)}, f32[256,512]{1,0:T(8,128)S(1)}, u32[]{:S(2)}) copy-start(f32[256,512]{1,0:T(8,128)S(1)} %get-tuple-element.75.conv_ref) | copy-start | bytes 1572868
  94.1 16.8 %copy-start.10 = (bf16[256,512]{1,0:T(8,128)(2,1)}, bf16[256,512]{1,0:T(8,128)(2,1)S(1)}, u32[]{:S(2)}) copy-start(bf16[256,512]{1,0:T(8,128)(2,1)S(1)} %get-tuple-element.76.chan_ref) | copy-start | bytes 786436
  94.1 16.8 %copy-start.21 = (f32[256,512]{1,0:T(8,128)}, f32[256,512]{1,0:T(8,128)S(1)}, u32[]{:S(2)}) copy-start(f32[256,512]{1,0:T(8,128)S(1)} %get-tuple-element.78.gate_ref) | copy-start | bytes 1572868
  94.2 16.8 %copy-start.43 = (f32[16,512]{1,0:T(8,128)S(1)}, f32[16,512]{1,0:T(8,128)}, u32[]{:S(2)}) copy-start(f32[16,512]{1,0:T(8,128)} %negate_bitcast_fusion.rate_ref) | copy-start | bytes 98308
  94.2 16.8 %copy-start.58 = (f32[512]{0:T(512)S(1)}, f32[512]{0:T(512)}, u32[]{:S(2)}) copy-start(f32[512]{0:T(512)} %dynamic_slice.25) | copy-start | bytes 6148
  109.7 9.2 %copy-start.7 = (f32[256,512]{1,0:T(8,128)}, f32[256,512]{1,0:T(8,128)S(1)}, u32[]{:S(2)}) copy-start(f32[256,512]{1,0:T(8,128)S(1)} %fusion.41.raw_ref) | copy-start | bytes 1572868
  110.3 8.6 %copy-start.2 = (f32[256,16,128]{2,1,0:T(8,128)}, f32[256,16,128]{2,1,0:T(8,128)S(1)}, u32[]{:S(2)}) copy-start(f32[256,16,128]{2,1,0:T(8,128)S(1)} %broadcast_in_dim.62.out_ref) | copy-start | bytes 6291460
  111.0 8.7 %copy-start.3 = (f32[256,16,128]{2,1,0:T(8,128)}, f32[256,16,128]{2,1,0:T(8,128)S(1)}, u32[]{:S(2)}) copy-start(f32[256,16,128]{2,1,0:T(8,128)S(1)} %broadcast_in_dim.61.in_ref) | copy-start | bytes 6291460
  174.5 5.4 copy-start.67
  174.8 5.0 copy-start.22
  174.8 5.0 copy-start.34
  174.9 5.0 copy-start.53
  248.1 4.5 copy-start.61
  300.5 19.1 %copy-start.25 = (f32[32,2048]{1,0:T(8,128)}, f32[32,2048]{1,0:T(8,128)S(1)}, u32[]{:S(2)}) copy-start(f32[32,2048]{1,0:T(8,128)S(1)} %get-tuple-element.92.refs_1_.refs_6_) | copy-start | bytes 786436
  300.5 4.8 copy-start.82
  315.7 3.8 copy-start.33
  376.2 4.9 copy-start.23
  383.9 47.4 %copy-start.68 = (f32[1024,512]{0,1:T(8,128)S(1)}, f32[1024,512]{0,1:T(8,128)}, u32[]{:S(2)}) copy-start(f32[1024,512]{0,1:T(8,128)} %copy-done.67) | copy-start | bytes 6291460
  431.2 5.0 copy-start.17
  431.3 4.9 copy-start.81
  438.7 6.2 copy-start.83
  446.3 60.7 %copy-start.62 = (bf16[2048,256]{1,0:T(8,128)(2,1)S(1)}, bf16[2048,256]{1,0:T(8,128)(2,1)}, u32[]{:S(2)}) copy-start(bf16[2048,256]{1,0:T(8,128)(2,1)} %convolution_convert_fusion.12) | copy-start | bytes 3145732
  509.9 50.7 %all-to-all-start.1 = ((bf16[8,256,1024]{2,1,0:T(8,128)(2,1)}), bf16[8,256,1024]{2,1,0:T(8,128)(2,1)}, u32[]{:S(2)}, u32[]{:S(2)}) async-start(bf16[8,256,1024]{2,1,0:T(8,128)(2,1)} %pad_maximum_fusion), calls=%async_computation.1 | async-start | bytes 8388608 | tf_op jit(solution)/shard_map/all_to_all | solution.py:1403
  544.5 4.3 copy-start.70
  544.5 6.3 copy-start.16
  544.5 7.1 %copy-start.9 = (bf16[4,3,256,512]{3,2,1,0:T(8,128)(2,1)S(1)}, bf16[4,3,256,512]{3,2,1,0:T(8,128)(2,1)}, u32[]{:S(2)}) copy-start(bf16[4,3,256,512]{3,2,1,0:T(8,128)(2,1)} %copy-done.8) | copy-start | bytes 9437188
  556.1 34.5 %copy-start.80 = (pred[256]{0:T(512)(128)(4,1)S(1)}, pred[256]{0:T(512)(128)(4,1)}, u32[]{:S(2)}) copy-start(pred[256]{0:T(512)(128)(4,1)} %constant.64.clone.1) | copy-start | bytes 772
  560.6 36.9 %copy-start.6 = (bf16[8,256,1024]{2,1,0:T(8,128)(2,1)S(1)}, bf16[8,256,1024]{2,1,0:T(8,128)(2,1)}, u32[]{:S(2)}) copy-start(bf16[8,256,1024]{2,1,0:T(8,128)(2,1)} %copy-done.4) | copy-start | bytes 12582916
  590.6 9.2 %copy-start.18 = (bf16[4,1,256,1024]{3,2,1,0:T(8,128)(2,1)}, bf16[4,1,256,1024]{3,2,1,0:T(8,128)(2,1)S(1)}, u32[]{:S(2)}) copy-start(bf16[4,1,256,1024]{3,2,1,0:T(8,128)(2,1)S(1)} %get-tuple-element.120) | copy-start | bytes 6291460
  603.7 4.1 copy-start.75
  603.7 4.1 copy-start.76
  603.7 4.1 copy-start.77
  607.8 3.6 copy-start.52
  676.1 4.7 copy-start.19
  684.2 7.5 %copy-start.32 = (f32[128,2048]{1,0:T(8,128)S(1)}, f32[128,2048]{1,0:T(8,128)}, u32[]{:S(2)}) copy-start(f32[128,2048]{1,0:T(8,128)} %copy-done.31) | copy-start | bytes 3145732
  684.2 8.5 %copy-start.30 = (f32[128,2048]{1,0:T(8,128)S(1)}, f32[128,2048]{1,0:T(8,128)}, u32[]{:S(2)}) copy-start(f32[128,2048]{1,0:T(8,128)} %copy-done.29) | copy-start | bytes 3145732
  684.2 9.4 %copy-start.1 = (f32[1024,4]{0,1:T(4,128)S(1)}, f32[1024,4]{0,1:T(4,128)}, u32[]{:S(2)}) copy-start(f32[1024,4]{0,1:T(4,128)} %param.22) | copy-start | bytes 49156
  (40 other events, 74.2 us)

commit v6 on v4

--- a/solution.py
+++ b/solution.py
@@ -1404,23 +1404,19 @@
 
 
 def spread_out_kernel(came_ref, pair_ref, last_ref, sum_ref):
-    size = last_ref.shape[1]
+    size = last_ref.shape[1] // 2
     half = came_ref.shape[2] - 3 * size
-    spot = pl.program_id(0)
-    for at in range(2):
-        pair_ref[at] = came_ref[0, :, at * size : (at + 1) * size].astype(jnp.float32)
-    last_ref[...] = came_ref[0, :, 2 * size : 3 * size].astype(jnp.float32)
-    piece = came_ref[0, :, 3 * size :].astype(jnp.float32)
+
+    @pl.when(pl.program_id(0) == 0)
+    def _():
+        sum_ref[...] = jnp.zeros_like(sum_ref)
+
     for core in range(2):
-        lanes = slice(core * half, (core + 1) * half)
-
-        @pl.when(spot == core)
-        def _():
-            sum_ref[:, lanes] = piece
-
-        @pl.when((spot > 1) & (lax.rem(spot, 2) == core))
-        def _():
-            sum_ref[:, lanes] += piece
+        to = slice(core * size, (core + 1) * size)
+        for at in range(2):
+            pair_ref[at, :, to] = came_ref[core, :, at * size : (at + 1) * size].astype(jnp.float32)
+        last_ref[:, to] = came_ref[core, :, 2 * size : 3 * size].astype(jnp.float32)
+        sum_ref[:, core * half : (core + 1) * half] += came_ref[core, :, 3 * size :].astype(jnp.float32)
 
 
 def spread_out(came, columns):
@@ -1428,11 +1424,11 @@
     size, half = columns // 3, came.shape[2] - columns
     return pl.pallas_call(
         spread_out_kernel,
-        grid=(spots,),
-        in_specs=[pl.BlockSpec((1, rows, came.shape[2]), lambda i: (i, 0, 0))],
+        grid=(spots // 2,),
+        in_specs=[pl.BlockSpec((2, rows, came.shape[2]), lambda i: (i, 0, 0))],
         out_specs=[
-            pl.BlockSpec((2, rows, size), lambda i: (0, 0, i)),
-            pl.BlockSpec((rows, size), lambda i: (0, i)),
+            pl.BlockSpec((2, rows, 2 * size), lambda i: (0, 0, i)),
+            pl.BlockSpec((rows, 2 * size), lambda i: (0, i)),
             pl.BlockSpec((rows, 2 * half), lambda i: (0, 0)),
         ],
         out_shape=[
@@ -1440,6 +1436,7 @@
             jax.ShapeDtypeStruct((rows, spots * size), jnp.float32),
             jax.ShapeDtypeStruct((rows, 2 * half), jnp.float32),
         ],
+        compiler_params=pltpu.CompilerParams(vmem_limit_bytes=32 << 20),
         name="spread_out",
     )(came)
 

time: 703 us -> 701 us (level)
  no operation moved by 1% of the time
where the time goes in v6:
time: 701 us; the launch traced here: 696 us
  Pallas kernels  539 us (77%)
  matrix products  66.8 us (10%)
  local copies, waits for them, and re-layouts  46.5 us (7%)
  other arithmetic  28.2 us (4%)
  starting transfers between devices  10.5 us (1%)
    pallas_call x9, Pallas kernels, edge(): pl.pallas_call(partial(edge_kernel, kind, extra, loads, ways, rows, parts...  438 us
    pallas_call x1, Pallas kernels, opening(): pl.pallas_call(partial(opening_kernel, ways, rows), in_specs=[vmem] * 2 +...  58.8 us
    dot_general x9, matrix products, project_t(): lax.dot_general(left, right, (((1,), (1,)), ((), ())), preferred_element_...  24.5 us
    dot_general x8, matrix products, project(): return jnp.dot(left, right, preferred_element_type=jnp.float32)  24.4 us
    pallas_call x1, Pallas kernels, scan_backward(): pl.pallas_call(partial(scan_backward_kernel, groups, tokens // groups), g...  21.1 us
    unnamed x176, local copies, waits for them, and re-layouts  20.7 us
    dot_general x11, matrix products, outer_rows(): lax.dot_general(left, right, (((0,), (0,)), ((), ())), preferred_element_...  17.9 us
  transfers between devices with their start and end apart: 3, of which 1 were waited for; matrix products, arithmetic and copies ran while one was open for 6% of the time, Pallas kernels for 22%

profile of v6, /device:TPU:1, one launch (start us, length us, event | category | flops | bytes accessed | tf_op | source)
XLA Modules:
  0.0 695.8 jit_solution(12766578714775533910)
XLA Ops:
  4.6 1.7 copy-done.64
  6.2 58.8 %opening.1 = (bf16[256,2048]{1,0:T(8,128)(2,1)S(1)}, bf16[8,256,1024]{2,1,0:T(8,128)(2,1)S(1)}, bf16[8,304,512]{2,1,0:T(8,128)(2,1)S(1)}) custom-call(bf16[128,2048]{1,0:T(8,128)(2,1)S(1)} %copy-done.35, f32[1,2048]{1,0:T(1,128)S(1)} %get-tuple-element.166.gain_ref.refs_2_, bf16[2,256,1024]{2,1,0:T(8,128)(2,1)S(1)} %copy-done.28, ...), custom_call_target="tpu_custom_call" | custom-call | flops 1 | bytes 1 | tf_op jit(solution)/shard_map/opening/pallas_call | solution.py:1191
  65.0 2.0 copy-done.4
  67.1 5.3 all-to-all-start
  79.0 1.6 slice.196
  80.6 2.7 reshape.228
  84.8 1.8 dynamic-slice_convert_fusion
  88.9 2.2 copy-done.5
  91.1 2.9 front.1
  94.8 15.1 %mix_sum.1 = f32[256,256]{1,0:T(8,128)S(1)} custom-call(f32[256,256]{1,0:T(8,128)S(1)} %get-tuple-element.76.refs_0_), custom_call_target="tpu_custom_call" | custom-call | flops 1 | bytes 1 | tf_op jit(solution)/shard_map/mix_sum/pallas_call | solution.py:1096
  111.7 8.0 %scan_forward.1 = bf16[256,512]{1,0:T(8,128)(2,1)S(1)} custom-call(f32[256]{0:T(256)S(1)} %subtract_bitcast_fusion.keep_ref, bf16[256,512]{1,0:T(8,128)(2,1)S(1)} %get-tuple-element.75.chan_ref, f32[256,512]{1,0:T(8,128)S(1)} %fusion.47.raw_ref, f32[256,512]{1,0:T(8,128)S(1)} %get-tuple-element.77.gate_ref, f32[1,512]{1,0:T(1,128)S(1)} %bitcast.114, ...), custom_call_target="tpu_custom_call" | custom-call | flops 1 | bytes 17179869184 | tf_op jit(solution)/shard_map/scan_forward/pallas_call | solution.py:120
  121.0 48.8 %edge_one.1 = (bf16[1024,2048]{1,0:T(8,128)(2,1)}, f32[32,2048]{1,0:T(8,128)S(1)}, bf16[8,256,1024]{2,1,0:T(8,128)(2,1)}) custom-call(bf16[256,2048]{1,0:T(8,128)(2,1)S(1)} %convolution_convert_fusion.10.refs_0_, f32[32,2048]{1,0:T(8,128)S(1)} %copy-done.12, f32[1,2048]{1,0:T(1,128)S(1)} %copy-done.50, bf16[3,256,512]{2,1,0:T(8,128)(2,1)S(1)} %copy-done.37, ...), custom_call_target="tpu_custom_call" | custom-call | flops 1 | bytes 1 | tf_op jit(solution)/shard_map/edge_one/pallas_call | solution.py:1096
  170.1 5.2 fusion.11
  175.7 5.0 convolution_convert_fusion.3.refs_0_
  180.7 58.9 %edge_two.1 = (bf16[256,2048]{1,0:T(8,128)(2,1)S(1)}, f32[32,2048]{1,0:T(8,128)S(1)}, bf16[1024,2048]{1,0:T(8,128)(2,1)}, bf16[8,256,1024]{2,1,0:T(8,128)(2,1)}) custom-call(bf16[1024,2048]{1,0:T(8,128)(2,1)} %convolution_convert_fusion.3.refs_0_, f32[32,2048]{1,0:T(8,128)S(1)} %get-tuple-element.80.refs_1_, ...), custom_call_target="tpu_custom_call", output_to_operand_aliasing={{3}: (4, {})} | custom-call | flops 1 | bytes 1 | tf_op jit(solution)/shard_map/edge_two/pallas_call | solution.py:1096
  239.7 3.0 fusion.2.joint_ref
  244.7 58.8 %edge_three.1 = (bf16[1024,2048]{1,0:T(8,128)(2,1)}, f32[32,2048]{1,0:T(8,128)S(1)}, bf16[8,256,768]{2,1,0:T(8,128)(2,1)}) custom-call(bf16[256,2048]{1,0:T(8,128)(2,1)S(1)} %convolution_convert_fusion.15.refs_0_, f32[32,2048]{1,0:T(8,128)S(1)} %get-tuple-element.87.refs_1_, f32[1,2048]{1,0:T(1,128)S(1)} %copy-done.55, bf16[2,256,2048]{2,1,0:T(8,128)(2,1)S(1)} %copy-done.20, ...), custom_call_target="tpu_custom_call" | custom-call | flops 1 | bytes 1 | tf_op jit(solution)/shard_map/edge_three/pallas_call | solution.py:1096
  303.5 5.8 fusion.8
  309.4 1.7 fusion.18
  311.5 2.5 convolution_convert_fusion.9
  314.1 4.4 convolution_convert_fusion.2.refs_0_
  319.9 3.4 convolution_convert_fusion.1.refs_4_
  323.2 56.7 %edge_four.1 = (bf16[256,2048]{1,0:T(8,128)(2,1)S(1)}, f32[32,2048]{1,0:T(8,128)S(1)}, f32[1,2048]{1,0:T(1,128)S(1)}, bf16[128,2048]{1,0:T(8,128)(2,1)S(1)}, bf16[1,256,2048]{2,1,0:T(8,128)(2,1)S(1)}) custom-call(bf16[1024,2048]{1,0:T(8,128)(2,1)} %convolution_convert_fusion.2.refs_0_, f32[32,2048]{1,0:T(8,128)S(1)} %get-tuple-element.90.refs_1_.refs_6_, ...), custom_call_target="tpu_custom_call" | custom-call | flops 1 | bytes 1 | tf_op jit(solution)/shard_map/edge_four/pallas_call | solution.py:1096
  381.9 1.9 attend_back.1
  384.8 2.7 convolution_convert_fusion.4
  387.5 47.4 %edge_five.1 = (bf16[1024,2048]{1,0:T(8,128)(2,1)}, f32[32,2048]{1,0:T(8,128)S(1)}, f32[1,2048]{1,0:T(1,128)S(1)}, bf16[2,256,2048]{2,1,0:T(8,128)(2,1)S(1)}) custom-call(bf16[256,2048]{1,0:T(8,128)(2,1)S(1)} %fusion.4.refs_0_, f32[32,2048]{1,0:T(8,128)S(1)} %get-tuple-element.87.refs_1_, f32[1,2048]{1,0:T(1,128)S(1)} %copy-done.54, ...), custom_call_target="tpu_custom_call" | custom-call | flops 1 | bytes 1 | tf_op jit(solution)/shard_map/edge_five/pallas_call | solution.py:1096
  435.0 4.9 fusion.21
  439.9 2.5 convolution_convert_fusion.8
  442.4 6.2 convolution_convert_fusion.refs_0_
  450.0 60.6 %edge_six.1 = (bf16[256,2048]{1,0:T(8,128)(2,1)S(1)}, f32[32,2048]{1,0:T(8,128)S(1)}, f32[1,2048]{1,0:T(1,128)S(1)}, bf16[4,3,256,512]{3,2,1,0:T(8,128)(2,1)S(1)}) custom-call(bf16[1024,2048]{1,0:T(8,128)(2,1)} %convolution_convert_fusion.refs_0_, f32[32,2048]{1,0:T(8,128)S(1)} %copy-done.34, f32[1,2048]{1,0:T(1,128)S(1)} %copy-done.51, ...), custom_call_target="tpu_custom_call" | custom-call | flops 1 | bytes 1 | tf_op jit(solution)/shard_map/edge_six/pallas_call | solution.py:1096
  510.7 2.6 pad_maximum_fusion
  513.6 5.1 all-to-all-start.1
  518.7 3.1 fusion.13.dmix_ref
  521.9 21.1 %scan_backward.1 = (f32[256,512]{1,0:T(8,128)}, bf16[256,512]{1,0:T(8,128)(2,1)}, bf16[256,512]{1,0:T(8,128)(2,1)}, f32[256,16,128]{2,1,0:T(8,128)}, f32[256,16,...) custom-call(f32[256]{0:T(256)} %copy-done.60, bf16[256,512]{1,0:T(8,128)(2,1)} %copy-done.10, ...), custom_call_target="tpu_custom_call" | custom-call | flops 1 | bytes 17179869184 | tf_op jit(solution)/shard_map/scan_backward/pallas_call | solution.py:230
  543.7 2.2 reduce_sum.64
  545.9 2.2 reduce_sum.65
  548.2 4.3 convert_element_type.137
  555.3 1.7 convert_reduce_fusion
  556.9 2.1 convolution_convert_fusion.5
  561.8 2.5 all-to-all-done.1.came_ref
  565.4 28.9 %mix_grad_sum.1 = (f32[256,256]{1,0:T(8,128)S(1)}, bf16[4,1,256,1024]{3,2,1,0:T(8,128)(2,1)S(1)}) custom-call(f32[256,256]{1,0:T(8,128)S(1)} %copy-done.27, bf16[8,256,512]{2,1,0:T(8,128)(2,1)S(1)} %bitcast.106), custom_call_target="tpu_custom_call" | custom-call | flops 1 | bytes 1 | tf_op jit(solution)/shard_map/mix_grad_sum/pallas_call | solution.py:1096
  601.2 2.2 convolution_convert_fusion.11.refs_0_
  603.5 2.1 convolution_convert_fusion.6
  607.4 4.1 convert_element_type.132
  611.6 3.5 pad.26.refs_8_
  615.1 62.7 %edge_seven.1 = (f32[128,2048]{1,0:T(8,128)S(1)}, f32[32,1024]{1,0:T(8,128)S(1)}, f32[128,2048]{1,0:T(8,128)S(1)}, bf16[4,1,256,1024]{3,2,1,0:T(8,128)(2,1)}, bf16[4,1,304,1024]{3,2,1,0:T(8,128)(2,1)}) custom-call(bf16[256,2048]{1,0:T(8,128)(2,1)S(1)} %convolution_convert_fusion.11.refs_0_, f32[32,2048]{1,0:T(8,128)S(1)} %copy-done.12, ...), custom_call_target="tpu_custom_call" | custom-call | flops 1 | bytes 1 | tf_op jit(solution)/shard_map/edge_seven/pallas_call | solution.py:1096
  682.3 2.2 convert_reduce_fusion.3
  687.9 5.7 spread_out.1
  (254 shorter events, 53.0 us)
Async XLA Ops:
  0.6 71.7 %copy-start = (f32[1024,4]{0,1:T(4,128)S(1)}, f32[1024,4]{0,1:T(4,128)}, u32[]{:S(2)}) copy-start(f32[1024,4]{0,1:T(4,128)} %param.22) | copy-start | bytes 49156
  0.7 85.9 %collective-permute-start = (s32[2,4]{1,0:T(2,128)}, s32[2,4]{1,0:T(2,128)}, u32[]{:S(2)}, u32[]{:S(2)}) collective-permute-start(s32[2,4]{1,0:T(2,128)} %param.18), channel_id=1, source_target_pairs={{0,4},{4,0},{8,12},{12,8},{16,20},{20,16},{24,28},{28,24},{1,5},{5... | collective-permute-start | bytes 104 | tf_op jit(solution)/shard_map/ppermute | solution.py:1484
  2.4 3.9 copy-start.52
  67.1 103.1 %all-to-all-start = ((bf16[8,256,768]{2,1,0:T(8,128)(2,1)}), bf16[8,256,768]{2,1,0:T(8,128)(2,1)}, u32[]{:S(2)}, u32[]{:S(2)}) async-start(bf16[8,256,768]{2,1,0:T(8,128)(2,1)} %copy-done.64), calls=%async_computation | async-start | bytes 6291456 | tf_op jit(solution)/shard_map/all_to_all | solution.py:1403
  76.9 12.0 %copy-start.56 = (f32[512]{0:T(512)}, f32[512]{0:T(512)S(1)}, u32[]{:S(2)}) copy-start(f32[512]{0:T(512)S(1)} %dynamic_slice.22) | copy-start | bytes 6148
  77.6 34.0 %copy-start.58 = (f32[512]{0:T(512)}, f32[512]{0:T(512)S(1)}, u32[]{:S(2)}) copy-start(f32[512]{0:T(512)S(1)} %dynamic_slice.23) | copy-start | bytes 6148
  80.6 6.7 copy-start.81
  80.6 7.0 %copy-start.80 = (s32[2]{0:T(128)S(1)}, s32[2]{0:T(128)}, u32[]{:S(2)}) copy-start(s32[2]{0:T(128)} %iota_multiply_fusion) | copy-start | bytes 28
  80.6 8.3 %copy-start.48 = (f32[4,512]{1,0:T(4,128)S(1)}, f32[4,512]{1,0:T(4,128)}, u32[]{:S(2)}) copy-start(f32[4,512]{1,0:T(4,128)} %dynamic-slice_bitcast_fusion.taps_ref) | copy-start | bytes 24580
  84.7 9.3 %copy-start.13 = (bf16[256,512]{1,0:T(8,128)(2,1)}, bf16[256,512]{1,0:T(8,128)(2,1)S(1)}, u32[]{:S(2)}) copy-start(bf16[256,512]{1,0:T(8,128)(2,1)S(1)} %pad.23.select_ref) | copy-start | bytes 786436
  91.1 19.1 %copy-start.66 = (bf16[2336,512]{1,0:T(8,128)(2,1)S(1)}, bf16[2336,512]{1,0:T(8,128)(2,1)}, u32[]{:S(2)}) copy-start(bf16[2336,512]{1,0:T(8,128)(2,1)} %copy-done.65) | copy-start | bytes 7176196
  94.8 16.8 %copy-start.10 = (bf16[256,512]{1,0:T(8,128)(2,1)}, bf16[256,512]{1,0:T(8,128)(2,1)S(1)}, u32[]{:S(2)}) copy-start(bf16[256,512]{1,0:T(8,128)(2,1)S(1)} %get-tuple-element.75.chan_ref) | copy-start | bytes 786436
  94.8 16.8 %copy-start.21 = (f32[256,512]{1,0:T(8,128)}, f32[256,512]{1,0:T(8,128)S(1)}, u32[]{:S(2)}) copy-start(f32[256,512]{1,0:T(8,128)S(1)} %get-tuple-element.77.gate_ref) | copy-start | bytes 1572868
  94.8 16.8 %copy-start.44 = (f32[16,512]{1,0:T(8,128)S(1)}, f32[16,512]{1,0:T(8,128)}, u32[]{:S(2)}) copy-start(f32[16,512]{1,0:T(8,128)} %negate_bitcast_fusion.rate_ref) | copy-start | bytes 98308
  94.8 16.8 %copy-start.59 = (f32[512]{0:T(512)S(1)}, f32[512]{0:T(512)}, u32[]{:S(2)}) copy-start(f32[512]{0:T(512)} %dynamic_slice.25) | copy-start | bytes 6148
  110.4 9.3 %copy-start.7 = (f32[256,512]{1,0:T(8,128)}, f32[256,512]{1,0:T(8,128)S(1)}, u32[]{:S(2)}) copy-start(f32[256,512]{1,0:T(8,128)S(1)} %fusion.47.raw_ref) | copy-start | bytes 1572868
  111.0 8.7 %copy-start.2 = (f32[256,16,128]{2,1,0:T(8,128)}, f32[256,16,128]{2,1,0:T(8,128)S(1)}, u32[]{:S(2)}) copy-start(f32[256,16,128]{2,1,0:T(8,128)S(1)} %broadcast_in_dim.62.out_ref) | copy-start | bytes 6291460
  111.7 8.9 %copy-start.3 = (f32[256,16,128]{2,1,0:T(8,128)}, f32[256,16,128]{2,1,0:T(8,128)S(1)}, u32[]{:S(2)}) copy-start(f32[256,16,128]{2,1,0:T(8,128)S(1)} %broadcast_in_dim.61.in_ref) | copy-start | bytes 6291460
  169.8 10.9 %copy-start.33 = (f32[32,2048]{1,0:T(8,128)}, f32[32,2048]{1,0:T(8,128)S(1)}, u32[]{:S(2)}) copy-start(f32[32,2048]{1,0:T(8,128)S(1)} %get-tuple-element.80.refs_1_) | copy-start | bytes 786436
  175.4 5.3 copy-start.68
  175.7 5.0 copy-start.36
  175.7 5.0 copy-start.54
  239.7 4.5 copy-start.62
  239.7 5.0 copy-start.55
  303.5 19.7 %copy-start.25 = (f32[32,2048]{1,0:T(8,128)}, f32[32,2048]{1,0:T(8,128)S(1)}, u32[]{:S(2)}) copy-start(f32[32,2048]{1,0:T(8,128)S(1)} %get-tuple-element.90.refs_1_.refs_6_) | copy-start | bytes 786436
  303.5 5.8 copy-start.74
  303.5 5.8 copy-start.84
  379.9 4.9 copy-start.23
  387.5 47.4 %copy-start.69 = (f32[1024,512]{0,1:T(8,128)S(1)}, f32[1024,512]{0,1:T(8,128)}, u32[]{:S(2)}) copy-start(f32[1024,512]{0,1:T(8,128)} %copy-done.68) | copy-start | bytes 6291460
  434.9 5.0 copy-start.17
  435.0 4.9 copy-start.83
  442.4 6.2 copy-start.85
  450.0 60.6 %copy-start.63 = (bf16[2048,256]{1,0:T(8,128)(2,1)S(1)}, bf16[2048,256]{1,0:T(8,128)(2,1)}, u32[]{:S(2)}) copy-start(bf16[2048,256]{1,0:T(8,128)(2,1)} %convolution_convert_fusion.12) | copy-start | bytes 3145732
  513.6 50.7 %all-to-all-start.1 = ((bf16[8,256,1024]{2,1,0:T(8,128)(2,1)}), bf16[8,256,1024]{2,1,0:T(8,128)(2,1)}, u32[]{:S(2)}, u32[]{:S(2)}) async-start(bf16[8,256,1024]{2,1,0:T(8,128)(2,1)} %pad_maximum_fusion), calls=%async_computation.1 | async-start | bytes 8388608 | tf_op jit(solution)/shard_map/all_to_all | solution.py:1403
  548.1 4.3 copy-start.71
  548.2 6.2 copy-start.16
  548.2 7.1 %copy-start.9 = (bf16[4,3,256,512]{3,2,1,0:T(8,128)(2,1)S(1)}, bf16[4,3,256,512]{3,2,1,0:T(8,128)(2,1)}, u32[]{:S(2)}) copy-start(bf16[4,3,256,512]{3,2,1,0:T(8,128)(2,1)} %copy-done.8) | copy-start | bytes 9437188
  559.8 34.5 %copy-start.82 = (pred[256]{0:T(512)(128)(4,1)S(1)}, pred[256]{0:T(512)(128)(4,1)}, u32[]{:S(2)}) copy-start(pred[256]{0:T(512)(128)(4,1)} %constant.64.clone.1) | copy-start | bytes 772
  564.3 36.9 %copy-start.6 = (bf16[8,256,1024]{2,1,0:T(8,128)(2,1)S(1)}, bf16[8,256,1024]{2,1,0:T(8,128)(2,1)}, u32[]{:S(2)}) copy-start(bf16[8,256,1024]{2,1,0:T(8,128)(2,1)} %copy-done.4) | copy-start | bytes 12582916
  594.3 9.1 %copy-start.18 = (bf16[4,1,256,1024]{3,2,1,0:T(8,128)(2,1)}, bf16[4,1,256,1024]{3,2,1,0:T(8,128)(2,1)S(1)}, u32[]{:S(2)}) copy-start(bf16[4,1,256,1024]{3,2,1,0:T(8,128)(2,1)S(1)} %get-tuple-element.118) | copy-start | bytes 6291460
  607.4 4.1 copy-start.77
  607.4 4.1 copy-start.78
  607.4 4.1 copy-start.79
  611.5 3.6 copy-start.53
  679.8 4.7 copy-start.19
  687.9 5.8 copy-start.32
  687.9 6.7 copy-start.30
  687.9 7.7 %copy-start.1 = (f32[1024,4]{0,1:T(4,128)S(1)}, f32[1024,4]{0,1:T(4,128)}, u32[]{:S(2)}) copy-start(f32[1024,4]{0,1:T(4,128)} %param.22) | copy-start | bytes 49156
  (42 other events, 76.5 us)
